TPU v7x, 512 devices: a whole 4x8x8 slice. The times are simulated.
512 devices in a mesh: gx: 16 (over x, y_lo, core), gy: 32 (over z, y_hi).
Axes of the slice: x: 4, y: 8 (y_hi: 4, y_lo: 2; y = y_hi * 2 + y_lo), z: 8, core: 2. Of those that a mesh axis runs over, the one named last changes fastest.
Arguments:
- features: bfloat16 [16, 32, 16, 64, 192], P('gx', 'gy'), may hold values from -45 to 45
- cotangent: bfloat16 [16, 32, 16, 64, 192], P('gx', 'gy'), may hold values from -6 to 6
- counts: int32 [16, 32], P('gx', 'gy'), may hold values from 2 to 16, as said below
- neighbours: int32 [16, 32, 16, 27], P('gx', 'gy'), may hold values from 0 to 56, as said below
- send_x: int32 [16, 32, 2, 8], P('gx', 'gy'), may hold values from 0 to 16, as said below
- send_y: int32 [16, 32, 2, 12], P('gx', 'gy'), may hold values from 0 to 32, as said below
- action: float32 [128], replicated, may hold values from -6 to 6
- conv_weight: bfloat16 [192, 27, 192], replicated, may hold values from -0.078125 to 0.078125
- film_weight: float32 [128, 384], replicated, may hold values from -0.5 to 0.5
Outputs:
- output: bfloat16 [16, 32, 16, 64, 192], P('gx', 'gy')
- grad_features: bfloat16 [16, 32, 16, 64, 192], P('gx', 'gy')
- grad_conv_weight: float32 [192, 27, 192], P('gx')
- grad_film_weight: float32 [128, 384], replicated
Inputs may be any that keep to these rules, and one draw needn't show every extreme that they name: Slots below counts[i, j] hold the tile's active blocks, the others are unused; some tile has 16. `neighbours`: rows index E of the tile: local slots, the zero block at 16, 8 rows from the lower and 8 from the upper x neighbour, 12 from the lower and 12 from the upper y neighbour. 16 where the neighbouring block is inactive or outside the scene, and in every row of unused slots. `send_x`: [.., 0, :] the active blocks of the tile's lowest x layer of blocks, [.., 1, :] of its highest, as slot numbers, packed to the front, filled with 16; where 16 >= 8, some tile's list has no filler. `send_y`: [.., 0, :] the active blocks of the lowest y layer of Ex (local slots and blocks received along x), [.., 1, :] of the highest, as rows of Ex, packed to the front, filled with 16; where 16 >= 8, some tile's list has no filler.
All inputs are finite; a program needn't handle non-finite values.
Results may differ from a plain program's by a relative error of at most 0.007.
Values may be sent and summed in bfloat16 or wider, within the bound.
No kernel may reach another device: no remote copies, remote signals or barrier semaphores. Data moves between devices by JAX's collectives and lax.ppermute only.
A program may use at most 128 MiB of HBM per device.

v0:
```python
import jax
import jax.numpy as jnp
import numpy as np
from jax import lax
from jax.sharding import PartitionSpec as P


def with_halo(cells, sides, width):
    for axis, dim in sides:
        count = lax.axis_size(axis)
        ends = count - 1
        head = lax.slice_in_dim(cells, 0, width, axis=dim)
        tail = lax.slice_in_dim(cells, cells.shape[dim] - width, cells.shape[dim], axis=dim)
        cells = jnp.concatenate(
            [
                lax.ppermute(tail, axis, [(i, (i + 1) % count) for i in range(ends)]),
                cells,
                lax.ppermute(head, axis, [((i + 1) % count, i) for i in range(ends)]),
            ],
            axis=dim,
        )
    return cells


def offset_tables():
    block_table = np.zeros((64, 27), np.int32)
    voxel_table = np.zeros((64, 27), np.int32)
    for cell_index in range(64):
        position = [cell_index // 16, cell_index // 4 % 4, cell_index % 4]
        for offset_index in range(27):
            stride = [offset_index // 9 - 1, offset_index // 3 % 3 - 1, offset_index % 3 - 1]
            target = [position[axis_number] + stride[axis_number] for axis_number in range(3)]
            blocks = [(coordinate + 4) // 4 for coordinate in target]
            within = [(coordinate + 4) % 4 for coordinate in target]
            block_table[cell_index, offset_index] = (blocks[0] * 3 + blocks[1]) * 3 + blocks[2]
            voxel_table[cell_index, offset_index] = (within[0] * 4 + within[1]) * 4 + within[2]
    return (block_table, voxel_table)


def extend(local, list_x, list_y):
    zero_block = jnp.zeros((1,) + local.shape[1:], local.dtype)
    padded = jnp.concatenate([local, zero_block], axis=0)
    faces_x = padded[list_x]
    beside_x = with_halo(faces_x, (("gx", 0),), 1)
    widened = jnp.concatenate([padded, beside_x[0], beside_x[3]], axis=0)
    faces_y = widened[list_y]
    beside_y = with_halo(faces_y, (("gy", 0),), 1)
    return jnp.concatenate([widened, beside_y[0], beside_y[3]], axis=0)


def columns(extended, lookup):
    flat = extended.reshape(-1, extended.shape[-1])
    return flat[lookup].reshape(lookup.shape[0], -1)


def body(features, cotangent, counts, neighbours, send_x, send_y, action, conv_weight, film_weight):
    block_table, voxel_table = offset_tables()
    slots, voxels, channels = (features.shape[2], features.shape[3], features.shape[4])
    rows_total = slots * voxels
    tile_count = counts[0, 0]
    live = (jnp.arange(slots) < tile_count).astype(jnp.float32)[:, None, None]
    inputs = features[0, 0].astype(jnp.float32) * live
    lookup = (neighbours[0, 0][:, block_table] * voxels + voxel_table).reshape(rows_total, -1)
    list_x = send_x[0, 0]
    list_y = send_y[0, 0]
    live_cells = tile_count.astype(jnp.float32) * voxels
    cell_total, first_sum, square_sum = lax.psum(
        (live_cells, jnp.sum(inputs, axis=(0, 1)), jnp.sum(inputs * inputs, axis=(0, 1))),
        ("gx", "gy"),
    )
    mean = first_sum / cell_total
    variance = square_sum / cell_total - mean * mean
    inverse = lax.rsqrt(variance + 1e-05)
    film = jnp.dot(action, film_weight, precision=lax.Precision.HIGHEST)
    scale = 1.0 + film[:channels]
    shift = film[channels:]
    normed = (inputs - mean) * inverse
    before = normed * scale + shift
    hidden = (jnp.maximum(before, 0.0) * live).astype(jnp.bfloat16)
    cols_hidden = columns(extend(hidden, list_x, list_y), lookup)
    weight_rows = conv_weight.reshape(channels, -1)
    mixed = lax.dot_general(
        cols_hidden, weight_rows, (((1,), (1,)), ((), ())), preferred_element_type=jnp.float32
    )
    output = ((inputs + mixed.reshape(slots, voxels, channels)) * live).astype(jnp.bfloat16)
    upstream = cotangent[0, 0] * live.astype(jnp.bfloat16)
    upstream_rows = upstream.reshape(rows_total, channels)
    share = channels // lax.axis_size("gx")
    summed = lax.psum(
        lax.dot_general(
            upstream_rows, cols_hidden, (((0,), (0,)), ((), ())), preferred_element_type=jnp.float32
        ),
        ("gx", "gy"),
    )
    mine = lax.dynamic_slice_in_dim(summed, lax.axis_index("gx") * share, share, 0)
    grad_weight = mine.reshape(share, -1, channels)
    cols_upstream = columns(extend(upstream, list_x, list_y), lookup)
    flipped = jnp.transpose(conv_weight[:, ::-1, :], (1, 0, 2)).reshape(-1, channels)
    back = jnp.dot(cols_upstream, flipped, preferred_element_type=jnp.float32).reshape(
        slots, voxels, channels
    )
    active = (before > 0).astype(jnp.float32) * live
    slope = back * active
    shift_grad, scale_grad = lax.psum(
        (jnp.sum(slope, axis=(0, 1)), jnp.sum(slope * normed, axis=(0, 1))), ("gx", "gy")
    )
    grad_film = action[:, None] * jnp.concatenate([scale_grad, shift_grad])[None, :]
    grad_inputs = (
        upstream.astype(jnp.float32)
        + inverse
        * (
            slope * scale
            - scale * shift_grad / cell_total
            - normed * scale * scale_grad / cell_total
        )
    ) * live
    return (
        output[None, None],
        grad_inputs.astype(jnp.bfloat16)[None, None],
        grad_weight,
        grad_film,
    )


def solution(mesh):
    placed = (
        P("gx", "gy", None, None, None),
        P("gx", "gy", None, None, None),
        P("gx", "gy"),
        P("gx", "gy", None, None),
        P("gx", "gy", None, None),
        P("gx", "gy", None, None),
        P(),
        P(),
        P(),
    )
    return jax.shard_map(
        body,
        mesh=mesh,
        in_specs=placed,
        out_specs=(
            P("gx", "gy", None, None, None),
            P("gx", "gy", None, None, None),
            P("gx", None, None),
            P(),
        ),
        check_vma=False,
    )
```

profile of v0, /device:TPU:1, one launch (start us, length us, event | category | flops | bytes accessed | tf_op | source)
XLA Modules:
  0.0 761.7 jit_solution(11795385287883415273)
XLA Ops:
  7.9 0.2 copy-done
  8.1 0.9 convolution_reduce_fusion
  9.1 0.7 compare_select_fusion.2
  9.8 0.7 compare_select_fusion.1
  10.6 1.3 fusion.20
  11.9 106.1 %all-reduce.3 = (f32[192]{0:T(256)S(1)}, f32[]{:T(128)}, f32[192]{0:T(256)S(1)}) all-reduce(f32[192]{0:T(256)S(1)} %get-tuple-element.7, f32[]{:T(128)S(6)} %mul.139, f32[192]{0:T(256)S(1)} %get-tuple-element.6), channel_id=1, replica_groups=mesh['gx'=16,'gy'=32] {'gx','gy'}, use_global_device_ids=true, to_apply=%region_1.0 | all-reduce | flops 385 | bytes 3080 | tf_op jit(solution)/shard_map/psum | solution.py:67
  118.1 0.6 add_rsqrt_fusion
  118.7 1.4 constant_dynamic-update-slice_fusion.3
  120.3 0.6 pad_clamp_fusion.1
  120.9 0.6 gather_fusion
  121.5 0.8 slice_bitcast_fusion.6
  122.3 3.0 collective-permute-start
  125.3 2.0 collective-permute-start.1
  127.4 2.0 constant_dynamic-update-slice_fusion.7
  129.4 0.9 concatenate.28
  130.3 1.8 gather_fusion.4
  132.1 0.9 slice_bitcast_fusion.4
  133.0 3.5 collective-permute-start.4
  136.5 1.9 collective-permute-start.5
  138.4 3.5 rev.3
  142.0 4.6 copy.29
  146.5 0.6 constant_dynamic-update-slice_fusion.6
  147.2 4.2 gather_fusion.2
  151.4 1.4 copy.26
  152.9 1.3 reshape.235
  154.2 1.1 broadcast_add_fusion
  155.3 0.8 copy.34
  156.2 1.6 compare_select_fusion
  157.7 1.1 copy.28
  158.9 1.0 reshape.186
  159.9 0.9 broadcast_clamp_fusion
  160.8 1.9 broadcast_multiply_fusion
  162.8 3.0 fusion.6
  165.7 1.8 gather_fusion.5
  167.6 1.0 slice_bitcast_fusion
  168.6 5.1 collective-permute-start.6
  173.7 1.3 collective-permute-start.7
  174.9 1.8 gather_fusion.1
  176.8 1.0 slice_bitcast_fusion.2
  177.7 4.9 collective-permute-start.2
  182.6 1.5 collective-permute-start.3
  184.1 1.7 constant_dynamic-update-slice_fusion.5
  185.8 1.7 constant_dynamic-update-slice_fusion.4
  187.5 1.0 constant_dynamic-update-slice_fusion.1
  188.4 1.0 constant_dynamic-update-slice_fusion
  189.4 1.8 bitcast_dynamic-update-slice_fusion.1
  191.2 12.5 %collective-permute-done.7 = bf16[1,12,64,192]{3,2,1,0:T(8,128)(2,1)} collective-permute-done((bf16[1,12,64,192]{3,2,1,0:T(8,128)(2,1)}, bf16[1,12,64,192]{3,2,1,0:T(8,128)(2,1)}, u32[]{:S(2)}, u32[]{:S(2)}) %collective-permute-start.7) | collective-permute-done | bytes 294944 | tf_op jit(solution)/shard_map/ppermute | solution.py:18
  203.7 1.8 bitcast_dynamic-update-slice_fusion
  205.5 103.7 %gather_fusion.6 = bf16[27648,192]{1,0:T(8,128)(2,1)} fusion(bf16[3648,192]{1,0:T(8,128)(2,1)} %bitcast.93, s32[27648]{0:T(1024)S(1)} %broadcast_clamp_fusion), kind=kCustom, calls=%fused_computation.6 | custom fusion | bytes 21344256 | tf_op jit(solution)/shard_map/gather | solution.py:53
  309.2 23.0 %dot_general.19 = bf16[16,64,5184]{2,1,0:T(8,128)(2,1)} reshape(bf16[27648,192]{1,0:T(8,128)(2,1)} %gather_fusion.6) | data formatting | bytes 21233664 | tf_op jit(solution)/shard_map/dot_general | solution.py:99
  332.3 108.7 %gather_fusion.3 = bf16[27648,192]{1,0:T(8,128)(2,1)} fusion(bf16[3648,192]{1,0:T(8,128)(2,1)S(1)} %bitcast.92, s32[27648]{0:T(1024)S(1)} %broadcast_clamp_fusion), kind=kCustom, calls=%fused_computation.3 | custom fusion | bytes 21344256 | tf_op jit(solution)/shard_map/gather | solution.py:53
  441.0 23.0 %reshape.157 = bf16[1024,5184]{1,0:T(8,128)(2,1)} reshape(bf16[27648,192]{1,0:T(8,128)(2,1)} %gather_fusion.3) | data formatting | bytes 21233664 | tf_op jit(solution)/shard_map/reshape | solution.py:53
  464.0 8.3 %fusion.25 = f32[192,5184]{1,0:T(8,128)} fusion(bf16[1024,192]{1,0:T(8,128)(2,1)S(1)} %bitcast.95, bf16[1024,5184]{1,0:T(8,128)(2,1)} %reshape.157), kind=kOutput, calls=%fused_computation.80 | convolution fusion | flops 2038431744 | bytes 14991360 | tf_op jit(solution)/shard_map/dot_general | solution.py:90
  472.3 1.0 copy-done.2
  473.3 6.9 fusion.24
  480.3 23.0 %dot_general.17 = bf16[16,64,5184]{2,1,0:T(8,128)(2,1)} reshape(bf16[27648,192]{1,0:T(8,128)(2,1)} %gather_fusion.3) | data formatting | bytes 21233664 | tf_op jit(solution)/shard_map/dot_general | solution.py:82
  503.3 96.6 %all-reduce.2 = (f32[192]{0:T(256)S(1)}, f32[192]{0:T(256)S(1)}) all-reduce(f32[192]{0:T(256)S(1)} %get-tuple-element.5, f32[192]{0:T(256)S(1)} %get-tuple-element.4), channel_id=1, replica_groups=mesh['gx'=16,'gy'=32] {'gx','gy'}, use_global_device_ids=true, to_apply=%region_8.0 | all-reduce | flops 384 | bytes 3072 | tf_op jit(solution)/shard_map/psum | solution.py:104
  600.0 0.8 multiply_divide_fusion
  600.8 0.8 broadcast_multiply_fusion.1
  601.6 2.0 fusion.21
  603.6 7.9 %fusion.2 = bf16[1,1,16,64,192]{4,3,2,1,0:T(8,128)(2,1)} fusion(bf16[16,64,5184]{2,1,0:T(8,128)(2,1)} %dot_general.17, bf16[192,5184,1]{0,1,2:T(8,128)(2,1)S(1)} %bitcast.96, bf16[1,1,16,64,192]{4,3,2,1,0:T(8,128)(2,1)S(1)} %copy-done.2, f32[16]{0:T(128)S(1)} %copy-done.17), kind=kOutput, calls=%fused_computation.13 | convolution fusion | flops 2039414784 | bytes 13393984 | tf_op jit(solution)/shard_map/dot_general | solution.py:82
  611.5 141.3 %all-reduce.6.cloned.1.call-done = f32[192,5184]{1,0:T(8,128)} async-done(((f32[192,5184]{1,0:T(8,128)}), f32[192,5184]{1,0:T(8,128)}) %all-reduce.6.cloned.1.call-update) | async-done | bytes 3981328 | tf_op jit(solution)/shard_map/psum | solution.py:89
  752.8 1.1 constant_dynamic-slice_fusion
  753.9 0.9 reshape.158
  (65 shorter events, 0.8 us)
Async XLA Ops:
  7.2 0.9 copy-start
  7.2 745.7 %all-reduce.6.cloned.1.call-start = ((), (), s32[]{:S(2)}) async-start(), calls=%async_computation | async-start | bytes 8060928 | tf_op jit(solution)/shard_map/psum | solution.py:89
  7.9 112.9 %copy-start.16 = (f32[16]{0:T(128)}, f32[16]{0:T(128)S(1)}, u32[]{:S(2)}) copy-start(f32[16]{0:T(128)S(1)} %compare_convert_fusion) | copy-start | bytes 196
  9.1 111.8 %copy-start.7 = (f32[192]{0:T(256)}, f32[192]{0:T(256)S(1)}, u32[]{:S(2)}) copy-start(f32[192]{0:T(256)S(1)} %get-tuple-element.29) | copy-start | bytes 2308
  9.1 111.8 %copy-start.18 = (f32[192]{0:T(256)}, f32[192]{0:T(256)S(1)}, u32[]{:S(2)}) copy-start(f32[192]{0:T(256)S(1)} %get-tuple-element.30) | copy-start | bytes 2308
  118.7 2.1 copy-start.9
  118.7 2.1 copy-start.11
  120.9 6.5 copy-start.6
  122.3 40.4 %collective-permute-start = (bf16[1,8,64,192]{3,2,1,0:T(8,128)(2,1)}, bf16[1,8,64,192]{3,2,1,0:T(8,128)(2,1)}, u32[]{:S(2)}, u32[]{:S(2)}) collective-permute-start(bf16[1,8,64,192]{3,2,1,0:T(8,128)(2,1)} %get-tuple-element.26), channel_id=1, source_target_pairs={{0,32},{32,64},{64,96},{96,128},{128,160},{160,192},{192,224},{224... | collective-permute-start | bytes 589832 | tf_op jit(solution)/shard_map/ppermute | solution.py:16
  125.3 37.5 %collective-permute-start.1 = (bf16[1,8,64,192]{3,2,1,0:T(8,128)(2,1)}, bf16[1,8,64,192]{3,2,1,0:T(8,128)(2,1)}, u32[]{:S(2)}, u32[]{:S(2)}) collective-permute-start(bf16[1,8,64,192]{3,2,1,0:T(8,128)(2,1)} %get-tuple-element.25), channel_id=1, source_target_pairs={{32,0},{64,32},{96,64},{128,96},{160,128},{192,160},{224,192},{256... | collective-permute-start | bytes 589832 | tf_op jit(solution)/shard_map/ppermute | solution.py:18
  127.4 2.0 copy-start.21
  133.0 29.8 %collective-permute-start.4 = (bf16[1,8,64,192]{3,2,1,0:T(8,128)(2,1)}, bf16[1,8,64,192]{3,2,1,0:T(8,128)(2,1)}, u32[]{:S(2)}, u32[]{:S(2)}) collective-permute-start(bf16[1,8,64,192]{3,2,1,0:T(8,128)(2,1)} %get-tuple-element.24), channel_id=1, source_target_pairs={{0,32},{32,64},{64,96},{96,128},{128,160},{160,192},{192,224},{224... | collective-permute-start | bytes 589832 | tf_op jit(solution)/shard_map/ppermute | solution.py:16
  136.5 26.3 %collective-permute-start.5 = (bf16[1,8,64,192]{3,2,1,0:T(8,128)(2,1)}, bf16[1,8,64,192]{3,2,1,0:T(8,128)(2,1)}, u32[]{:S(2)}, u32[]{:S(2)}) collective-permute-start(bf16[1,8,64,192]{3,2,1,0:T(8,128)(2,1)} %get-tuple-element.23), channel_id=1, source_target_pairs={{32,0},{64,32},{96,64},{128,96},{160,128},{192,160},{224,192},{256... | collective-permute-start | bytes 589832 | tf_op jit(solution)/shard_map/ppermute | solution.py:18
  142.0 5.2 copy-start.14
  142.0 5.3 copy-start.15
  151.4 2.8 copy-start.5
  162.8 3.0 copy-start.13
  168.6 20.8 %collective-permute-start.6 = (bf16[1,12,64,192]{3,2,1,0:T(8,128)(2,1)}, bf16[1,12,64,192]{3,2,1,0:T(8,128)(2,1)}, u32[]{:S(2)}, u32[]{:S(2)}) collective-permute-start(bf16[1,12,64,192]{3,2,1,0:T(8,128)(2,1)} %get-tuple-element.20), channel_id=1, source_target_pairs={{0,1},{1,2},{2,3},{3,4},{4,5},{5,6},{6,7},{7,8},{8,9},{9,10},{10,1... | collective-permute-start | bytes 884744 | tf_op jit(solution)/shard_map/ppermute | solution.py:16
  173.7 30.1 %collective-permute-start.7 = (bf16[1,12,64,192]{3,2,1,0:T(8,128)(2,1)}, bf16[1,12,64,192]{3,2,1,0:T(8,128)(2,1)}, u32[]{:S(2)}, u32[]{:S(2)}) collective-permute-start(bf16[1,12,64,192]{3,2,1,0:T(8,128)(2,1)} %get-tuple-element.19), channel_id=1, source_target_pairs={{1,0},{2,1},{3,2},{4,3},{5,4},{6,5},{7,6},{8,7},{9,8},{10,9},{11,1... | collective-permute-start | bytes 884744 | tf_op jit(solution)/shard_map/ppermute | solution.py:18
  177.7 154.5 %collective-permute-start.2 = (bf16[1,12,64,192]{3,2,1,0:T(8,128)(2,1)}, bf16[1,12,64,192]{3,2,1,0:T(8,128)(2,1)S(1)}, u32[]{:S(2)}, u32[]{:S(2)}) collective-permute-start(bf16[1,12,64,192]{3,2,1,0:T(8,128)(2,1)} %get-tuple-element.22), channel_id=1, source_target_pairs={{0,1},{1,2},{2,3},{3,4},{4,5},{5,6},{6,7},{7,8},{8,9},{9,10},{10,1... | collective-permute-start | bytes 884744 | tf_op jit(solution)/shard_map/ppermute | solution.py:16
  182.6 149.6 %collective-permute-start.3 = (bf16[1,12,64,192]{3,2,1,0:T(8,128)(2,1)}, bf16[1,12,64,192]{3,2,1,0:T(8,128)(2,1)S(1)}, u32[]{:S(2)}, u32[]{:S(2)}) collective-permute-start(bf16[1,12,64,192]{3,2,1,0:T(8,128)(2,1)} %get-tuple-element.21), channel_id=1, source_target_pairs={{1,0},{2,1},{3,2},{4,3},{5,4},{6,5},{7,6},{8,7},{9,8},{10,9},{11,1... | collective-permute-start | bytes 884744 | tf_op jit(solution)/shard_map/ppermute | solution.py:18
  441.0 23.0 %copy-start.3 = (bf16[1,1,16,64,192]{4,3,2,1,0:T(8,128)(2,1)S(1)}, bf16[1,1,16,64,192]{4,3,2,1,0:T(8,128)(2,1)}, u32[]{:S(2)}) copy-start(bf16[1,1,16,64,192]{4,3,2,1,0:T(8,128)(2,1)} %broadcast_multiply_fusion) | copy-start | bytes 1179652
  472.3 1.0 copy-start.2
  472.3 1.0 copy-start.8
  472.3 1.0 copy-start.10
  472.3 1.0 copy-start.12
  472.3 1.0 copy-start.17
  472.3 1.0 copy-start.19
  480.3 120.5 %copy-start.20 = (f32[128]{0:T(128)S(1)}, f32[128]{0:T(128)}, u32[]{:S(2)}) copy-start(f32[128]{0:T(128)} %param.18) | copy-start | bytes 1540
  600.0 3.6 copy-start.4
  603.6 151.2 %copy-start.1 = (f32[128,384]{1,0:T(8,128)S(1)}, f32[128,384]{1,0:T(8,128)}, u32[]{:S(2)}) copy-start(f32[128,384]{1,0:T(8,128)} %param.20) | copy-start | bytes 589828
Sparse Core Ops, SparseCore 0:
  472.5 280.3 all-reduce.5
where the time goes:
time: 765 us; the launch traced here: 762 us
  local copies, waits for them, and re-layouts  323 us (42%)
  blocking collectives  203 us (27%)
  waiting for transfers between devices  154 us (20%)
  matrix products  24.1 us (3%)
  starting transfers between devices  23.2 us (3%)
  other arithmetic  19.5 us (3%)
  between operations  15.1 us (2%)
    gather x2, local copies, waits for them, and re-layouts, columns(): return flat[lookup].reshape(lookup.shape[0], -1)  212 us
    psum x1, waiting for transfers between devices, body(): lax.psum(lax.dot_general(upstream_rows, cols_hidden, (((0,), (0,)), ((),...  141 us
    psum x1, blocking collectives, body(): lax.psum((live_cells, jnp.sum(inputs, axis=(0, 1)), jnp.sum(inputs * inpu...  106 us
    psum x1, blocking collectives, body(): lax.psum((jnp.sum(slope, axis=(0, 1)), jnp.sum(slope * normed, axis=(0, 1...  96.6 us
    dot_general x1, local copies, waits for them, and re-layouts, body(): lax.dot_general(cols_hidden, weight_rows, (((1,), (1,)), ((), ())), prefe...  23 us
    reshape x1, local copies, waits for them, and re-layouts, columns(): return flat[lookup].reshape(lookup.shape[0], -1)  23 us
    dot_general x1, local copies, waits for them, and re-layouts, body(): jnp.dot(cols_upstream, flipped, preferred_element_type=jnp.float32)  23 us
    ppermute x4, starting transfers between devices, with_halo(): lax.ppermute(tail, axis, [(i, (i + 1) % count) for i in range(ends)])  16.5 us
  transfers between devices with their start and end apart: 9, of which 2 were waited for; matrix products, arithmetic and copies ran while one was open for 28% of the time, Pallas kernels for 0%

commit v1 on v0

v1 whole, which is shorter than its diff:
```python
import functools

import jax
import jax.numpy as jnp
from jax import lax
from jax.experimental import pallas as pl
from jax.experimental.pallas import tpu as pltpu
from jax.sharding import PartitionSpec as P

SLOTS = 16
VOXELS = 64
CHANNELS = 192
PAIRS = 14
VMEM_LIMIT = 56 * 1024 * 1024
F32 = jnp.float32
BF16 = jnp.bfloat16


def iota(shape, dim):
    return lax.broadcasted_iota(jnp.int32, shape, dim)


def dot(left, right):
    return jnp.dot(left, right, preferred_element_type=F32)


def dot_nt(left, right):
    return lax.dot_general(left, right, (((1,), (1,)), ((), ())), preferred_element_type=F32)


def swap_matrix(count):
    row, col = iota((256, 256), 0), iota((256, 256), 1)
    hit = ((row >> 4) == (col & 15)) & ((row & 15) == (col >> 4))
    if count is not None:
        hit = hit & ((row & 15) < count)
    return jnp.where(hit, 1.0, 0.0).astype(BF16)


def list_column(ref, side, length, rows, half):
    row = iota((rows, 1), 0)
    entry = jnp.full((rows, 1), -1, jnp.int32)
    for e in range(length):
        value = ref[side, e]
        entry = jnp.where((row == e) | (row == e + half), value, entry)
    return entry


def pick(column, width, low, high, base, second, half):
    rows = column.shape[0]
    row, col = iota((rows, width), 0), iota((rows, width), 1)
    target = column - low + base + jnp.where(row >= half, second, 0)
    hit = (column >= low) & (column < high) & (col == target)
    return jnp.where(hit, 1.0, 0.0).astype(BF16)


def pack_kernel(counts, send_x, feat, cot, action, film_weight, fields, stats, faces, film):
    count = counts[0]
    swap = swap_matrix(count)
    total = jnp.zeros((1, CHANNELS), F32)
    square = jnp.zeros((1, CHANNELS), F32)
    for g in range(4):
        part = slice(16 * g, 16 * g + 16)
        moved = dot(swap, feat[:, part, :].reshape(256, CHANNELS))
        total += jnp.sum(moved, axis=0, keepdims=True)
        square += jnp.sum(moved * moved, axis=0, keepdims=True)
        fields[part, 0:16, :] = moved.astype(BF16).reshape(16, 16, CHANNELS)
        moved = dot(swap, cot[:, part, :].reshape(256, CHANNELS))
        fields[part, 16:32, :] = moved.astype(BF16).reshape(16, 16, CHANNELS)
    row = iota((8, CHANNELS), 0)
    cells = (count * VOXELS).astype(F32)
    lines = jnp.where(row == 0, total, jnp.where(row == 1, square, jnp.where(row == 2, cells, 0.0)))
    for i in range(stats.shape[0]):
        stats[i, :, :] = lines
    for side in range(2):
        chosen = pick(list_column(send_x, side, 8, 16, 8), 32, 0, SLOTS, 0, 16, 8)
        for i in range(16):
            faces[side, i, :, :] = dot(chosen, fields[48 * side + i]).astype(BF16)
    film[...] = lax.dot_general(
        action[...],
        film_weight[...],
        (((1,), (0,)), ((), ())),
        precision=lax.Precision.HIGHEST,
        preferred_element_type=F32,
    )


def cross_kernel(send_y, fields, lower, upper, faces):
    for side in range(2):
        column = list_column(send_y, side, 12, 32, 16)
        local = pick(column, 32, 0, SLOTS, 0, 16, 16)
        from_lower = pick(column, 16, 17, 25, 0, 8, 16)
        from_upper = pick(column, 16, 25, 33, 0, 8, 16)
        for a in range(4):
            for c in range(4):
                value = dot(local, fields[16 * a + 12 * side + c])
                if a == 3:
                    value += dot(from_lower, lower[12 * side + c])
                if a == 0:
                    value += dot(from_upper, upper[12 * side + c])
                faces[side, 4 * a + c, :, :] = value.astype(BF16)


def norm_terms(stats, film):
    sums = jnp.sum(stats[...], axis=0)
    cells = sums[2:3, :]
    mean = sums[0:1, :] / cells
    variance = sums[1:2, :] / cells - mean * mean
    inverse = lax.rsqrt(variance + 1e-05)
    scale = 1.0 + film[:, :CHANNELS]
    shift = film[:, CHANNELS:]
    return cells, mean, inverse, scale, shift


def main_kernel(
    counts, fields, lower, upper, lower_y, upper_y, rule, stats, film, weight,
    output, gradients, kept, hid, low, high, low_y, high_y, padded, acc_m, acc_b, turned,
):
    count = counts[0]
    cells, mean, inverse, scale, shift = norm_terms(stats, film)

    def act(x):
        return jnp.maximum((x.astype(F32) - mean) * inverse * scale + shift, 0.0)

    live = iota((16, 1), 0) < count

    def local_part(i, carry):
        at = pl.ds(i * 16, 16)
        x = act(fields[at, 0:16, :].reshape(256, CHANNELS)).reshape(16, 16, CHANNELS)
        hid[at, 0:16, :] = jnp.where(live[None], x, 0.0).astype(BF16)
        hid[at, 16:32, :] = fields[at, 16:32, :]
        return carry

    lax.fori_loop(0, 4, local_part, 0)
    first_x = iota((256, 1), 0) % 16 < 8
    for source, target in ((lower, low), (upper, high)):
        x = source[...].reshape(256, CHANNELS)
        x = jnp.where(first_x, act(x), x.astype(F32))
        target[...] = x.astype(BF16).reshape(16, 16, CHANNELS)
    for source, target in ((lower_y, low_y), (upper_y, high_y)):
        x = act(source[:, 0:16, :].reshape(256, CHANNELS))
        target[:, 0:16, :] = x.astype(BF16).reshape(16, 16, CHANNELS)
        target[:, 16:32, :] = source[:, 16:32, :]

    entries = rule[...]
    row32 = iota((32, 128), 0)
    col32 = iota((32, 128), 1)
    second = row32 >= 16
    hot = []
    for n in range(27):
        column = entries[:, n : n + 1]
        column = jnp.concatenate([column, column], axis=0)
        target = jnp.where(second, column + 16, column)
        target = jnp.where(column >= 17, column + 15 + jnp.where(second, 8, 0), target)
        target = jnp.where(column >= 25, column + 23 + jnp.where(second, 8, 0), target)
        target = jnp.where(column >= 33, column + 31 + jnp.where(second, 16, 0), target)
        target = jnp.where(column >= 45, column + 51 + jnp.where(second, 16, 0), target)
        hit = (column != 16) & (col32 == target)
        hot.append(jnp.where(hit, 1.0, 0.0).astype(BF16))

    none16 = jnp.zeros((16, CHANNELS), BF16)
    none32 = jnp.zeros((32, CHANNELS), BF16)
    for a in range(4):
        for b in range(4):
            for c in range(4):
                own = hid[16 * a + 4 * b + c]
                padded[a + 1, b + 1, c + 1, :, :] = own
                ways = [
                    [(q + 1, 0)] + ([(5, 1)] if q == 0 else []) + ([(0, -1)] if q == 3 else [])
                    for q in (a, b, c)
                ]
                places = [(x, y, z) for x in ways[0] for y in ways[1] for z in ways[2]][1:]
                if not places:
                    continue
                listed = jnp.concatenate(
                    [
                        own,
                        low[4 * b + c] if a == 3 else none16,
                        high[4 * b + c] if a == 0 else none16,
                        low_y[4 * a + c] if b == 3 else none32,
                        high_y[4 * a + c] if b == 0 else none32,
                    ],
                    axis=0,
                )
                chosen = jnp.concatenate(
                    [hot[9 * (x[1] + 1) + 3 * (y[1] + 1) + z[1] + 1] for x, y, z in places], axis=0
                )
                found = dot(chosen, listed).astype(BF16)
                for m, (x, y, z) in enumerate(places):
                    padded[x[0], y[0], z[0], :, :] = found[32 * m : 32 * m + 32]

    row, col = iota((256, CHANNELS), 0), iota((256, CHANNELS), 1)
    spread = ((row & 15) < 12) & (col == (row >> 4) * 12 + (row & 15))
    spread = jnp.where(spread, 1.0, 0.0).astype(BF16)
    turned[...] = dot_nt(spread, fields[:, 16:32, :].reshape(1024, CHANNELS)).astype(BF16)

    acc_m[...] = jnp.zeros_like(acc_m)
    acc_b[...] = jnp.zeros_like(acc_b)

    def window(k, at):
        k = jnp.minimum(k, 26)
        x, y, z = k // 9, (k // 3) % 3, k % 3
        part = padded[pl.ds(x, 4), pl.ds(y, 4), pl.ds(z, 4), at, :]
        return part.reshape(1024, CHANNELS)

    def step(t, carry):
        k1, k2 = 2 * t, 2 * t + 1
        left1, left2 = window(k1, slice(0, 16)), window(k2, slice(0, 16))
        acc_m[...] += dot_nt(left1, weight[k1]) + dot_nt(left2, weight[k2])
        grad1 = dot(turned[...], left1)
        grad2 = dot(turned[...], left2)
        tail = jnp.concatenate([grad1[:, 128:], grad2[:, 128:]], axis=1)
        packed = jnp.concatenate([grad1[:, :128], grad2[:, :128], tail], axis=1)
        gradients[:, pl.ds(t, 1), :, :] = packed.astype(BF16).reshape(16, 1, 16, 384)
        up1, up2 = window(k1, slice(16, 32)), window(k2, slice(16, 32))
        back2 = jnp.where(k2 > 26, 27, 26 - k2)
        acc_b[...] += dot(up1, weight[26 - k1]) + dot(up2, weight[back2])
        return carry

    lax.fori_loop(0, PAIRS, step, 0)

    swap = swap_matrix(None)
    shift_grad = jnp.zeros((1, CHANNELS), F32)
    scale_grad = jnp.zeros((1, CHANNELS), F32)
    live256 = (iota((256, 1), 0) & 15) < count
    for g in range(4):
        at = slice(256 * g, 256 * g + 256)
        x = fields[16 * g : 16 * g + 16, 0:16, :].reshape(256, CHANNELS).astype(F32)
        mixed = jnp.where(live256, x + acc_m[at, :], 0.0).astype(BF16)
        output[:, 16 * g : 16 * g + 16, :] = dot(swap, mixed).astype(BF16).reshape(16, 16, CHANNELS)
        normed = (x - mean) * inverse
        slope = jnp.where(live256 & (normed * scale + shift > 0), acc_b[at, :], 0.0)
        shift_grad += jnp.sum(slope, axis=0, keepdims=True)
        scale_grad += jnp.sum(slope * normed, axis=0, keepdims=True)
        up = fields[16 * g : 16 * g + 16, 16:32, :].reshape(256, CHANNELS).astype(F32)
        kept[at, :] = up + inverse * (slope * scale)
    sums = jnp.concatenate([scale_grad, shift_grad], axis=1)
    first = sums.astype(BF16).astype(F32)
    rest = sums - first
    second_part = rest.astype(BF16).astype(F32)
    row = iota((16, 384), 0)
    lines = jnp.where(
        row == 12, first, jnp.where(row == 13, second_part, jnp.where(row == 14, rest - second_part, 0.0))
    )
    held = gradients[:, 0, :, :].astype(F32)
    gradients[:, 0, :, :] = jnp.where((row < 12)[None], held, lines[None]).astype(BF16)


def share_kernel(parts, shares):
    for t in range(PAIRS):
        total = jnp.sum(parts[:, t, :, :].astype(F32), axis=0)
        if t == 0:
            sums = total[12:13] + total[13:14] + total[14:15]
            first = sums.astype(BF16).astype(F32)
            rest = sums - first
            second = rest.astype(BF16).astype(F32)
            third = rest - second
        for m in range(3):
            share, place = divmod(3 * t + m, 2)
            shares[share, place, :, :] = total[:, 128 * m : 128 * m + 128].astype(BF16)
    for tile in range(3 * PAIRS, 64):
        share, place = divmod(tile, 2)
        shares[share, place, :, :] = jnp.zeros((16, 128), BF16)
    row = iota((16, 128), 0)
    lines = jnp.zeros((16, 128), F32)
    for e, piece in enumerate((first, second, third)):
        for m in range(3):
            lines = jnp.where(row == 3 * e + m, piece[:, 128 * m : 128 * m + 128], lines)
    for share in range(32):
        shares[share, 2, :, :] = lines.astype(BF16)


def finish_kernel(counts, parts, stats, film, action, fields, kept, mine, grad_film, grad_inputs):
    total = jnp.sum(parts[...].astype(F32), axis=0)
    for i in range(32):
        mine[i, :, :, :] = total[0:2].astype(BF16)
    tile = total[2]
    line = tile[0:3] + tile[3:6] + tile[6:9]
    sums = jnp.concatenate([line[0:1], line[1:2], line[2:3]], axis=1)
    scale_grad, shift_grad = sums[:, :CHANNELS], sums[:, CHANNELS:]
    cells, mean, inverse, scale, shift = norm_terms(stats, film)
    grad_film[...] = action[...] * sums
    swap = swap_matrix(None)
    live = (iota((256, 1), 0) & 15) < counts[0]
    for g in range(4):
        x = fields[16 * g : 16 * g + 16, 0:16, :].reshape(256, CHANNELS).astype(F32)
        normed = (x - mean) * inverse
        value = kept[256 * g : 256 * g + 256, :] - inverse * (
            scale * shift_grad / cells + normed * scale * scale_grad / cells
        )
        value = jnp.where(live, value, 0.0).astype(BF16)
        value = dot(swap, value).astype(BF16).reshape(16, 16, CHANNELS)
        grad_inputs[:, 16 * g : 16 * g + 16, :] = value


SMEM = pl.BlockSpec(memory_space=pltpu.SMEM)
VMEM = pl.BlockSpec(memory_space=pltpu.VMEM)


def call(kernel, specs, outs, scratch=(), flops=0, name=None):
    shapes = [jax.ShapeDtypeStruct(shape, dtype) for shape, dtype in outs]
    moved = sum(int(jnp.dtype(d).itemsize) * functools.reduce(int.__mul__, s) for s, d in outs)
    return pl.pallas_call(
        kernel,
        out_shape=shapes,
        in_specs=specs,
        out_specs=[VMEM] * len(outs),
        scratch_shapes=list(scratch),
        compiler_params=pltpu.CompilerParams(vmem_limit_bytes=VMEM_LIMIT),
        cost_estimate=pl.CostEstimate(flops=flops, bytes_accessed=2 * moved, transcendentals=0),
        name=name,
    )


def exchange(array, axis):
    return lax.all_to_all(array, axis, 0, 0, tiled=True)


def body(features, cotangent, counts, neighbours, send_x, send_y, action, conv_weight, film_weight):
    size_x, size_y = lax.axis_size("gx"), lax.axis_size("gy")
    count = counts.reshape(1)
    fields, stats, faces, film = call(
        pack_kernel,
        [SMEM, SMEM, VMEM, VMEM, VMEM, VMEM],
        [
            ((VOXELS, 32, CHANNELS), BF16),
            ((size_x, 8, CHANNELS), F32),
            ((2, 16, 16, CHANNELS), BF16),
            ((1, 2 * CHANNELS), F32),
        ],
        flops=10**9,
        name="pack",
    )(count, send_x[0, 0], features[0, 0], cotangent[0, 0], action[None], film_weight)
    up_x = [(i, i + 1) for i in range(size_x - 1)]
    down_x = [(i + 1, i) for i in range(size_x - 1)]
    up_y = [(i, i + 1) for i in range(size_y - 1)]
    down_y = [(i + 1, i) for i in range(size_y - 1)]
    lower = lax.ppermute(faces[1], "gx", up_x)
    upper = lax.ppermute(faces[0], "gx", down_x)
    stats = jnp.sum(exchange(stats, "gx"), axis=0)
    weight = jnp.pad(jnp.transpose(conv_weight, (1, 0, 2)), ((0, 1), (0, 0), (0, 0)))
    (cross,) = call(
        cross_kernel, [SMEM, VMEM, VMEM, VMEM], [((2, 16, 32, CHANNELS), BF16)], flops=10**8, name="cross"
    )(send_y[0, 0], fields, lower, upper)
    lower_y = lax.ppermute(cross[1], "gy", up_y)
    upper_y = lax.ppermute(cross[0], "gy", down_y)
    stats = exchange(jnp.broadcast_to(stats[None], (size_y,) + stats.shape), "gy")
    output, gradients, kept = call(
        main_kernel,
        [SMEM] + [VMEM] * 9,
        [
            ((SLOTS, VOXELS, CHANNELS), BF16),
            ((16, PAIRS, 16, 384), BF16),
            ((1024, CHANNELS), F32),
        ],
        [
            pltpu.VMEM((VOXELS, 32, CHANNELS), BF16),
            pltpu.VMEM((16, 16, CHANNELS), BF16),
            pltpu.VMEM((16, 16, CHANNELS), BF16),
            pltpu.VMEM((16, 32, CHANNELS), BF16),
            pltpu.VMEM((16, 32, CHANNELS), BF16),
            pltpu.VMEM((6, 6, 6, 32, CHANNELS), BF16),
            pltpu.VMEM((1024, CHANNELS), F32),
            pltpu.VMEM((1024, CHANNELS), F32),
            pltpu.VMEM((256, 1024), BF16),
        ],
        flops=10**10,
        name="convolve",
    )(count, fields, lower, upper, lower_y, upper_y, neighbours[0, 0], stats, film, weight)
    gradients = exchange(gradients, "gx")
    (shares,) = call(
        share_kernel, [VMEM], [((32, 3, 16, 128), BF16)], flops=10**6, name="share"
    )(gradients)
    shares = exchange(shares, "gy")
    mine, grad_film, grad_inputs = call(
        finish_kernel,
        [SMEM] + [VMEM] * 6,
        [
            ((32, 2, 16, 128), BF16),
            ((128, 2 * CHANNELS), F32),
            ((SLOTS, VOXELS, CHANNELS), BF16),
        ],
        flops=10**9,
        name="finish",
    )(count, shares, stats, film, action[:, None], fields, kept)
    tiles = exchange(mine, "gy").reshape(64, 16, 128)[: 3 * PAIRS]
    tiles = tiles.reshape(PAIRS, 3, 16, 128)[:, :, :12].astype(F32)
    even = jnp.concatenate([tiles[:, 0], tiles[:, 2, :, :64]], axis=-1)
    odd = jnp.concatenate([tiles[:, 1], tiles[:, 2, :, 64:]], axis=-1)
    grad_weight = jnp.stack([even, odd], axis=1).reshape(28, 12, CHANNELS)[:27].transpose(1, 0, 2)
    return output[None, None], grad_inputs[None, None], grad_weight, grad_film


def solution(mesh):
    tile = P("gx", "gy")
    return jax.shard_map(
        body,
        mesh=mesh,
        in_specs=(tile, tile, tile, tile, tile, tile, P(), P(), P()),
        out_specs=(tile, tile, P("gx"), P()),
        check_vma=False,
    )
```

time: 765 us -> 179 us (0.23)
  local copies, waits for them, and re-layouts: 323 us -> 9.15 us
  blocking collectives: 203 us -> 61 us
  waiting for transfers between devices: 154 us -> 29.4 us
  Pallas kernels: 0 us -> 33.2 us
  matrix products: 24.1 us -> 0 us
  starting transfers between devices: 23.2 us -> 42.9 us
  other arithmetic: 19.5 us -> 0.13 us
  between operations: 15.1 us -> 1.44 us
    gather x8 -> x0, local copies, waits for them, and re-layouts: 224 us -> none  [the longest x2 212 us: columns(): return flat[lookup].reshape(lookup.shape[0], -1)]
    psum x2 -> x0, blocking collectives: 203 us -> none  [the longest x1 106 us: body(): lax.psum((live_cells, jnp.sum(inputs, axis=(0, 1)), jnp.sum(inputs * inpu...]
    psum x1 -> x0, waiting for transfers between devices: 141 us -> none  [body(): lax.psum(lax.dot_general(upstream_rows, cols_hidden, (((0,), (0,)), ((),...]
    all_to_all x0 -> x2, blocking collectives: none -> 61 us  [exchange(): return lax.all_to_all(array, axis, 0, 0, tiled=True)]
    dot_general x2 -> x0, local copies, waits for them, and re-layouts: 46 us -> none  [the longest x1 23 us: body(): lax.dot_general(cols_hidden, weight_rows, (((1,), (1,)), ((), ())), prefe...]
    pallas_call x0 -> x5, Pallas kernels: none -> 33.2 us  [the longest x1 21.7 us: body(): call(main_kernel, [SMEM] + [VMEM] * 9, [((SLOTS, VOXELS, CHANNELS), BF16)...]
    all_to_all x0 -> x3, starting transfers between devices: none -> 32.1 us  [exchange(): return lax.all_to_all(array, axis, 0, 0, tiled=True)]
    dot_general x4 -> x0, matrix products: 24.1 us -> none  [the longest x1 8.32 us: body(): lax.dot_general(upstream_rows, cols_hidden, (((0,), (0,)), ((), ())), pre...]
  transfers between devices with their start and end apart: 9 -> 7, of which waited for: 2 -> 4; matrix products, arithmetic and copies ran while one was open for 28% -> 3% of each run, Pallas kernels for 0% -> 1%
where the time goes in v1:
time: 179 us; the launch traced here: 177 us
  blocking collectives  61 us (34%)
  starting transfers between devices  42.9 us (24%)
  Pallas kernels  33.2 us (19%)
  waiting for transfers between devices  29.4 us (16%)
  local copies, waits for them, and re-layouts  9.15 us (5%)
    all_to_all x2, blocking collectives, exchange(): return lax.all_to_all(array, axis, 0, 0, tiled=True)  61 us
    all_to_all x3, starting transfers between devices, exchange(): return lax.all_to_all(array, axis, 0, 0, tiled=True)  32.1 us
    pallas_call x1, Pallas kernels, body(): call(main_kernel, [SMEM] + [VMEM] * 9, [((SLOTS, VOXELS, CHANNELS), BF16)...  21.7 us
    all_to_all x3, waiting for transfers between devices, exchange(): return lax.all_to_all(array, axis, 0, 0, tiled=True)  12.7 us
    ppermute x1, waiting for transfers between devices, body(): upper_y = lax.ppermute(cross[0], 'gy', down_y)  9.46 us
    ppermute x1, waiting for transfers between devices, body(): upper = lax.ppermute(faces[0], 'gx', down_x)  4.34 us
    ppermute x1, starting transfers between devices, body(): lower_y = lax.ppermute(cross[1], 'gy', up_y)  4.05 us
  transfers between devices with their start and end apart: 7, of which 4 were waited for; matrix products, arithmetic and copies ran while one was open for 3% of the time, Pallas kernels for 1%

profile of v1, /device:TPU:1, one launch (start us, length us, event | category | flops | bytes accessed | tf_op | source)
XLA Modules:
  0.0 177.2 jit_solution(13983718205597276581)
XLA Ops:
  1.3 2.8 %pack.1 = (bf16[64,32,192]{2,1,0:T(8,128)(2,1)}, f32[16,8,192]{2,1,0:T(8,128)}, bf16[2,16,16,192]{3,2,1,0:T(8,128)(2,1)}, f32[1,384]{1,0:T(1,128)}) custom-call(s32[1]{0:T(128)} %bitcast.40.counts, s32[2,8]{1,0:T(2,128)} %bitcast.51, bf16[16,64,192]{2,1,0:T(8,128)(2,1)} %bitcast.48, bf16[16,64,192]{2,1,0:T(8,128)(2,1)} %bitcast.49, f32[1,128]{1,0:T(1,128)} %bitcast.46, ...), custom_call_target="tpu_custom_call" | custom-call | flops 1000000000 | bytes 2165760 | tf_op jit(solution)/shard_map/pack/pallas_call | solution.py:321
  4.1 0.0 copy-start
  4.1 10.4 %all-to-all-start = ((f32[16,8,192]{2,1,0:T(8,128)}), f32[16,8,192]{2,1,0:T(8,128)S(1)}, u32[]{:S(2)}, u32[]{:S(2)}) async-start(f32[16,8,192]{2,1,0:T(8,128)} %get-tuple-element.16), calls=%async_computation | async-start | bytes 262144 | tf_op jit(solution)/shard_map/all_to_all | solution.py:315
  14.6 1.0 slice_bitcast_fusion.3
  15.5 3.5 %collective-permute-start = (bf16[16,16,192]{2,1,0:T(8,128)(2,1)S(1)}, bf16[16,16,192]{2,1,0:T(8,128)(2,1)S(1)}, u32[]{:S(2)}, u32[]{:S(2)}) collective-permute-start(bf16[16,16,192]{2,1,0:T(8,128)(2,1)S(1)} %get-tuple-element.31), channel_id=1, source_target_pairs={{0,32},{32,64},{64,96},{96,128},{128,160},{160,192},{192,224},{224... | collective-permute-start | bytes 294920 | tf_op jit(solution)/shard_map/ppermute | solution.py:337
  19.1 1.9 %collective-permute-start.1 = (bf16[16,16,192]{2,1,0:T(8,128)(2,1)S(1)}, bf16[16,16,192]{2,1,0:T(8,128)(2,1)S(1)}, u32[]{:S(2)}, u32[]{:S(2)}) collective-permute-start(bf16[16,16,192]{2,1,0:T(8,128)(2,1)S(1)} %get-tuple-element.30), channel_id=1, source_target_pairs={{32,0},{64,32},{96,64},{128,96},{160,128},{192,160},{224,192},{256... | collective-permute-start | bytes 294920 | tf_op jit(solution)/shard_map/ppermute | solution.py:338
  21.0 0.0 collective-permute-done.lower
  21.0 0.0 copy-start.3
  21.0 4.3 %collective-permute-done.1.upper = bf16[16,16,192]{2,1,0:T(8,128)(2,1)S(1)} collective-permute-done((bf16[16,16,192]{2,1,0:T(8,128)(2,1)S(1)}, bf16[16,16,192]{2,1,0:T(8,128)(2,1)S(1)}, u32[]{:S(2)}, u32[]{:S(2)}) %collective-permute-start.1) | collective-permute-done | bytes 98336 | tf_op jit(solution)/shard_map/ppermute | solution.py:338
  25.4 0.0 copy-start.4
  25.4 0.0 copy-done.3
  25.4 0.6 copy-done.4
  26.0 2.5 %cross.1 = bf16[2,16,32,192]{3,2,1,0:T(8,128)(2,1)} custom-call(s32[2,12]{1,0:T(2,128)} %bitcast.45, bf16[64,32,192]{2,1,0:T(8,128)(2,1)} %get-tuple-element.14.fields, bf16[16,16,192]{2,1,0:T(8,128)(2,1)} %copy-done.3, bf16[16,16,192]{2,1,0:T(8,128)(2,1)} %copy-done.4), custom_call_target="tpu_custom_call" | custom-call | flops 100000000 | bytes 786432 | tf_op jit(solution)/shard_map/cross/pallas_call | solution.py:341
  28.5 0.0 all-to-all-done
  28.5 0.7 broadcast_in_dim.19
  29.2 11.4 %all-to-all-start.1 = ((f32[32,8,192]{2,1,0:T(8,128)}), f32[32,8,192]{2,1,0:T(8,128)S(1)}, u32[]{:S(2)}, u32[]{:S(2)}) async-start(f32[32,8,192]{2,1,0:T(8,128)} %broadcast_in_dim.19), calls=%async_computation.1 | async-start | bytes 524288 | tf_op jit(solution)/shard_map/all_to_all | solution.py:315
  40.7 1.1 slice_bitcast_fusion.1
  41.8 4.0 %collective-permute-start.2 = (bf16[16,32,192]{2,1,0:T(8,128)(2,1)S(1)}, bf16[16,32,192]{2,1,0:T(8,128)(2,1)S(1)}, u32[]{:S(2)}, u32[]{:S(2)}) collective-permute-start(bf16[16,32,192]{2,1,0:T(8,128)(2,1)S(1)} %get-tuple-element.25), channel_id=1, source_target_pairs={{0,1},{1,2},{2,3},{3,4},{4,5},{5,6},{6,7},{7,8},{8,9},{9,10},{10,1... | collective-permute-start | bytes 589832 | tf_op jit(solution)/shard_map/ppermute | solution.py:344
  45.8 1.3 collective-permute-start.3
  47.1 0.0 copy-done
  47.1 2.1 %pad.4.weight = bf16[28,192,192]{2,1,0:T(8,128)(2,1)} pad(bf16[27,192,192]{2,1,0:T(8,128)(2,1)S(1)} %bitcast.43, bf16[]{:T(256)} %constant.4.clone.1), padding=0_1x0_0x0_0 | pad | bytes 4055042 | tf_op jit(solution)/shard_map/jit(_pad)/pad | solution.py:340
  49.2 2.9 %collective-permute-done.2.lower_y = bf16[16,32,192]{2,1,0:T(8,128)(2,1)S(1)} collective-permute-done((bf16[16,32,192]{2,1,0:T(8,128)(2,1)S(1)}, bf16[16,32,192]{2,1,0:T(8,128)(2,1)S(1)}, u32[]{:S(2)}, u32[]{:S(2)}) %collective-permute-start.2) | collective-permute-done | bytes 196640 | tf_op jit(solution)/shard_map/ppermute | solution.py:344
  52.1 0.0 copy-start.6
  52.1 9.5 %collective-permute-done.3.upper_y = bf16[16,32,192]{2,1,0:T(8,128)(2,1)S(1)} collective-permute-done((bf16[16,32,192]{2,1,0:T(8,128)(2,1)S(1)}, bf16[16,32,192]{2,1,0:T(8,128)(2,1)S(1)}, u32[]{:S(2)}, u32[]{:S(2)}) %collective-permute-start.3) | collective-permute-done | bytes 196640 | tf_op jit(solution)/shard_map/ppermute | solution.py:345
  61.6 0.0 copy-start.7
  61.6 0.0 all-to-all-done.1.stats
  61.6 0.0 copy-start.2
  61.6 0.0 copy-done.6
  61.6 0.7 copy-done.7
  62.3 0.1 copy-done.2
  62.4 21.7 %convolve.1 = (bf16[16,64,192]{2,1,0:T(8,128)(2,1)}, bf16[16,14,16,384]{3,2,1,0:T(8,128)(2,1)}, f32[1024,192]{1,0:T(8,128)}) custom-call(s32[1]{0:T(128)} %bitcast.41.counts, bf16[64,32,192]{2,1,0:T(8,128)(2,1)} %get-tuple-element.14.fields, bf16[16,16,192]{2,1,0:T(8,128)(2,1)} %copy-done.3, bf16[16,16,192]{2,1,0:T(8,128)(2,1)} %copy-done.4, ...), custom_call_target="tpu_custom_call" | custom-call | flops 10000000000 | bytes 7864320 | tf_op jit(solution)/shard_map/convolve/pallas_call | solution.py:347
  84.0 41.0 %all_to_all.25.parts = bf16[16,14,16,384]{3,2,1,0:T(8,128)(2,1)} all-to-all(bf16[16,14,16,384]{3,2,1,0:T(8,128)(2,1)} %get-tuple-element.19), channel_id=1, replica_groups=mesh['gx'=16,'gy'=32] {'gx'}, dimensions={0} | all-to-all | bytes 5505024 | tf_op jit(solution)/shard_map/all_to_all | solution.py:315
  125.1 0.0 copy-start.5
  125.1 2.9 %share.1 = bf16[32,3,16,128]{3,2,1,0:T(8,128)(2,1)} custom-call(bf16[16,14,16,384]{3,2,1,0:T(8,128)(2,1)} %all_to_all.25.parts), custom_call_target="tpu_custom_call" | custom-call | flops 1000000 | bytes 786432 | tf_op jit(solution)/shard_map/share/pallas_call | solution.py:370
  128.0 10.2 %all-to-all-start.3 = ((bf16[32,3,16,128]{3,2,1,0:T(8,128)(2,1)}), bf16[32,3,16,128]{3,2,1,0:T(8,128)(2,1)S(1)}, u32[]{:S(2)}, u32[]{:S(2)}) async-start(bf16[32,3,16,128]{3,2,1,0:T(8,128)(2,1)} %share.1), calls=%async_computation.3 | async-start | bytes 786432 | tf_op jit(solution)/shard_map/all_to_all | solution.py:315
  138.2 0.0 copy-done.5
  138.2 0.7 copy.13.action
  138.9 12.7 %all-to-all-done.3.parts = bf16[32,3,16,128]{3,2,1,0:T(8,128)(2,1)S(1)} async-done(((bf16[32,3,16,128]{3,2,1,0:T(8,128)(2,1)}), bf16[32,3,16,128]{3,2,1,0:T(8,128)(2,1)S(1)}, u32[]{:S(2)}, u32[]{:S(2)}) %all-to-all-start.3) | async-done | bytes 393248 | tf_op jit(solution)/shard_map/all_to_all | solution.py:315
  151.6 0.0 copy-start.1
  151.6 0.7 copy-done.1
  152.4 3.3 %finish.1 = (bf16[32,2,16,128]{3,2,1,0:T(8,128)(2,1)}, f32[128,384]{1,0:T(8,128)}, bf16[16,64,192]{2,1,0:T(8,128)(2,1)}) custom-call(s32[1]{0:T(128)} %bitcast.42.counts, bf16[32,3,16,128]{3,2,1,0:T(8,128)(2,1)} %copy-done.1, f32[32,8,192]{2,1,0:T(8,128)} %copy-done.2, f32[1,384]{1,0:T(1,128)} %get-tuple-element.17.film, f32[128,1]{1,0:T(8,128)} %copy.13.action, ...), custom_call_target="tpu_custom_call" | custom-call | flops 1000000000 | bytes 1703936 | tf_op jit(solution)/shard_map/finish/pallas_call | solution.py:374
  155.7 19.9 %all_to_all.26 = bf16[32,2,16,128]{3,2,1,0:T(8,128)(2,1)S(1)} all-to-all(bf16[32,2,16,128]{3,2,1,0:T(8,128)(2,1)} %get-tuple-element.22), channel_id=1, replica_groups=mesh['gx'=16,'gy'=32] {'gy'}, dimensions={0} | all-to-all | bytes 524288 | tf_op jit(solution)/shard_map/all_to_all | solution.py:315
  175.7 0.1 slice_bitcast_fusion.7
  175.9 0.3 copy.16
  176.2 0.2 reshape.23
  176.4 0.8 slice_bitcast_fusion
  (6 shorter events, 0.2 us)
Async XLA Ops:
  4.1 43.0 %copy-start = (bf16[192,27,192]{2,0,1:T(8,128)(2,1)S(1)}, bf16[192,27,192]{2,0,1:T(8,128)(2,1)}, u32[]{:S(2)}) copy-start(bf16[192,27,192]{2,0,1:T(8,128)(2,1)} %param.16) | copy-start | bytes 5971972
  4.1 24.4 %all-to-all-start = ((f32[16,8,192]{2,1,0:T(8,128)}), f32[16,8,192]{2,1,0:T(8,128)S(1)}, u32[]{:S(2)}, u32[]{:S(2)}) async-start(f32[16,8,192]{2,1,0:T(8,128)} %get-tuple-element.16), calls=%async_computation | async-start | bytes 262144 | tf_op jit(solution)/shard_map/all_to_all | solution.py:315
  15.5 5.5 %collective-permute-start = (bf16[16,16,192]{2,1,0:T(8,128)(2,1)S(1)}, bf16[16,16,192]{2,1,0:T(8,128)(2,1)S(1)}, u32[]{:S(2)}, u32[]{:S(2)}) collective-permute-start(bf16[16,16,192]{2,1,0:T(8,128)(2,1)S(1)} %get-tuple-element.31), channel_id=1, source_target_pairs={{0,32},{32,64},{64,96},{96,128},{128,160},{160,192},{192,224},{224... | collective-permute-start | bytes 294920 | tf_op jit(solution)/shard_map/ppermute | solution.py:337
  19.1 6.3 %collective-permute-start.1 = (bf16[16,16,192]{2,1,0:T(8,128)(2,1)S(1)}, bf16[16,16,192]{2,1,0:T(8,128)(2,1)S(1)}, u32[]{:S(2)}, u32[]{:S(2)}) collective-permute-start(bf16[16,16,192]{2,1,0:T(8,128)(2,1)S(1)} %get-tuple-element.30), channel_id=1, source_target_pairs={{32,0},{64,32},{96,64},{128,96},{160,128},{192,160},{224,192},{256... | collective-permute-start | bytes 294920 | tf_op jit(solution)/shard_map/ppermute | solution.py:338
  21.0 4.4 %copy-start.3 = (bf16[16,16,192]{2,1,0:T(8,128)(2,1)}, bf16[16,16,192]{2,1,0:T(8,128)(2,1)S(1)}, u32[]{:S(2)}) copy-start(bf16[16,16,192]{2,1,0:T(8,128)(2,1)S(1)} %collective-permute-done.lower) | copy-start | bytes 294916
  25.4 0.7 copy-start.4
  29.2 32.3 %all-to-all-start.1 = ((f32[32,8,192]{2,1,0:T(8,128)}), f32[32,8,192]{2,1,0:T(8,128)S(1)}, u32[]{:S(2)}, u32[]{:S(2)}) async-start(f32[32,8,192]{2,1,0:T(8,128)} %broadcast_in_dim.19), calls=%async_computation.1 | async-start | bytes 524288 | tf_op jit(solution)/shard_map/all_to_all | solution.py:315
  41.8 10.4 %collective-permute-start.2 = (bf16[16,32,192]{2,1,0:T(8,128)(2,1)S(1)}, bf16[16,32,192]{2,1,0:T(8,128)(2,1)S(1)}, u32[]{:S(2)}, u32[]{:S(2)}) collective-permute-start(bf16[16,32,192]{2,1,0:T(8,128)(2,1)S(1)} %get-tuple-element.25), channel_id=1, source_target_pairs={{0,1},{1,2},{2,3},{3,4},{4,5},{5,6},{6,7},{7,8},{8,9},{9,10},{10,1... | collective-permute-start | bytes 589832 | tf_op jit(solution)/shard_map/ppermute | solution.py:344
  45.8 15.8 %collective-permute-start.3 = (bf16[16,32,192]{2,1,0:T(8,128)(2,1)S(1)}, bf16[16,32,192]{2,1,0:T(8,128)(2,1)S(1)}, u32[]{:S(2)}, u32[]{:S(2)}) collective-permute-start(bf16[16,32,192]{2,1,0:T(8,128)(2,1)S(1)} %get-tuple-element.24), channel_id=1, source_target_pairs={{1,0},{2,1},{3,2},{4,3},{5,4},{6,5},{7,6},{8,7},{9,8},{10,9},{11,1... | collective-permute-start | bytes 589832 | tf_op jit(solution)/shard_map/ppermute | solution.py:345
  52.1 9.5 %copy-start.6 = (bf16[16,32,192]{2,1,0:T(8,128)(2,1)}, bf16[16,32,192]{2,1,0:T(8,128)(2,1)S(1)}, u32[]{:S(2)}) copy-start(bf16[16,32,192]{2,1,0:T(8,128)(2,1)S(1)} %collective-permute-done.2.lower_y) | copy-start | bytes 589828
  61.6 0.7 copy-start.7
  61.6 0.8 copy-start.2
  125.1 13.1 %copy-start.5 = (f32[128]{0:T(128)S(1)}, f32[128]{0:T(128)}, u32[]{:S(2)}) copy-start(f32[128]{0:T(128)} %param.15) | copy-start | bytes 1540
  128.0 23.7 %all-to-all-start.3 = ((bf16[32,3,16,128]{3,2,1,0:T(8,128)(2,1)}), bf16[32,3,16,128]{3,2,1,0:T(8,128)(2,1)S(1)}, u32[]{:S(2)}, u32[]{:S(2)}) async-start(bf16[32,3,16,128]{3,2,1,0:T(8,128)(2,1)} %share.1), calls=%async_computation.3 | async-start | bytes 786432 | tf_op jit(solution)/shard_map/all_to_all | solution.py:315
  151.6 0.7 copy-start.1

commit v2 on v1

v2 whole, which is shorter than its diff:
```python
import jax
import jax.numpy as jnp
from jax import lax
from jax.experimental import pallas as pl
from jax.experimental.pallas import tpu as pltpu
from jax.sharding import PartitionSpec as P

SLOTS = 16
VOXELS = 64
CHANNELS = 192
TILES = 11
VMEM_LIMIT = 56 * 1024 * 1024
F32 = jnp.float32
BF16 = jnp.bfloat16


def iota(shape, dim):
    return lax.broadcasted_iota(jnp.int32, shape, dim)


def dot(left, right):
    return jnp.dot(left, right, preferred_element_type=F32)


def dot_nt(left, right):
    return lax.dot_general(left, right, (((1,), (1,)), ((), ())), preferred_element_type=F32)


def swap_matrix(count):
    row, col = iota((256, 256), 0), iota((256, 256), 1)
    hit = ((row >> 4) == (col & 15)) & ((row & 15) == (col >> 4))
    if count is not None:
        hit = hit & ((row & 15) < count)
    return jnp.where(hit, 1.0, 0.0).astype(BF16)


def list_column(ref, side, length, rows, half):
    row = iota((rows, 1), 0)
    entry = jnp.full((rows, 1), -1, jnp.int32)
    for e in range(length):
        value = ref[side, e]
        entry = jnp.where((row == e) | (row == e + half), value, entry)
    return entry


def pick(column, width, low, high, base, second, half):
    rows = column.shape[0]
    row, col = iota((rows, width), 0), iota((rows, width), 1)
    target = column - low + base + jnp.where(row >= half, second, 0)
    hit = (column >= low) & (column < high) & (col == target)
    return jnp.where(hit, 1.0, 0.0).astype(BF16)


def pack_lines(first, second):
    rest = jnp.concatenate([first[:, 128:], second[:, 128:]], axis=1)
    return [first[:, :128], second[:, :128], rest]


def unpack_lines(lines):
    first = jnp.concatenate([lines[0:1], lines[2:3, :64]], axis=1)
    second = jnp.concatenate([lines[1:2], lines[2:3, 64:]], axis=1)
    return first, second


def stack_lines(lines, rows):
    row = iota((rows, 128), 0)
    block = jnp.zeros((rows, 128), F32)
    for e, line in enumerate(lines):
        block = jnp.where(row == e, line, block)
    return block


def pack_kernel(counts, send_x, feat, cot, action, film_weight, held, up, stats, faces, film):
    count = counts[0]
    swap = swap_matrix(count)
    total = jnp.zeros((1, CHANNELS), F32)
    square = jnp.zeros((1, CHANNELS), F32)
    for g in range(4):
        part = slice(16 * g, 16 * g + 16)
        moved = dot(swap, feat[:, part, :].reshape(256, CHANNELS))
        total += jnp.sum(moved, axis=0, keepdims=True)
        square += jnp.sum(moved * moved, axis=0, keepdims=True)
        held[part, :, :] = moved.astype(BF16).reshape(16, 16, CHANNELS)
        moved = dot(swap, cot[:, part, :].reshape(256, CHANNELS))
        up[part, :, :] = moved.astype(BF16).reshape(16, 16, CHANNELS)
    cells = (count * VOXELS).astype(F32)
    block = stack_lines(pack_lines(total, square) + [cells], 4)
    for i in range(stats.shape[0]):
        stats[i, :, :] = block
    for side in range(2):
        chosen = pick(list_column(send_x, side, 8, 16, 8), 32, 0, SLOTS, 0, 16, 8)
        for i in range(16):
            both = jnp.concatenate([held[48 * side + i], up[48 * side + i]], axis=0)
            faces[side, i, :, :] = dot(chosen, both).astype(BF16)
    film[...] = lax.dot_general(
        action[...],
        film_weight[...],
        (((1,), (0,)), ((), ())),
        precision=lax.Precision.HIGHEST,
        preferred_element_type=F32,
    )


def cross_kernel(send_y, held, up, lower, upper, stats, faces, up_faces, spread):
    block = jnp.sum(stats[...], axis=0)
    for i in range(spread.shape[0]):
        spread[i, :, :] = block
    for side in range(2):
        column = list_column(send_y, side, 12, 32, 16)
        local = pick(column, 32, 0, SLOTS, 0, 16, 16)
        from_lower = pick(column, 16, 17, 25, 0, 8, 16)
        from_upper = pick(column, 16, 25, 33, 0, 8, 16)
        for a in range(4):
            for c in range(4):
                v = 16 * a + 12 * side + c
                value = dot(local, jnp.concatenate([held[v], up[v]], axis=0))
                if a == 3:
                    value += dot(from_lower, lower[12 * side + c])
                if a == 0:
                    value += dot(from_upper, upper[12 * side + c])
                value = value.astype(BF16)
                faces[side, 4 * a + c, :, :] = value[0:16]
                up_faces[side, 4 * a + c, :, :] = value[16:32]


def norm_terms(stats, film):
    lines = jnp.sum(stats[...], axis=0)
    total, square = unpack_lines(lines)
    cells = lines[3:4, 0:1]
    mean = total / cells
    variance = square / cells - mean * mean
    inverse = lax.rsqrt(variance + 1e-05)
    scale = 1.0 + film[:, :CHANNELS]
    shift = film[:, CHANNELS:]
    return cells, mean, inverse, scale, shift


def gather_blocks(rule, half, own, low, high, low_y, high_y, padded):
    entries = rule[...]
    col = iota((16, 80), 1)
    hot = []
    for n in range(27):
        column = entries[:, n : n + 1]
        target = jnp.where(column >= 17, column - 1 + half, column)
        target = jnp.where(column >= 25, column + 7 + half, target)
        target = jnp.where(column >= 33, column + 15, target)
        target = jnp.where(column >= 45, column + 19, target)
        hit = (column != 16) & (col == target)
        hot.append(jnp.where(hit, 1.0, 0.0).astype(BF16))
    none = jnp.zeros((16, CHANNELS), BF16)
    for a in range(4):
        for b in range(4):
            for c in range(4):
                mine = own[16 * a + 4 * b + c]
                padded[a + 1, b + 1, c + 1, :, :] = mine
                ways = [
                    [(q + 1, 0)] + ([(5, 1)] if q == 0 else []) + ([(0, -1)] if q == 3 else [])
                    for q in (a, b, c)
                ]
                places = [(x, y, z) for x in ways[0] for y in ways[1] for z in ways[2]][1:]
                if not places:
                    continue
                listed = jnp.concatenate(
                    [
                        mine,
                        low[4 * b + c] if a == 3 else none,
                        high[4 * b + c] if a == 0 else none,
                        low_y[4 * a + c] if b == 3 else none,
                        high_y[4 * a + c] if b == 0 else none,
                    ],
                    axis=0,
                )
                chosen = jnp.concatenate(
                    [hot[9 * (x[1] + 1) + 3 * (y[1] + 1) + z[1] + 1] for x, y, z in places], axis=0
                )
                found = dot(chosen, listed).astype(BF16)
                for m, (x, y, z) in enumerate(places):
                    padded[x[0], y[0], z[0], :, :] = found[16 * m : 16 * m + 16]


def window(padded, k):
    x, y, z = k // 9, (k // 3) % 3, k % 3
    part = padded[pl.ds(x, 4), pl.ds(y, 4), pl.ds(z, 4), :, :]
    return part.reshape(1024, CHANNELS)


def weight_kernel(
    counts, held, up, lower, upper, lower_y, upper_y, rule, stats, film,
    gradients, padded, hid, low, high, low_y, high_y, turned,
):
    cells, mean, inverse, scale, shift = norm_terms(stats, film)

    def act(x):
        x = (x.astype(F32) - mean) * inverse * scale + shift
        return jnp.maximum(x, 0.0).astype(BF16)

    live = (iota((256, 1), 0) & 15) < counts[0]

    def local_part(i, carry):
        at = pl.ds(i * 16, 16)
        x = act(held[at, :, :].reshape(256, CHANNELS))
        x = jnp.where(live, x.astype(F32), 0.0).astype(BF16)
        hid[at, :, :] = x.reshape(16, 16, CHANNELS)
        return carry

    lax.fori_loop(0, 4, local_part, 0)
    for source, target in ((lower, low), (upper, high), (lower_y, low_y), (upper_y, high_y)):
        target[...] = act(source[...].reshape(256, CHANNELS)).reshape(16, 16, CHANNELS)
    gather_blocks(rule, 0, hid, low, high, low_y, high_y, padded)

    row, col = iota((256, CHANNELS), 0), iota((256, CHANNELS), 1)
    group = row >> 4
    wide = up[...].reshape(1024, CHANNELS)
    for m in range(4):
        place = (row + 4 * m) & 15
        spread = (place < 12) & (col == group * 12 + place)
        spread = jnp.where(spread, 1.0, 0.0).astype(BF16)
        turned[m, :, :] = dot_nt(spread, wide).astype(BF16)

    line = iota((256, 384), 0) & 15

    def pair(m, k1, k2):
        grad1 = dot(turned[m], window(padded, k1))
        grad2 = dot(turned[m], window(padded, k2)) if k2 is not None else jnp.zeros_like(grad1)
        rest = jnp.concatenate([grad1[:, 128:], grad2[:, 128:]], axis=1)
        return jnp.concatenate([grad1[:, :128], grad2[:, :128], rest], axis=1)

    def store(at, value):
        gradients[:, pl.ds(at, 1), :, :] = value.astype(BF16).reshape(16, 1, 16, 384)

    def step(q, carry):
        k = 8 * q
        first, second = pair(0, k, k + 1), pair(1, k + 2, k + 3)
        store(3 * q, jnp.where(line < 12, first, second))
        third = pair(2, k + 4, k + 5)
        store(3 * q + 1, jnp.where(line < 8, second, third))
        fourth = pair(3, k + 6, k + 7)
        store(3 * q + 2, jnp.where(line < 4, third, fourth))
        return carry

    lax.fori_loop(0, 3, step, 0)
    first, second = pair(0, 24, 25), pair(1, 26, None)
    store(9, jnp.where(line < 12, first, second))
    store(10, jnp.where(line < 8, second, 0.0))


def field_kernel(
    counts, held, up, lower, upper, lower_y, upper_y, rule, stats, film, weight, padded,
    output, kept, sums, wide, acc_m, acc_b,
):
    count = counts[0]
    cells, mean, inverse, scale, shift = norm_terms(stats, film)
    gather_blocks(rule, 8, up, lower, upper, lower_y, upper_y, wide)
    acc_m[...] = jnp.zeros_like(acc_m)
    acc_b[...] = jnp.zeros_like(acc_b)

    def step(t, carry):
        k = 3 * t
        total = dot_nt(window(padded, k), weight[k])
        total += dot_nt(window(padded, k + 1), weight[k + 1])
        acc_m[...] += total + dot_nt(window(padded, k + 2), weight[k + 2])
        total = dot(window(wide, k), weight[26 - k])
        total += dot(window(wide, k + 1), weight[25 - k])
        acc_b[...] += total + dot(window(wide, k + 2), weight[24 - k])
        return carry

    lax.fori_loop(0, 9, step, 0)

    swap = swap_matrix(None)
    shift_grad = jnp.zeros((1, CHANNELS), F32)
    scale_grad = jnp.zeros((1, CHANNELS), F32)
    live = (iota((256, 1), 0) & 15) < count
    for g in range(4):
        at = slice(256 * g, 256 * g + 256)
        part = slice(16 * g, 16 * g + 16)
        x = held[part, :, :].reshape(256, CHANNELS).astype(F32)
        mixed = jnp.where(live, x + acc_m[at, :], 0.0).astype(BF16)
        output[:, part, :] = dot(swap, mixed).astype(BF16).reshape(16, 16, CHANNELS)
        normed = (x - mean) * inverse
        slope = jnp.where(live & (normed * scale + shift > 0), acc_b[at, :], 0.0)
        shift_grad += jnp.sum(slope, axis=0, keepdims=True)
        scale_grad += jnp.sum(slope * normed, axis=0, keepdims=True)
        kept[at, :] = up[part, :, :].reshape(256, CHANNELS).astype(F32) + inverse * (slope * scale)
    block = stack_lines(pack_lines(scale_grad, shift_grad), 4)
    sums[...] = block


def place_of(share):
    return (share // 3, share % 3) if share < 30 else (10, 2 * (share - 30))


def share_kernel(parts, sums, shares):
    lines = jnp.sum(sums[...], axis=0)
    first = lines.astype(BF16).astype(F32)
    second = lines - first
    block = stack_lines([first[e : e + 1] for e in range(3)] + [second[e : e + 1] for e in range(3)], 8)
    for tile in range(TILES):
        total = jnp.sum(parts[:, tile, :, :].astype(F32), axis=0)
        for share in range(32):
            if place_of(share)[0] == tile:
                third = place_of(share)[1]
                mine = total[:, 128 * third : 128 * third + 128]
                shares[share, :, :] = jnp.concatenate([mine, block], axis=0).astype(BF16)


def own_kernel(parts, mine, sums):
    total = jnp.sum(parts[...].astype(F32), axis=0)
    for i in range(mine.shape[0]):
        mine[i, :, :] = total[0:16].astype(BF16)
    sums[...] = total[16:24]


def finish_kernel(counts, sums, stats, film, action, held, kept, grad_film, grad_inputs):
    lines = sums[0:3, :] + sums[3:6, :]
    scale_grad, shift_grad = unpack_lines(lines)
    cells, mean, inverse, scale, shift = norm_terms(stats, film)
    grad_film[:, :CHANNELS] = action[...] * scale_grad
    grad_film[:, CHANNELS:] = action[...] * shift_grad
    swap = swap_matrix(None)
    live = (iota((256, 1), 0) & 15) < counts[0]
    for g in range(4):
        part = slice(16 * g, 16 * g + 16)
        x = held[part, :, :].reshape(256, CHANNELS).astype(F32)
        normed = (x - mean) * inverse
        value = kept[256 * g : 256 * g + 256, :] - inverse * (
            scale * shift_grad / cells + normed * scale * scale_grad / cells
        )
        value = jnp.where(live, value, 0.0).astype(BF16)
        grad_inputs[:, part, :] = dot(swap, value).astype(BF16).reshape(16, 16, CHANNELS)


def unpack_kernel(tiles, grad_weight):
    zero = jnp.zeros((16, 128), BF16)
    thirds = [
        jnp.concatenate([tiles[3 * u + n] for u in range(10)] + [last], axis=0)
        for n, last in enumerate((tiles[30], zero, tiles[31]))
    ]
    even = jnp.concatenate([thirds[0], thirds[2][:, :64]], axis=1)
    odd = jnp.concatenate([thirds[1], thirds[2][:, 64:]], axis=1)
    row, col = iota((384, 352), 0), iota((384, 352), 1)
    k = row & 31
    chosen = (k < 27) & (col == (row >> 5) + 12 * (k >> 1) + 176 * (k & 1))
    chosen = jnp.where(chosen, 1.0, 0.0).astype(BF16)
    found = dot(chosen, jnp.concatenate([even, odd], axis=0)).reshape(12, 32, CHANNELS)
    grad_weight[...] = found[:, :27, :]


SMEM = pl.BlockSpec(memory_space=pltpu.SMEM)
VMEM = pl.BlockSpec(memory_space=pltpu.VMEM)


def call(kernel, scalars, arrays, outs, scratch=(), flops=0, name=None):
    shapes = [jax.ShapeDtypeStruct(shape, dtype) for shape, dtype in outs]
    moved = sum(x.size * x.dtype.itemsize for x in [*arrays, *shapes])
    return pl.pallas_call(
        kernel,
        out_shape=shapes,
        in_specs=[SMEM] * len(scalars) + [VMEM] * len(arrays),
        out_specs=[VMEM] * len(outs),
        scratch_shapes=[pltpu.VMEM(*s) for s in scratch],
        compiler_params=pltpu.CompilerParams(vmem_limit_bytes=VMEM_LIMIT),
        cost_estimate=pl.CostEstimate(flops=flops, bytes_accessed=moved, transcendentals=0),
        name=name,
    )(*scalars, *arrays)


def exchange(array, axis):
    return lax.all_to_all(array, axis, 0, 0, tiled=True)


def body(features, cotangent, counts, neighbours, send_x, send_y, action, conv_weight, film_weight):
    size_x, size_y = lax.axis_size("gx"), lax.axis_size("gy")
    count = counts.reshape(1)
    rule = neighbours[0, 0]
    block = ((VOXELS, 16, CHANNELS), BF16)
    face = ((16, 16, CHANNELS), BF16)
    spaced = ((6, 6, 6, 16, CHANNELS), BF16)
    held, up, stats, faces, film = call(
        pack_kernel,
        [count, send_x[0, 0]],
        [features[0, 0], cotangent[0, 0], action[None], film_weight],
        [block, block, ((size_x, 4, 128), F32), ((2, *face[0]), BF16), ((1, 2 * CHANNELS), F32)],
        flops=10**9,
        name="pack",
    )
    up_x = [(i, i + 1) for i in range(size_x - 1)]
    down_x = [(i + 1, i) for i in range(size_x - 1)]
    up_y = [(i, i + 1) for i in range(size_y - 1)]
    down_y = [(i + 1, i) for i in range(size_y - 1)]
    lower = lax.ppermute(faces[1], "gx", up_x)
    upper = lax.ppermute(faces[0], "gx", down_x)
    stats = exchange(stats, "gx")
    weight = jnp.transpose(conv_weight, (1, 0, 2))
    cross, cross_up, stats = call(
        cross_kernel,
        [send_y[0, 0]],
        [held, up, lower, upper, stats],
        [((2, *face[0]), BF16), ((2, *face[0]), BF16), ((size_y, 4, 128), F32)],
        flops=10**8,
        name="cross",
    )
    lower_y = lax.ppermute(cross[1], "gy", up_y)
    upper_y = lax.ppermute(cross[0], "gy", down_y)
    lower_u = lax.ppermute(cross_up[1], "gy", up_y)
    upper_u = lax.ppermute(cross_up[0], "gy", down_y)
    stats = exchange(stats, "gy")
    gradients, padded = call(
        weight_kernel,
        [count],
        [held, up, lower, upper, lower_y, upper_y, rule, stats, film],
        [((16, TILES, 16, 384), BF16), spaced],
        [block, face, face, face, face, ((4, 256, 1024), BF16)],
        flops=4 * 10**9,
        name="weight",
    )
    gradients = exchange(gradients, "gx")
    output, kept, sums = call(
        field_kernel,
        [count],
        [held, up, lower, upper, lower_u, upper_u, rule, stats, film, weight, padded],
        [((SLOTS, VOXELS, CHANNELS), BF16), ((1024, CHANNELS), F32), ((4, 128), F32)],
        [spaced, ((1024, CHANNELS), F32), ((1024, CHANNELS), F32)],
        flops=6 * 10**9,
        name="field",
    )
    sums = lax.all_gather(sums, "gx")
    (shares,) = call(share_kernel, [], [gradients, sums], [((size_y, 24, 128), BF16)], name="share")
    shares = exchange(shares, "gy")
    mine, sums = call(
        own_kernel, [], [shares], [((size_y, 16, 128), BF16), ((8, 128), F32)], name="own"
    )
    tiles = exchange(mine, "gy")
    grad_film, grad_inputs = call(
        finish_kernel,
        [count],
        [sums, stats, film, action[:, None], held, kept],
        [((128, 2 * CHANNELS), F32), ((SLOTS, VOXELS, CHANNELS), BF16)],
        flops=10**9,
        name="finish",
    )
    (grad_weight,) = call(unpack_kernel, [], [tiles], [((12, 27, CHANNELS), F32)], name="unpack")
    return output[None, None], grad_inputs[None, None], grad_weight, grad_film


def solution(mesh):
    tile = P("gx", "gy")
    return jax.shard_map(
        body,
        mesh=mesh,
        in_specs=(tile, tile, tile, tile, tile, tile, P(), P(), P()),
        out_specs=(tile, tile, P("gx"), P()),
        check_vma=False,
    )
```

time: 179 us -> 191 us (1.067)
  waiting for transfers between devices: 29.4 us -> 43.1 us
  blocking collectives: 61 us -> 55.6 us
  Pallas kernels: 33.2 us -> 38.3 us
  local copies, waits for them, and re-layouts: 9.15 us -> 6.8 us
    all_to_all x2, blocking collectives: 61 us -> 30.8 us  [exchange(): return lax.all_to_all(array, axis, 0, 0, tiled=True)]
    ppermute x0 -> x2, waiting for transfers between devices: none -> 24.9 us  [the longest x1 24.9 us: body(): lower_u = lax.ppermute(cross_up[1], 'gy', up_y)]
    all_gather x0 -> x1, blocking collectives: none -> 24.8 us  [body(): sums = lax.all_gather(sums, 'gx')]
    all_to_all x3, starting transfers between devices: 32.1 us -> 23.4 us  [exchange(): return lax.all_to_all(array, axis, 0, 0, tiled=True)]
    ppermute x0 -> x2, starting transfers between devices: none -> 5.74 us  [the longest x1 4.44 us: body(): lower_u = lax.ppermute(cross_up[1], 'gy', up_y)]
    pallas_call x5 -> x8, Pallas kernels: 33.2 us -> 38.3 us  [call(): pl.pallas_call(kernel, out_shape=shapes, in_specs=[SMEM] * len(scalars) +...]
    all_to_all x3, waiting for transfers between devices: 12.7 us -> 7.6 us  [exchange(): return lax.all_to_all(array, axis, 0, 0, tiled=True)]
    ppermute x1, waiting for transfers between devices: 4.34 us -> 0.01 us  [body(): upper = lax.ppermute(faces[0], 'gx', down_x)]
  transfers between devices with their start and end apart: 7 -> 9, of which waited for: 4 -> 4; matrix products, arithmetic and copies ran while one was open for 3% -> 1% of each run, Pallas kernels for 1% -> 9%
where the time goes in v2:
time: 191 us; the launch traced here: 190 us
  blocking collectives  55.6 us (29%)
  starting transfers between devices  44.6 us (23%)
  waiting for transfers between devices  43.1 us (23%)
  Pallas kernels  38.3 us (20%)
  local copies, waits for them, and re-layouts  6.8 us (4%)
    pallas_call x8, Pallas kernels, call(): pl.pallas_call(kernel, out_shape=shapes, in_specs=[SMEM] * len(scalars) +...  38.3 us
    all_to_all x2, blocking collectives, exchange(): return lax.all_to_all(array, axis, 0, 0, tiled=True)  30.8 us
    ppermute x1, waiting for transfers between devices, body(): lower_u = lax.ppermute(cross_up[1], 'gy', up_y)  24.9 us
    all_gather x1, blocking collectives, body(): sums = lax.all_gather(sums, 'gx')  24.8 us
    all_to_all x3, starting transfers between devices, exchange(): return lax.all_to_all(array, axis, 0, 0, tiled=True)  23.4 us
    ppermute x1, waiting for transfers between devices, body(): upper_y = lax.ppermute(cross[0], 'gy', down_y)  9.97 us
    all_to_all x3, waiting for transfers between devices, exchange(): return lax.all_to_all(array, axis, 0, 0, tiled=True)  7.6 us
    ppermute x1, starting transfers between devices, body(): upper = lax.ppermute(faces[0], 'gx', down_x)  5.49 us
  transfers between devices with their start and end apart: 9, of which 4 were waited for; matrix products, arithmetic and copies ran while one was open for 1% of the time, Pallas kernels for 9%

profile of v2, /device:TPU:1, one launch (start us, length us, event | category | flops | bytes accessed | tf_op | source)
XLA Modules:
  0.0 189.8 jit_solution(10952972007498913510)
XLA Ops:
  1.3 2.8 %pack.1 = (bf16[64,16,192]{2,1,0:T(8,128)(2,1)}, bf16[64,16,192]{2,1,0:T(8,128)(2,1)}, f32[16,4,128]{2,1,0:T(4,128)}, bf16[2,16,16,192]{3,2,1,0:T(8,128)(2,1)}, f32[1,384]{1,0:T(1,128)}) custom-call(s32[1]{0:T(128)} %bitcast.24.counts, s32[2,8]{1,0:T(2,128)} %bitcast.37, bf16[16,64,192]{2,1,0:T(8,128)(2,1)} %bitcast.33, bf16[16,64,192]{2,1,0:T(8,128)(2,1)} %bitcast.34, ...), custom_call_target="tpu_custom_call" | custom-call | flops 1000000000 | bytes 2000896 | tf_op jit(solution)/shard_map/pack/pallas_call | solution.py:355
  4.1 1.0 slice_bitcast_fusion.4
  5.1 4.6 %collective-permute-start = (bf16[16,16,192]{2,1,0:T(8,128)(2,1)S(1)}, bf16[16,16,192]{2,1,0:T(8,128)(2,1)S(1)}, u32[]{:S(2)}, u32[]{:S(2)}) collective-permute-start(bf16[16,16,192]{2,1,0:T(8,128)(2,1)S(1)} %get-tuple-element.43), channel_id=1, source_target_pairs={{0,32},{32,64},{64,96},{96,128},{128,160},{160,192},{192,224},{224... | collective-permute-start | bytes 294920 | tf_op jit(solution)/shard_map/ppermute | solution.py:390
  9.7 5.5 %collective-permute-start.1 = (bf16[16,16,192]{2,1,0:T(8,128)(2,1)S(1)}, bf16[16,16,192]{2,1,0:T(8,128)(2,1)S(1)}, u32[]{:S(2)}, u32[]{:S(2)}) collective-permute-start(bf16[16,16,192]{2,1,0:T(8,128)(2,1)S(1)} %get-tuple-element.42), channel_id=1, source_target_pairs={{32,0},{64,32},{96,64},{128,96},{160,128},{192,160},{224,192},{256... | collective-permute-start | bytes 294920 | tf_op jit(solution)/shard_map/ppermute | solution.py:391
  15.2 9.2 %all_to_all.25.stats = f32[16,4,128]{2,1,0:T(4,128)} all-to-all(f32[16,4,128]{2,1,0:T(4,128)} %get-tuple-element.24), channel_id=1, replica_groups=mesh['gx'=16,'gy'=32] {'gx'}, dimensions={0} | all-to-all | bytes 65536 | tf_op jit(solution)/shard_map/all_to_all | solution.py:368
  24.4 0.0 collective-permute-done.lower
  24.4 0.0 copy-start.3
  24.4 0.0 collective-permute-done.1.upper
  24.4 0.0 copy-start.4
  24.4 0.6 copy-done.3
  25.0 0.0 copy-done.4
  25.1 2.4 %cross.1 = (bf16[2,16,16,192]{3,2,1,0:T(8,128)(2,1)}, bf16[2,16,16,192]{3,2,1,0:T(8,128)(2,1)}, f32[32,4,128]{2,1,0:T(4,128)}) custom-call(s32[2,12]{1,0:T(2,128)} %bitcast.29, bf16[64,16,192]{2,1,0:T(8,128)(2,1)} %get-tuple-element.21.held, bf16[64,16,192]{2,1,0:T(8,128)(2,1)} %get-tuple-element.22.up, bf16[16,16,192]{2,1,0:T(8,128)(2,1)} %copy-done.3, ...), custom_call_target="tpu_custom_call" | custom-call | flops 100000000 | bytes 1474560 | tf_op jit(solution)/shard_map/cross/pallas_call | solution.py:355
  27.5 14.6 %all-to-all-start.1 = ((f32[32,4,128]{2,1,0:T(4,128)}), f32[32,4,128]{2,1,0:T(4,128)S(1)}, u32[]{:S(2)}, u32[]{:S(2)}) async-start(f32[32,4,128]{2,1,0:T(4,128)} %get-tuple-element.26), calls=%async_computation.1 | async-start | bytes 131072 | tf_op jit(solution)/shard_map/all_to_all | solution.py:368
  42.1 1.0 slice_bitcast_fusion
  43.1 4.0 %collective-permute-start.4 = (bf16[16,16,192]{2,1,0:T(8,128)(2,1)S(1)}, bf16[16,16,192]{2,1,0:T(8,128)(2,1)S(1)}, u32[]{:S(2)}, u32[]{:S(2)}) collective-permute-start(bf16[16,16,192]{2,1,0:T(8,128)(2,1)S(1)} %get-tuple-element.39), channel_id=1, source_target_pairs={{0,1},{1,2},{2,3},{3,4},{4,5},{5,6},{6,7},{7,8},{8,9},{9,10},{10,1... | collective-permute-start | bytes 294920 | tf_op jit(solution)/shard_map/ppermute | solution.py:402
  47.1 1.3 collective-permute-start.5
  48.4 0.6 collective-permute-done.4.lower_y
  49.0 0.0 copy-start.7
  49.0 10.0 %collective-permute-done.5.upper_y = bf16[16,16,192]{2,1,0:T(8,128)(2,1)S(1)} collective-permute-done((bf16[16,16,192]{2,1,0:T(8,128)(2,1)S(1)}, bf16[16,16,192]{2,1,0:T(8,128)(2,1)S(1)}, u32[]{:S(2)}, u32[]{:S(2)}) %collective-permute-start.5) | collective-permute-done | bytes 98336 | tf_op jit(solution)/shard_map/ppermute | solution.py:403
  59.0 0.0 copy-start.9
  59.0 0.0 all-to-all-done.1.stats
  59.0 0.0 copy-start.5
  59.0 0.0 copy-done.7
  59.0 0.6 copy-done.9
  59.7 0.0 copy-done.5
  59.7 9.3 %weight.1 = (bf16[16,11,16,384]{3,2,1,0:T(8,128)(2,1)}, bf16[6,6,6,16,192]{4,3,2,1,0:T(8,128)(2,1)}) custom-call(s32[1]{0:T(128)} %bitcast.25.counts, bf16[64,16,192]{2,1,0:T(8,128)(2,1)} %get-tuple-element.21.held, bf16[64,16,192]{2,1,0:T(8,128)(2,1)} %get-tuple-element.22.up, bf16[16,16,192]{2,1,0:T(8,128)(2,1)} %copy-done.3, ...), custom_call_target="tpu_custom_call" | custom-call | flops 4000000000 | bytes 4738240 | tf_op jit(solution)/shard_map/weight/pallas_call | solution.py:355
  69.0 0.0 copy-start.2
  69.0 4.2 %all-to-all-start.2 = ((bf16[16,11,16,384]{3,2,1,0:T(8,128)(2,1)}), bf16[16,11,16,384]{3,2,1,0:T(8,128)(2,1)S(1)}, u32[]{:S(2)}, u32[]{:S(2)}) async-start(bf16[16,11,16,384]{3,2,1,0:T(8,128)(2,1)} %get-tuple-element.31), calls=%async_computation.2 | async-start | bytes 4325376 | tf_op jit(solution)/shard_map/all_to_all | solution.py:368
  73.2 0.0 copy-done.2
  73.2 4.4 %collective-permute-start.2 = (bf16[16,16,192]{2,1,0:T(8,128)(2,1)S(1)}, bf16[16,16,192]{2,1,0:T(8,128)(2,1)S(1)}, u32[]{:S(2)}, u32[]{:S(2)}) collective-permute-start(bf16[16,16,192]{2,1,0:T(8,128)(2,1)S(1)} %get-tuple-element.41), channel_id=1, source_target_pairs={{0,1},{1,2},{2,3},{3,4},{4,5},{5,6},{6,7},{7,8},{8,9},{9,10},{10,1... | collective-permute-start | bytes 294920 | tf_op jit(solution)/shard_map/ppermute | solution.py:404
  77.7 1.3 collective-permute-start.3
  79.0 24.9 %collective-permute-done.2.lower_y = bf16[16,16,192]{2,1,0:T(8,128)(2,1)S(1)} collective-permute-done((bf16[16,16,192]{2,1,0:T(8,128)(2,1)S(1)}, bf16[16,16,192]{2,1,0:T(8,128)(2,1)S(1)}, u32[]{:S(2)}, u32[]{:S(2)}) %collective-permute-start.2) | collective-permute-done | bytes 98336 | tf_op jit(solution)/shard_map/ppermute | solution.py:404
  103.9 0.0 copy-start.8
  103.9 0.0 collective-permute-done.3.upper_y
  103.9 0.0 copy-start.10
  103.9 0.6 copy-done.8
  104.6 0.0 copy-done.10
  104.6 14.7 %field.1 = (bf16[16,64,192]{2,1,0:T(8,128)(2,1)}, f32[1024,192]{1,0:T(8,128)}, f32[4,128]{1,0:T(4,128)}) custom-call(s32[1]{0:T(128)} %bitcast.26.counts, bf16[64,16,192]{2,1,0:T(8,128)(2,1)} %get-tuple-element.21.held, bf16[64,16,192]{2,1,0:T(8,128)(2,1)} %get-tuple-element.22.up, bf16[16,16,192]{2,1,0:T(8,128)(2,1)} %copy-done.3, ...), custom_call_target="tpu_custom_call" | custom-call | flops 6000000000 | bytes 5747904 | tf_op jit(solution)/shard_map/field/pallas_call | solution.py:355
  119.3 0.0 copy-start.6
  119.3 24.8 %all-gather.1.sums = f32[16,4,128]{2,1,0:T(4,128)} all-gather(f32[1,4,128]{2,1,0:T(4,128)} %bitcast.28), channel_id=2, replica_groups=mesh['gx'=16,'gy'=32] {'gx'}, dimensions={0}, use_global_device_ids=true | all-gather | bytes 34816 | tf_op jit(solution)/shard_map/all_gather | solution.py:426
  144.0 0.0 all-to-all-done.2.parts
  144.0 0.0 copy-start
  144.0 1.4 copy-done
  145.4 2.6 %share.1 = bf16[32,24,128]{2,1,0:T(8,128)(2,1)} custom-call(bf16[16,11,16,384]{3,2,1,0:T(8,128)(2,1)} %copy-done, f32[16,4,128]{2,1,0:T(4,128)} %all-gather.1.sums), custom_call_target="tpu_custom_call" | custom-call | bytes 2392064 | tf_op jit(solution)/shard_map/share/pallas_call | solution.py:355
  148.0 21.6 %all_to_all.26.parts = bf16[32,24,128]{2,1,0:T(8,128)(2,1)} all-to-all(bf16[32,24,128]{2,1,0:T(8,128)(2,1)} %share.1), channel_id=1, replica_groups=mesh['gx'=16,'gy'=32] {'gy'}, dimensions={0} | all-to-all | bytes 393216 | tf_op jit(solution)/shard_map/all_to_all | solution.py:368
  169.6 1.6 own.1
  171.2 4.6 %all-to-all-start.4 = ((bf16[32,16,128]{2,1,0:T(8,128)(2,1)}), bf16[32,16,128]{2,1,0:T(8,128)(2,1)S(1)}, u32[]{:S(2)}, u32[]{:S(2)}) async-start(bf16[32,16,128]{2,1,0:T(8,128)(2,1)} %get-tuple-element.36), calls=%async_computation.4 | async-start | bytes 262144 | tf_op jit(solution)/shard_map/all_to_all | solution.py:368
  175.8 0.0 copy-done.6
  175.9 0.7 copy.14.action
  176.6 3.0 %finish.1 = (f32[128,384]{1,0:T(8,128)}, bf16[16,64,192]{2,1,0:T(8,128)(2,1)}) custom-call(s32[1]{0:T(128)} %bitcast.27.counts, f32[8,128]{1,0:T(8,128)} %get-tuple-element.33.sums, f32[32,4,128]{2,1,0:T(4,128)} %copy-done.5, f32[1,384]{1,0:T(1,128)} %get-tuple-element.27.film, f32[128,1]{1,0:T(8,128)} %copy.14.action, ...), custom_call_target="tpu_custom_call" | custom-call | flops 1000000000 | bytes 1841152 | tf_op jit(solution)/shard_map/finish/pallas_call | solution.py:355
  179.6 7.6 %all-to-all-done.4.tiles = bf16[32,16,128]{2,1,0:T(8,128)(2,1)S(1)} async-done(((bf16[32,16,128]{2,1,0:T(8,128)(2,1)}), bf16[32,16,128]{2,1,0:T(8,128)(2,1)S(1)}, u32[]{:S(2)}, u32[]{:S(2)}) %all-to-all-start.4) | async-done | bytes 131104 | tf_op jit(solution)/shard_map/all_to_all | solution.py:368
  187.1 0.0 copy-start.1
  187.2 0.6 copy-done.1
  187.8 2.0 %unpack.1 = f32[12,27,192]{2,1,0:T(8,128)} custom-call(bf16[32,16,128]{2,1,0:T(8,128)(2,1)} %copy-done.1), custom_call_target="tpu_custom_call" | custom-call | bytes 379904 | tf_op jit(solution)/shard_map/unpack/pallas_call | solution.py:355
  (1 shorter events, 0.0 us)
Async XLA Ops:
  5.1 19.3 %collective-permute-start = (bf16[16,16,192]{2,1,0:T(8,128)(2,1)S(1)}, bf16[16,16,192]{2,1,0:T(8,128)(2,1)S(1)}, u32[]{:S(2)}, u32[]{:S(2)}) collective-permute-start(bf16[16,16,192]{2,1,0:T(8,128)(2,1)S(1)} %get-tuple-element.43), channel_id=1, source_target_pairs={{0,32},{32,64},{64,96},{96,128},{128,160},{160,192},{192,224},{224... | collective-permute-start | bytes 294920 | tf_op jit(solution)/shard_map/ppermute | solution.py:390
  9.7 14.7 %collective-permute-start.1 = (bf16[16,16,192]{2,1,0:T(8,128)(2,1)S(1)}, bf16[16,16,192]{2,1,0:T(8,128)(2,1)S(1)}, u32[]{:S(2)}, u32[]{:S(2)}) collective-permute-start(bf16[16,16,192]{2,1,0:T(8,128)(2,1)S(1)} %get-tuple-element.42), channel_id=1, source_target_pairs={{32,0},{64,32},{96,64},{128,96},{160,128},{192,160},{224,192},{256... | collective-permute-start | bytes 294920 | tf_op jit(solution)/shard_map/ppermute | solution.py:391
  24.4 0.7 copy-start.3
  24.4 0.7 copy-start.4
  27.5 31.5 %all-to-all-start.1 = ((f32[32,4,128]{2,1,0:T(4,128)}), f32[32,4,128]{2,1,0:T(4,128)S(1)}, u32[]{:S(2)}, u32[]{:S(2)}) async-start(f32[32,4,128]{2,1,0:T(4,128)} %get-tuple-element.26), calls=%async_computation.1 | async-start | bytes 131072 | tf_op jit(solution)/shard_map/all_to_all | solution.py:368
  43.1 6.0 %collective-permute-start.4 = (bf16[16,16,192]{2,1,0:T(8,128)(2,1)S(1)}, bf16[16,16,192]{2,1,0:T(8,128)(2,1)S(1)}, u32[]{:S(2)}, u32[]{:S(2)}) collective-permute-start(bf16[16,16,192]{2,1,0:T(8,128)(2,1)S(1)} %get-tuple-element.39), channel_id=1, source_target_pairs={{0,1},{1,2},{2,3},{3,4},{4,5},{5,6},{6,7},{7,8},{8,9},{9,10},{10,1... | collective-permute-start | bytes 294920 | tf_op jit(solution)/shard_map/ppermute | solution.py:402
  47.1 11.9 %collective-permute-start.5 = (bf16[16,16,192]{2,1,0:T(8,128)(2,1)S(1)}, bf16[16,16,192]{2,1,0:T(8,128)(2,1)S(1)}, u32[]{:S(2)}, u32[]{:S(2)}) collective-permute-start(bf16[16,16,192]{2,1,0:T(8,128)(2,1)S(1)} %get-tuple-element.38), channel_id=1, source_target_pairs={{1,0},{2,1},{3,2},{4,3},{5,4},{6,5},{7,6},{8,7},{9,8},{10,9},{11,1... | collective-permute-start | bytes 294920 | tf_op jit(solution)/shard_map/ppermute | solution.py:403
  49.0 10.0 %copy-start.7 = (bf16[16,16,192]{2,1,0:T(8,128)(2,1)}, bf16[16,16,192]{2,1,0:T(8,128)(2,1)S(1)}, u32[]{:S(2)}) copy-start(bf16[16,16,192]{2,1,0:T(8,128)(2,1)S(1)} %collective-permute-done.4.lower_y) | copy-start | bytes 294916
  59.0 0.7 copy-start.9
  59.0 0.7 copy-start.5
  69.0 4.2 %copy-start.2 = (bf16[2,16,16,192]{3,2,1,0:T(8,128)(2,1)S(1)}, bf16[2,16,16,192]{3,2,1,0:T(8,128)(2,1)}, u32[]{:S(2)}) copy-start(bf16[2,16,16,192]{3,2,1,0:T(8,128)(2,1)} %get-tuple-element.25) | copy-start | bytes 589828
  69.0 75.0 %all-to-all-start.2 = ((bf16[16,11,16,384]{3,2,1,0:T(8,128)(2,1)}), bf16[16,11,16,384]{3,2,1,0:T(8,128)(2,1)S(1)}, u32[]{:S(2)}, u32[]{:S(2)}) async-start(bf16[16,11,16,384]{3,2,1,0:T(8,128)(2,1)} %get-tuple-element.31), calls=%async_computation.2 | async-start | bytes 4325376 | tf_op jit(solution)/shard_map/all_to_all | solution.py:368
  73.2 30.7 %collective-permute-start.2 = (bf16[16,16,192]{2,1,0:T(8,128)(2,1)S(1)}, bf16[16,16,192]{2,1,0:T(8,128)(2,1)S(1)}, u32[]{:S(2)}, u32[]{:S(2)}) collective-permute-start(bf16[16,16,192]{2,1,0:T(8,128)(2,1)S(1)} %get-tuple-element.41), channel_id=1, source_target_pairs={{0,1},{1,2},{2,3},{3,4},{4,5},{5,6},{6,7},{7,8},{8,9},{9,10},{10,1... | collective-permute-start | bytes 294920 | tf_op jit(solution)/shard_map/ppermute | solution.py:404
  77.7 26.2 %collective-permute-start.3 = (bf16[16,16,192]{2,1,0:T(8,128)(2,1)S(1)}, bf16[16,16,192]{2,1,0:T(8,128)(2,1)S(1)}, u32[]{:S(2)}, u32[]{:S(2)}) collective-permute-start(bf16[16,16,192]{2,1,0:T(8,128)(2,1)S(1)} %get-tuple-element.40), channel_id=1, source_target_pairs={{1,0},{2,1},{3,2},{4,3},{5,4},{6,5},{7,6},{8,7},{9,8},{10,9},{11,1... | collective-permute-start | bytes 294920 | tf_op jit(solution)/shard_map/ppermute | solution.py:405
  103.9 0.7 copy-start.8
  103.9 0.7 copy-start.10
  119.3 56.6 %copy-start.6 = (f32[128]{0:T(128)S(1)}, f32[128]{0:T(128)}, u32[]{:S(2)}) copy-start(f32[128]{0:T(128)} %param.15) | copy-start | bytes 1540
  144.0 1.4 copy-start
  171.2 16.0 %all-to-all-start.4 = ((bf16[32,16,128]{2,1,0:T(8,128)(2,1)}), bf16[32,16,128]{2,1,0:T(8,128)(2,1)S(1)}, u32[]{:S(2)}, u32[]{:S(2)}) async-start(bf16[32,16,128]{2,1,0:T(8,128)(2,1)} %get-tuple-element.36), calls=%async_computation.4 | async-start | bytes 262144 | tf_op jit(solution)/shard_map/all_to_all | solution.py:368
  187.1 0.7 copy-start.1

commit v3 on v2

--- a/solution.py
+++ b/solution.py
@@ -70,7 +70,20 @@
     return block
 
 
-def pack_kernel(counts, send_x, feat, cot, action, film_weight, held, up, stats, faces, film):
+def join_fields(value):
+    first, second = value[0:16], value[16:32]
+    rest = jnp.concatenate([first[:, 128:], second[:, 128:]], axis=1)
+    return jnp.concatenate([first[:, :128], second[:, :128], rest], axis=1).astype(BF16)
+
+
+def one_field(joined, which):
+    tail = joined[..., 256:320] if which == 0 else joined[..., 320:384]
+    return jnp.concatenate([joined[..., 128 * which : 128 * which + 128], tail], axis=-1)
+
+
+def pack_kernel(
+    counts, send_x, send_y, feat, cot, action, film_weight, held, up, stats, faces, sides, film
+):
     count = counts[0]
     swap = swap_matrix(count)
     total = jnp.zeros((1, CHANNELS), F32)
@@ -92,6 +105,13 @@
         for i in range(16):
             both = jnp.concatenate([held[48 * side + i], up[48 * side + i]], axis=0)
             faces[side, i, :, :] = dot(chosen, both).astype(BF16)
+    for side in range(2):
+        chosen = pick(list_column(send_y, side, 12, 32, 16), 32, 0, SLOTS, 0, 16, 16)
+        for a in range(4):
+            for c in range(4):
+                v = 16 * a + 12 * side + c
+                both = jnp.concatenate([held[v], up[v]], axis=0)
+                sides[side, 4 * a + c, :, :] = join_fields(dot(chosen, both))
     film[...] = lax.dot_general(
         action[...],
         film_weight[...],
@@ -101,26 +121,23 @@
     )
 
 
-def cross_kernel(send_y, held, up, lower, upper, stats, faces, up_faces, spread):
+def cross_kernel(send_y, lower, upper, stats, corners, spread):
     block = jnp.sum(stats[...], axis=0)
     for i in range(spread.shape[0]):
         spread[i, :, :] = block
     for side in range(2):
         column = list_column(send_y, side, 12, 32, 16)
-        local = pick(column, 32, 0, SLOTS, 0, 16, 16)
         from_lower = pick(column, 16, 17, 25, 0, 8, 16)
         from_upper = pick(column, 16, 25, 33, 0, 8, 16)
-        for a in range(4):
-            for c in range(4):
-                v = 16 * a + 12 * side + c
-                value = dot(local, jnp.concatenate([held[v], up[v]], axis=0))
-                if a == 3:
-                    value += dot(from_lower, lower[12 * side + c])
-                if a == 0:
-                    value += dot(from_upper, upper[12 * side + c])
-                value = value.astype(BF16)
-                faces[side, 4 * a + c, :, :] = value[0:16]
-                up_faces[side, 4 * a + c, :, :] = value[16:32]
+        for c in range(4):
+            corners[side, c, :, :] = join_fields(dot(from_upper, upper[12 * side + c]))
+            corners[side, 4 + c, :, :] = join_fields(dot(from_lower, lower[12 * side + c]))
+
+
+def beside_y(side, corner, which):
+    part = one_field(side[...], which).astype(F32)
+    more = one_field(corner[...], which).astype(F32)
+    return jnp.concatenate([part[0:4] + more[0:4], part[4:12], part[12:16] + more[4:8]], axis=0)
 
 
 def norm_terms(stats, film):
@@ -185,7 +202,7 @@
 
 
 def weight_kernel(
-    counts, held, up, lower, upper, lower_y, upper_y, rule, stats, film,
+    counts, held, up, lower, upper, side_l, side_u, corner_l, corner_u, rule, stats, film,
     gradients, padded, hid, low, high, low_y, high_y, turned,
 ):
     cells, mean, inverse, scale, shift = norm_terms(stats, film)
@@ -204,8 +221,13 @@
         return carry
 
     lax.fori_loop(0, 4, local_part, 0)
-    for source, target in ((lower, low), (upper, high), (lower_y, low_y), (upper_y, high_y)):
-        target[...] = act(source[...].reshape(256, CHANNELS)).reshape(16, 16, CHANNELS)
+    for source, target in (
+        (lower[...], low),
+        (upper[...], high),
+        (beside_y(side_l, corner_l, 0), low_y),
+        (beside_y(side_u, corner_u, 0), high_y),
+    ):
+        target[...] = act(source.reshape(256, CHANNELS)).reshape(16, 16, CHANNELS)
     gather_blocks(rule, 0, hid, low, high, low_y, high_y, padded)
 
     row, col = iota((256, CHANNELS), 0), iota((256, CHANNELS), 1)
@@ -245,12 +267,22 @@
 
 
 def field_kernel(
-    counts, held, up, lower, upper, lower_y, upper_y, rule, stats, film, weight, padded,
-    output, kept, sums, wide, acc_m, acc_b,
+    counts, held, up, lower, upper, side_l, side_u, corner_l, corner_u, rule, stats, film,
+    weight_at, padded_at, output, kept, sums, wide, acc_m, acc_b, low_y, high_y, weight, padded, done,
 ):
+    copies = [
+        pltpu.make_async_copy(weight_at, weight, done.at[0]),
+        pltpu.make_async_copy(padded_at, padded, done.at[1]),
+    ]
+    for copy in copies:
+        copy.start()
     count = counts[0]
     cells, mean, inverse, scale, shift = norm_terms(stats, film)
-    gather_blocks(rule, 8, up, lower, upper, lower_y, upper_y, wide)
+    low_y[...] = beside_y(side_l, corner_l, 1).astype(BF16)
+    high_y[...] = beside_y(side_u, corner_u, 1).astype(BF16)
+    gather_blocks(rule, 8, up, lower, upper, low_y, high_y, wide)
+    for copy in copies:
+        copy.wait()
     acc_m[...] = jnp.zeros_like(acc_m)
     acc_b[...] = jnp.zeros_like(acc_b)
 
@@ -347,17 +379,19 @@
 
 SMEM = pl.BlockSpec(memory_space=pltpu.SMEM)
 VMEM = pl.BlockSpec(memory_space=pltpu.VMEM)
-
-
-def call(kernel, scalars, arrays, outs, scratch=(), flops=0, name=None):
+ANY = pl.BlockSpec(memory_space=pl.ANY)
+
+
+def call(kernel, scalars, arrays, outs, scratch=(), flops=0, name=None, left=0):
     shapes = [jax.ShapeDtypeStruct(shape, dtype) for shape, dtype in outs]
     moved = sum(x.size * x.dtype.itemsize for x in [*arrays, *shapes])
     return pl.pallas_call(
         kernel,
         out_shape=shapes,
-        in_specs=[SMEM] * len(scalars) + [VMEM] * len(arrays),
+        in_specs=[SMEM] * len(scalars) + [VMEM] * (len(arrays) - left) + [ANY] * left,
         out_specs=[VMEM] * len(outs),
-        scratch_shapes=[pltpu.VMEM(*s) for s in scratch],
+        scratch_shapes=[pltpu.VMEM(*s) for s in scratch]
+        + ([pltpu.SemaphoreType.DMA((left,))] if left else []),
         compiler_params=pltpu.CompilerParams(vmem_limit_bytes=VMEM_LIMIT),
         cost_estimate=pl.CostEstimate(flops=flops, bytes_accessed=moved, transcendentals=0),
         name=name,
@@ -375,11 +409,12 @@
     block = ((VOXELS, 16, CHANNELS), BF16)
     face = ((16, 16, CHANNELS), BF16)
     spaced = ((6, 6, 6, 16, CHANNELS), BF16)
-    held, up, stats, faces, film = call(
+    joined = ((2, 16, 16, 384), BF16)
+    held, up, stats, faces, sides, film = call(
         pack_kernel,
-        [count, send_x[0, 0]],
+        [count, send_x[0, 0], send_y[0, 0]],
         [features[0, 0], cotangent[0, 0], action[None], film_weight],
-        [block, block, ((size_x, 4, 128), F32), ((2, *face[0]), BF16), ((1, 2 * CHANNELS), F32)],
+        [block, block, ((size_y, 4, 128), F32), ((2, *face[0]), BF16), joined, ((1, 2 * CHANNELS), F32)],
         flops=10**9,
         name="pack",
     )
@@ -389,25 +424,25 @@
     down_y = [(i + 1, i) for i in range(size_y - 1)]
     lower = lax.ppermute(faces[1], "gx", up_x)
     upper = lax.ppermute(faces[0], "gx", down_x)
-    stats = exchange(stats, "gx")
+    side_l = lax.ppermute(sides[1], "gy", up_y)
+    side_u = lax.ppermute(sides[0], "gy", down_y)
+    stats = exchange(stats, "gy")
     weight = jnp.transpose(conv_weight, (1, 0, 2))
-    cross, cross_up, stats = call(
+    corners, stats = call(
         cross_kernel,
         [send_y[0, 0]],
-        [held, up, lower, upper, stats],
-        [((2, *face[0]), BF16), ((2, *face[0]), BF16), ((size_y, 4, 128), F32)],
+        [lower, upper, stats],
+        [((2, 8, 16, 384), BF16), ((size_x, 4, 128), F32)],
         flops=10**8,
         name="cross",
     )
-    lower_y = lax.ppermute(cross[1], "gy", up_y)
-    upper_y = lax.ppermute(cross[0], "gy", down_y)
-    lower_u = lax.ppermute(cross_up[1], "gy", up_y)
-    upper_u = lax.ppermute(cross_up[0], "gy", down_y)
-    stats = exchange(stats, "gy")
+    corner_l = lax.ppermute(corners[1], "gy", up_y)
+    corner_u = lax.ppermute(corners[0], "gy", down_y)
+    stats = exchange(stats, "gx")
     gradients, padded = call(
         weight_kernel,
         [count],
-        [held, up, lower, upper, lower_y, upper_y, rule, stats, film],
+        [held, up, lower, upper, side_l, side_u, corner_l, corner_u, rule, stats, film],
         [((16, TILES, 16, 384), BF16), spaced],
         [block, face, face, face, face, ((4, 256, 1024), BF16)],
         flops=4 * 10**9,
@@ -417,11 +452,12 @@
     output, kept, sums = call(
         field_kernel,
         [count],
-        [held, up, lower, upper, lower_u, upper_u, rule, stats, film, weight, padded],
+        [held, up, lower, upper, side_l, side_u, corner_l, corner_u, rule, stats, film, weight, padded],
         [((SLOTS, VOXELS, CHANNELS), BF16), ((1024, CHANNELS), F32), ((4, 128), F32)],
-        [spaced, ((1024, CHANNELS), F32), ((1024, CHANNELS), F32)],
+        [spaced, ((1024, CHANNELS), F32), ((1024, CHANNELS), F32), face, face, ((27, 192, 192), BF16), spaced],
         flops=6 * 10**9,
         name="field",
+        left=2,
     )
     sums = lax.all_gather(sums, "gx")
     (shares,) = call(share_kernel, [], [gradients, sums], [((size_y, 24, 128), BF16)], name="share")

time: 191 us -> 166 us (0.87)
  waiting for transfers between devices: 43.1 us -> 12.4 us
  blocking collectives: 55.6 us -> 65.9 us
  starting transfers between devices: 44.6 us -> 39.6 us
    ppermute x4, waiting for transfers between devices: 35.5 us -> 0.01 us  [the longest x1 0.01 us: body(): side_u = lax.ppermute(sides[0], 'gy', down_y)]
    all_to_all x2, blocking collectives: 30.8 us -> 39.4 us  [exchange(): return lax.all_to_all(array, axis, 0, 0, tiled=True)]
    all_to_all x3, waiting for transfers between devices: 7.6 us -> 12.4 us  [exchange(): return lax.all_to_all(array, axis, 0, 0, tiled=True)]
    all_to_all x3, starting transfers between devices: 23.4 us -> 20.7 us  [exchange(): return lax.all_to_all(array, axis, 0, 0, tiled=True)]
    ppermute x4, starting transfers between devices: 11.1 us -> 8.76 us  [the longest x1 4.04 us: body(): side_l = lax.ppermute(sides[1], 'gy', up_y)]
    unnamed x22 -> x20, local copies, waits for them, and re-layouts: 4.08 us -> 3.43 us
  transfers between devices with their start and end apart: 9 -> 9, of which waited for: 4 -> 2; matrix products, arithmetic and copies ran while one was open for 1% -> 2% of each run, Pallas kernels for 9% -> 12%
where the time goes in v3:
time: 166 us; the launch traced here: 165 us
  blocking collectives  65.9 us (40%)
  starting transfers between devices  39.6 us (24%)
  Pallas kernels  38.2 us (23%)
  waiting for transfers between devices  12.4 us (7%)
  local copies, waits for them, and re-layouts  7.17 us (4%)
    all_to_all x2, blocking collectives, exchange(): return lax.all_to_all(array, axis, 0, 0, tiled=True)  39.4 us
    pallas_call x8, Pallas kernels, call(): pl.pallas_call(kernel, out_shape=shapes, in_specs=[SMEM] * len(scalars) +...  38.2 us
    all_gather x1, blocking collectives, body(): sums = lax.all_gather(sums, 'gx')  26.4 us
    all_to_all x3, starting transfers between devices, exchange(): return lax.all_to_all(array, axis, 0, 0, tiled=True)  20.7 us
    all_to_all x3, waiting for transfers between devices, exchange(): return lax.all_to_all(array, axis, 0, 0, tiled=True)  12.4 us
    ppermute x1, starting transfers between devices, body(): upper = lax.ppermute(faces[0], 'gx', down_x)  5.49 us
    ppermute x1, starting transfers between devices, body(): lower = lax.ppermute(faces[1], 'gx', up_x)  4.6 us
    ppermute x1, starting transfers between devices, body(): side_l = lax.ppermute(sides[1], 'gy', up_y)  4.04 us
  transfers between devices with their start and end apart: 9, of which 2 were waited for; matrix products, arithmetic and copies ran while one was open for 2% of the time, Pallas kernels for 12%

profile of v3, /device:TPU:1, one launch (start us, length us, event | category | flops | bytes accessed | tf_op | source)
XLA Modules:
  0.0 164.7 jit_solution(2545401822475215744)
XLA Ops:
  1.3 3.0 %pack.1 = (bf16[64,16,192]{2,1,0:T(8,128)(2,1)}, bf16[64,16,192]{2,1,0:T(8,128)(2,1)}, f32[32,4,128]{2,1,0:T(4,128)}, bf16[2,16,16,192]{3,2,1,0:T(8,128)(2,1)}, ...) custom-call(s32[1]{0:T(128)} %bitcast.24.counts, s32[2,8]{1,0:T(2,128)} %bitcast.36, s32[2,12]{1,0:T(2,128)} %bitcast.37, ...), custom_call_target="tpu_custom_call" | custom-call | flops 1000000000 | bytes 2426880 | tf_op jit(solution)/shard_map/pack/pallas_call | solution.py:388
  4.2 1.0 slice_bitcast_fusion.2
  5.2 4.6 %collective-permute-start = (bf16[16,16,192]{2,1,0:T(8,128)(2,1)S(1)}, bf16[16,16,192]{2,1,0:T(8,128)(2,1)S(1)}, u32[]{:S(2)}, u32[]{:S(2)}) collective-permute-start(bf16[16,16,192]{2,1,0:T(8,128)(2,1)S(1)} %get-tuple-element.41), channel_id=1, source_target_pairs={{0,32},{32,64},{64,96},{96,128},{128,160},{160,192},{192,224},{224... | collective-permute-start | bytes 294920 | tf_op jit(solution)/shard_map/ppermute | solution.py:425
  9.8 5.5 %collective-permute-start.1 = (bf16[16,16,192]{2,1,0:T(8,128)(2,1)S(1)}, bf16[16,16,192]{2,1,0:T(8,128)(2,1)S(1)}, u32[]{:S(2)}, u32[]{:S(2)}) collective-permute-start(bf16[16,16,192]{2,1,0:T(8,128)(2,1)S(1)} %get-tuple-element.40), channel_id=1, source_target_pairs={{32,0},{64,32},{96,64},{128,96},{160,128},{192,160},{224,192},{256... | collective-permute-start | bytes 294920 | tf_op jit(solution)/shard_map/ppermute | solution.py:426
  15.3 11.2 %all-to-all-start = ((f32[32,4,128]{2,1,0:T(4,128)}), f32[32,4,128]{2,1,0:T(4,128)S(1)}, u32[]{:S(2)}, u32[]{:S(2)}) async-start(f32[32,4,128]{2,1,0:T(4,128)} %get-tuple-element.25), calls=%async_computation | async-start | bytes 131072 | tf_op jit(solution)/shard_map/all_to_all | solution.py:402
  26.6 1.1 slice_bitcast_fusion
  27.6 4.0 %collective-permute-start.2 = (bf16[16,16,384]{2,1,0:T(8,128)(2,1)S(1)}, bf16[16,16,384]{2,1,0:T(8,128)(2,1)S(1)}, u32[]{:S(2)}, u32[]{:S(2)}) collective-permute-start(bf16[16,16,384]{2,1,0:T(8,128)(2,1)S(1)} %get-tuple-element.39), channel_id=1, source_target_pairs={{0,1},{1,2},{2,3},{3,4},{4,5},{5,6},{6,7},{7,8},{8,9},{9,10},{10,1... | collective-permute-start | bytes 589832 | tf_op jit(solution)/shard_map/ppermute | solution.py:427
  31.7 1.3 collective-permute-start.3
  33.0 0.0 collective-permute-done.lower
  33.0 0.0 copy-start.6
  33.0 0.0 collective-permute-done.1.upper
  33.0 0.0 copy-start.7
  33.0 4.8 %all-to-all-done.stats = f32[32,4,128]{2,1,0:T(4,128)S(1)} async-done(((f32[32,4,128]{2,1,0:T(4,128)}), f32[32,4,128]{2,1,0:T(4,128)S(1)}, u32[]{:S(2)}, u32[]{:S(2)}) %all-to-all-start) | async-done | bytes 65568 | tf_op jit(solution)/shard_map/all_to_all | solution.py:402
  37.8 0.0 copy-done.6
  37.8 0.0 copy-done.7
  37.8 0.0 copy-start.2
  37.8 0.6 copy-done.2
  38.5 1.9 %cross.1 = (bf16[2,8,16,384]{3,2,1,0:T(8,128)(2,1)}, f32[16,4,128]{2,1,0:T(4,128)}) custom-call(s32[2,12]{1,0:T(2,128)} %bitcast.38, bf16[16,16,192]{2,1,0:T(8,128)(2,1)} %copy-done.6, bf16[16,16,192]{2,1,0:T(8,128)(2,1)} %copy-done.7, f32[32,4,128]{2,1,0:T(4,128)} %copy-done.2), custom_call_target="tpu_custom_call" | custom-call | flops 100000000 | bytes 491520 | tf_op jit(solution)/shard_map/cross/pallas_call | solution.py:388
  40.4 1.0 slice_bitcast_fusion.4
  41.4 2.1 %collective-permute-start.4 = (bf16[8,16,384]{2,1,0:T(8,128)(2,1)S(1)}, bf16[8,16,384]{2,1,0:T(8,128)(2,1)S(1)}, u32[]{:S(2)}, u32[]{:S(2)}) collective-permute-start(bf16[8,16,384]{2,1,0:T(8,128)(2,1)S(1)} %get-tuple-element.43), channel_id=1, source_target_pairs={{0,1},{1,2},{2,3},{3,4},{4,5},{5,6},{6,7},{7,8},{8,9},{9,10},{10,1... | collective-permute-start | bytes 294920 | tf_op jit(solution)/shard_map/ppermute | solution.py:439
  43.5 1.3 collective-permute-start.5
  44.8 14.3 %all_to_all.25.stats = f32[16,4,128]{2,1,0:T(4,128)} all-to-all(f32[16,4,128]{2,1,0:T(4,128)} %get-tuple-element.27), channel_id=1, replica_groups=mesh['gx'=16,'gy'=32] {'gx'}, dimensions={0} | all-to-all | bytes 65536 | tf_op jit(solution)/shard_map/all_to_all | solution.py:402
  59.2 0.0 collective-permute-done.2.side_l
  59.2 0.0 copy-start.4
  59.2 0.0 collective-permute-done.3.side_u
  59.2 0.0 copy-start.5
  59.2 0.0 collective-permute-done.4.corner_l
  59.2 0.0 copy-start.8
  59.2 0.0 collective-permute-done.5.corner_u
  59.2 0.0 copy-start.9
  59.2 0.6 copy-done.4
  59.9 0.1 copy-done.5
  59.9 0.0 copy-done.8
  59.9 0.1 copy-done.9
  60.0 9.4 %weight.1 = (bf16[16,11,16,384]{3,2,1,0:T(8,128)(2,1)}, bf16[6,6,6,16,192]{4,3,2,1,0:T(8,128)(2,1)}) custom-call(s32[1]{0:T(128)} %bitcast.25.counts, bf16[64,16,192]{2,1,0:T(8,128)(2,1)} %get-tuple-element.21.held, bf16[64,16,192]{2,1,0:T(8,128)(2,1)} %get-tuple-element.22.up, bf16[16,16,192]{2,1,0:T(8,128)(2,1)} %copy-done.6, ...), custom_call_target="tpu_custom_call" | custom-call | flops 4000000000 | bytes 5098688 | tf_op jit(solution)/shard_map/weight/pallas_call | solution.py:388
  69.4 3.9 %all-to-all-start.2 = ((bf16[16,11,16,384]{3,2,1,0:T(8,128)(2,1)}), bf16[16,11,16,384]{3,2,1,0:T(8,128)(2,1)S(1)}, u32[]{:S(2)}, u32[]{:S(2)}) async-start(bf16[16,11,16,384]{3,2,1,0:T(8,128)(2,1)} %get-tuple-element.31), calls=%async_computation.2 | async-start | bytes 4325376 | tf_op jit(solution)/shard_map/all_to_all | solution.py:402
  73.3 14.8 %field.1 = (bf16[16,64,192]{2,1,0:T(8,128)(2,1)}, f32[1024,192]{1,0:T(8,128)}, f32[4,128]{1,0:T(4,128)}) custom-call(s32[1]{0:T(128)} %bitcast.26.counts, bf16[64,16,192]{2,1,0:T(8,128)(2,1)} %get-tuple-element.21.held, bf16[64,16,192]{2,1,0:T(8,128)(2,1)} %get-tuple-element.22.up, bf16[16,16,192]{2,1,0:T(8,128)(2,1)} %copy-done.6, ...), custom_call_target="tpu_custom_call" | custom-call | flops 6000000000 | bytes 6108352 | tf_op jit(solution)/shard_map/field/pallas_call | solution.py:388
  88.1 0.0 copy-start.3
  88.1 26.4 %all-gather.1.sums = f32[16,4,128]{2,1,0:T(4,128)} all-gather(f32[1,4,128]{2,1,0:T(4,128)} %bitcast.28), channel_id=2, replica_groups=mesh['gx'=16,'gy'=32] {'gx'}, dimensions={0}, use_global_device_ids=true | all-gather | bytes 34816 | tf_op jit(solution)/shard_map/all_gather | solution.py:462
  114.5 0.0 all-to-all-done.2.parts
  114.5 0.0 copy-start
  114.5 1.4 copy-done
  115.9 2.6 %share.1 = bf16[32,24,128]{2,1,0:T(8,128)(2,1)} custom-call(bf16[16,11,16,384]{3,2,1,0:T(8,128)(2,1)} %copy-done, f32[16,4,128]{2,1,0:T(4,128)} %all-gather.1.sums), custom_call_target="tpu_custom_call" | custom-call | bytes 2392064 | tf_op jit(solution)/shard_map/share/pallas_call | solution.py:388
  118.5 25.1 %all_to_all.26.parts = bf16[32,24,128]{2,1,0:T(8,128)(2,1)} all-to-all(bf16[32,24,128]{2,1,0:T(8,128)(2,1)} %share.1), channel_id=1, replica_groups=mesh['gx'=16,'gy'=32] {'gy'}, dimensions={0} | all-to-all | bytes 393216 | tf_op jit(solution)/shard_map/all_to_all | solution.py:402
  143.6 1.6 own.1
  145.2 5.6 %all-to-all-start.4 = ((bf16[32,16,128]{2,1,0:T(8,128)(2,1)}), bf16[32,16,128]{2,1,0:T(8,128)(2,1)S(1)}, u32[]{:S(2)}, u32[]{:S(2)}) async-start(bf16[32,16,128]{2,1,0:T(8,128)(2,1)} %get-tuple-element.36), calls=%async_computation.4 | async-start | bytes 262144 | tf_op jit(solution)/shard_map/all_to_all | solution.py:402
  150.8 0.0 copy-done.3
  150.8 0.7 copy.14.action
  151.6 2.9 %finish.1 = (f32[128,384]{1,0:T(8,128)}, bf16[16,64,192]{2,1,0:T(8,128)(2,1)}) custom-call(s32[1]{0:T(128)} %bitcast.27.counts, f32[8,128]{1,0:T(8,128)} %get-tuple-element.33.sums, f32[16,4,128]{2,1,0:T(4,128)} %all_to_all.25.stats, f32[1,384]{1,0:T(1,128)} %get-tuple-element.28.film, f32[128,1]{1,0:T(8,128)} %copy.14.action, ...), custom_call_target="tpu_custom_call" | custom-call | flops 1000000000 | bytes 1808384 | tf_op jit(solution)/shard_map/finish/pallas_call | solution.py:388
  154.5 7.6 %all-to-all-done.4.tiles = bf16[32,16,128]{2,1,0:T(8,128)(2,1)S(1)} async-done(((bf16[32,16,128]{2,1,0:T(8,128)(2,1)}), bf16[32,16,128]{2,1,0:T(8,128)(2,1)S(1)}, u32[]{:S(2)}, u32[]{:S(2)}) %all-to-all-start.4) | async-done | bytes 131104 | tf_op jit(solution)/shard_map/all_to_all | solution.py:402
  162.1 0.0 copy-start.1
  162.1 0.6 copy-done.1
  162.8 2.0 %unpack.1 = f32[12,27,192]{2,1,0:T(8,128)} custom-call(bf16[32,16,128]{2,1,0:T(8,128)(2,1)} %copy-done.1), custom_call_target="tpu_custom_call" | custom-call | bytes 379904 | tf_op jit(solution)/shard_map/unpack/pallas_call | solution.py:388
Async XLA Ops:
  5.2 27.8 %collective-permute-start = (bf16[16,16,192]{2,1,0:T(8,128)(2,1)S(1)}, bf16[16,16,192]{2,1,0:T(8,128)(2,1)S(1)}, u32[]{:S(2)}, u32[]{:S(2)}) collective-permute-start(bf16[16,16,192]{2,1,0:T(8,128)(2,1)S(1)} %get-tuple-element.41), channel_id=1, source_target_pairs={{0,32},{32,64},{64,96},{96,128},{128,160},{160,192},{192,224},{224... | collective-permute-start | bytes 294920 | tf_op jit(solution)/shard_map/ppermute | solution.py:425
  9.8 23.2 %collective-permute-start.1 = (bf16[16,16,192]{2,1,0:T(8,128)(2,1)S(1)}, bf16[16,16,192]{2,1,0:T(8,128)(2,1)S(1)}, u32[]{:S(2)}, u32[]{:S(2)}) collective-permute-start(bf16[16,16,192]{2,1,0:T(8,128)(2,1)S(1)} %get-tuple-element.40), channel_id=1, source_target_pairs={{32,0},{64,32},{96,64},{128,96},{160,128},{192,160},{224,192},{256... | collective-permute-start | bytes 294920 | tf_op jit(solution)/shard_map/ppermute | solution.py:426
  15.3 22.5 %all-to-all-start = ((f32[32,4,128]{2,1,0:T(4,128)}), f32[32,4,128]{2,1,0:T(4,128)S(1)}, u32[]{:S(2)}, u32[]{:S(2)}) async-start(f32[32,4,128]{2,1,0:T(4,128)} %get-tuple-element.25), calls=%async_computation | async-start | bytes 131072 | tf_op jit(solution)/shard_map/all_to_all | solution.py:402
  27.6 31.5 %collective-permute-start.2 = (bf16[16,16,384]{2,1,0:T(8,128)(2,1)S(1)}, bf16[16,16,384]{2,1,0:T(8,128)(2,1)S(1)}, u32[]{:S(2)}, u32[]{:S(2)}) collective-permute-start(bf16[16,16,384]{2,1,0:T(8,128)(2,1)S(1)} %get-tuple-element.39), channel_id=1, source_target_pairs={{0,1},{1,2},{2,3},{3,4},{4,5},{5,6},{6,7},{7,8},{8,9},{9,10},{10,1... | collective-permute-start | bytes 589832 | tf_op jit(solution)/shard_map/ppermute | solution.py:427
  31.7 27.5 %collective-permute-start.3 = (bf16[16,16,384]{2,1,0:T(8,128)(2,1)S(1)}, bf16[16,16,384]{2,1,0:T(8,128)(2,1)S(1)}, u32[]{:S(2)}, u32[]{:S(2)}) collective-permute-start(bf16[16,16,384]{2,1,0:T(8,128)(2,1)S(1)} %get-tuple-element.38), channel_id=1, source_target_pairs={{1,0},{2,1},{3,2},{4,3},{5,4},{6,5},{7,6},{8,7},{9,8},{10,9},{11,1... | collective-permute-start | bytes 589832 | tf_op jit(solution)/shard_map/ppermute | solution.py:428
  33.0 4.8 %copy-start.6 = (bf16[16,16,192]{2,1,0:T(8,128)(2,1)}, bf16[16,16,192]{2,1,0:T(8,128)(2,1)S(1)}, u32[]{:S(2)}) copy-start(bf16[16,16,192]{2,1,0:T(8,128)(2,1)S(1)} %collective-permute-done.lower) | copy-start | bytes 294916
  33.0 4.8 %copy-start.7 = (bf16[16,16,192]{2,1,0:T(8,128)(2,1)}, bf16[16,16,192]{2,1,0:T(8,128)(2,1)S(1)}, u32[]{:S(2)}) copy-start(bf16[16,16,192]{2,1,0:T(8,128)(2,1)S(1)} %collective-permute-done.1.upper) | copy-start | bytes 294916
  37.8 0.6 copy-start.2
  41.4 17.8 %collective-permute-start.4 = (bf16[8,16,384]{2,1,0:T(8,128)(2,1)S(1)}, bf16[8,16,384]{2,1,0:T(8,128)(2,1)S(1)}, u32[]{:S(2)}, u32[]{:S(2)}) collective-permute-start(bf16[8,16,384]{2,1,0:T(8,128)(2,1)S(1)} %get-tuple-element.43), channel_id=1, source_target_pairs={{0,1},{1,2},{2,3},{3,4},{4,5},{5,6},{6,7},{7,8},{8,9},{9,10},{10,1... | collective-permute-start | bytes 294920 | tf_op jit(solution)/shard_map/ppermute | solution.py:439
  43.5 15.7 %collective-permute-start.5 = (bf16[8,16,384]{2,1,0:T(8,128)(2,1)S(1)}, bf16[8,16,384]{2,1,0:T(8,128)(2,1)S(1)}, u32[]{:S(2)}, u32[]{:S(2)}) collective-permute-start(bf16[8,16,384]{2,1,0:T(8,128)(2,1)S(1)} %get-tuple-element.42), channel_id=1, source_target_pairs={{1,0},{2,1},{3,2},{4,3},{5,4},{6,5},{7,6},{8,7},{9,8},{10,9},{11,1... | collective-permute-start | bytes 294920 | tf_op jit(solution)/shard_map/ppermute | solution.py:440
  59.2 0.7 copy-start.4
  59.2 0.7 copy-start.5
  59.2 0.7 copy-start.8
  59.2 0.8 copy-start.9
  69.4 45.1 %all-to-all-start.2 = ((bf16[16,11,16,384]{3,2,1,0:T(8,128)(2,1)}), bf16[16,11,16,384]{3,2,1,0:T(8,128)(2,1)S(1)}, u32[]{:S(2)}, u32[]{:S(2)}) async-start(bf16[16,11,16,384]{3,2,1,0:T(8,128)(2,1)} %get-tuple-element.31), calls=%async_computation.2 | async-start | bytes 4325376 | tf_op jit(solution)/shard_map/all_to_all | solution.py:402
  88.1 62.7 %copy-start.3 = (f32[128]{0:T(128)S(1)}, f32[128]{0:T(128)}, u32[]{:S(2)}) copy-start(f32[128]{0:T(128)} %param.15) | copy-start | bytes 1540
  114.5 1.4 copy-start
  145.2 16.9 %all-to-all-start.4 = ((bf16[32,16,128]{2,1,0:T(8,128)(2,1)}), bf16[32,16,128]{2,1,0:T(8,128)(2,1)S(1)}, u32[]{:S(2)}, u32[]{:S(2)}) async-start(bf16[32,16,128]{2,1,0:T(8,128)(2,1)} %get-tuple-element.36), calls=%async_computation.4 | async-start | bytes 262144 | tf_op jit(solution)/shard_map/all_to_all | solution.py:402
  162.1 0.7 copy-start.1

commit v4 on v2

--- a/solution.py
+++ b/solution.py
@@ -70,9 +70,21 @@
     return block
 
 
-def pack_kernel(counts, send_x, feat, cot, action, film_weight, held, up, stats, faces, film):
-    count = counts[0]
-    swap = swap_matrix(count)
+def join_fields(value):
+    first, second = value[0:16], value[16:32]
+    rest = jnp.concatenate([first[:, 128:], second[:, 128:]], axis=1)
+    return jnp.concatenate([first[:, :128], second[:, :128], rest], axis=1).astype(BF16)
+
+
+def one_field(joined, which):
+    tail = joined[..., 256:320] if which == 0 else joined[..., 320:384]
+    return jnp.concatenate([joined[..., 128 * which : 128 * which + 128], tail], axis=-1)
+
+
+def pack_kernel(
+    counts, send_x, feat, cot, action, film_weight, held, up, stats, faces, film
+):
+    swap = swap_matrix(counts[0])
     total = jnp.zeros((1, CHANNELS), F32)
     square = jnp.zeros((1, CHANNELS), F32)
     for g in range(4):
@@ -83,7 +95,7 @@
         held[part, :, :] = moved.astype(BF16).reshape(16, 16, CHANNELS)
         moved = dot(swap, cot[:, part, :].reshape(256, CHANNELS))
         up[part, :, :] = moved.astype(BF16).reshape(16, 16, CHANNELS)
-    cells = (count * VOXELS).astype(F32)
+    cells = (counts[0] * VOXELS).astype(F32)
     block = stack_lines(pack_lines(total, square) + [cells], 4)
     for i in range(stats.shape[0]):
         stats[i, :, :] = block
@@ -101,11 +113,12 @@
     )
 
 
-def cross_kernel(send_y, held, up, lower, upper, stats, faces, up_faces, spread):
+def cross_kernel(send_y, held, up, lower, upper, stats, face_low, face_high, spread):
     block = jnp.sum(stats[...], axis=0)
     for i in range(spread.shape[0]):
         spread[i, :, :] = block
     for side in range(2):
+        target = (face_low, face_high)[side]
         column = list_column(send_y, side, 12, 32, 16)
         local = pick(column, 32, 0, SLOTS, 0, 16, 16)
         from_lower = pick(column, 16, 17, 25, 0, 8, 16)
@@ -118,9 +131,7 @@
                     value += dot(from_lower, lower[12 * side + c])
                 if a == 0:
                     value += dot(from_upper, upper[12 * side + c])
-                value = value.astype(BF16)
-                faces[side, 4 * a + c, :, :] = value[0:16]
-                up_faces[side, 4 * a + c, :, :] = value[16:32]
+                target[4 * a + c, :, :] = join_fields(value)
 
 
 def norm_terms(stats, film):
@@ -185,8 +196,8 @@
 
 
 def weight_kernel(
-    counts, held, up, lower, upper, lower_y, upper_y, rule, stats, film,
-    gradients, padded, hid, low, high, low_y, high_y, turned,
+    counts, core, held, up, lower, upper, side_l, side_u, rule, stats, film,
+    near, far, padded, hid, low, high, low_y, high_y, turned,
 ):
     cells, mean, inverse, scale, shift = norm_terms(stats, film)
 
@@ -204,12 +215,17 @@
         return carry
 
     lax.fori_loop(0, 4, local_part, 0)
-    for source, target in ((lower, low), (upper, high), (lower_y, low_y), (upper_y, high_y)):
-        target[...] = act(source[...].reshape(256, CHANNELS)).reshape(16, 16, CHANNELS)
+    for source, target in (
+        (lower[...], low),
+        (upper[...], high),
+        (one_field(side_l[...], 0), low_y),
+        (one_field(side_u[...], 0), high_y),
+    ):
+        target[...] = act(source.reshape(256, CHANNELS)).reshape(16, 16, CHANNELS)
     gather_blocks(rule, 0, hid, low, high, low_y, high_y, padded)
 
     row, col = iota((256, CHANNELS), 0), iota((256, CHANNELS), 1)
-    group = row >> 4
+    group = ((row >> 4) & 7) * 2 + jnp.where(row >= 128, 1 - core[0], core[0])
     wide = up[...].reshape(1024, CHANNELS)
     for m in range(4):
         place = (row + 4 * m) & 15
@@ -226,7 +242,9 @@
         return jnp.concatenate([grad1[:, :128], grad2[:, :128], rest], axis=1)
 
     def store(at, value):
-        gradients[:, pl.ds(at, 1), :, :] = value.astype(BF16).reshape(16, 1, 16, 384)
+        value = value.astype(BF16).reshape(16, 1, 16, 384)
+        near[:, pl.ds(at, 1), :, :] = value[:8]
+        far[:, pl.ds(at, 1), :, :] = value[8:]
 
     def step(q, carry):
         k = 8 * q
@@ -244,58 +262,102 @@
     store(10, jnp.where(line < 8, second, 0.0))
 
 
-def field_kernel(
-    counts, held, up, lower, upper, lower_y, upper_y, rule, stats, film, weight, padded,
-    output, kept, sums, wide, acc_m, acc_b,
+def back_kernel(
+    counts, held, up, lower, upper, side_l, side_u, rule, stats, film,
+    weight_at, kept, sums, wide, acc, low_y, high_y, weight, done,
 ):
-    count = counts[0]
+    copy = pltpu.make_async_copy(weight_at, weight, done.at[0])
+    copy.start()
     cells, mean, inverse, scale, shift = norm_terms(stats, film)
-    gather_blocks(rule, 8, up, lower, upper, lower_y, upper_y, wide)
-    acc_m[...] = jnp.zeros_like(acc_m)
-    acc_b[...] = jnp.zeros_like(acc_b)
+    low_y[...] = one_field(side_l[...], 1)
+    high_y[...] = one_field(side_u[...], 1)
+    gather_blocks(rule, 8, up, lower, upper, low_y, high_y, wide)
+    acc[...] = jnp.zeros_like(acc)
+    copy.wait()
+
+    def step(t, carry):
+        k = 3 * t
+        total = dot(window(wide, k), weight[26 - k])
+        total += dot(window(wide, k + 1), weight[25 - k])
+        acc[...] += total + dot(window(wide, k + 2), weight[24 - k])
+        return carry
+
+    lax.fori_loop(0, 9, step, 0)
+    shift_grad = jnp.zeros((1, CHANNELS), F32)
+    scale_grad = jnp.zeros((1, CHANNELS), F32)
+    live = (iota((256, 1), 0) & 15) < counts[0]
+    for g in range(4):
+        at = slice(256 * g, 256 * g + 256)
+        part = slice(16 * g, 16 * g + 16)
+        x = held[part, :, :].reshape(256, CHANNELS).astype(F32)
+        normed = (x - mean) * inverse
+        slope = jnp.where(live & (normed * scale + shift > 0), acc[at, :], 0.0)
+        shift_grad += jnp.sum(slope, axis=0, keepdims=True)
+        scale_grad += jnp.sum(slope * normed, axis=0, keepdims=True)
+        kept[at, :] = up[part, :, :].reshape(256, CHANNELS).astype(F32) + inverse * (slope * scale)
+    sums[...] = jnp.concatenate([scale_grad, shift_grad], axis=1)
+
+
+def split(value):
+    first = value.astype(BF16).astype(F32)
+    second = (value - first).astype(BF16).astype(F32)
+    return first, second, value - first - second
+
+
+def combine_kernel(near, other, sums, parts):
+    for i in range(8):
+        parts[i, :, :, :] = (near[i].astype(F32) + other[i].astype(F32)).astype(BF16)
+    row = iota((16, 384), 0)
+    lines = jnp.zeros((16, 384), F32)
+    for e, piece in enumerate(split(sums[...])):
+        lines = jnp.where(row == 8 + e, piece, lines)
+    for i in range(8):
+        held = parts[i, TILES - 1, :, :].astype(F32)
+        parts[i, TILES - 1, :, :] = jnp.where(row < 8, held, lines).astype(BF16)
+
+
+def forward_kernel(
+    counts, held, weight_at, padded_at, output, acc, weight, padded, done
+):
+    copies = [
+        pltpu.make_async_copy(weight_at, weight, done.at[0]),
+        pltpu.make_async_copy(padded_at, padded, done.at[1]),
+    ]
+    for copy in copies:
+        copy.start()
+    acc[...] = jnp.zeros_like(acc)
+    for copy in copies:
+        copy.wait()
 
     def step(t, carry):
         k = 3 * t
         total = dot_nt(window(padded, k), weight[k])
         total += dot_nt(window(padded, k + 1), weight[k + 1])
-        acc_m[...] += total + dot_nt(window(padded, k + 2), weight[k + 2])
-        total = dot(window(wide, k), weight[26 - k])
-        total += dot(window(wide, k + 1), weight[25 - k])
-        acc_b[...] += total + dot(window(wide, k + 2), weight[24 - k])
+        acc[...] += total + dot_nt(window(padded, k + 2), weight[k + 2])
         return carry
 
     lax.fori_loop(0, 9, step, 0)
-
     swap = swap_matrix(None)
-    shift_grad = jnp.zeros((1, CHANNELS), F32)
-    scale_grad = jnp.zeros((1, CHANNELS), F32)
-    live = (iota((256, 1), 0) & 15) < count
+    live = (iota((256, 1), 0) & 15) < counts[0]
     for g in range(4):
-        at = slice(256 * g, 256 * g + 256)
         part = slice(16 * g, 16 * g + 16)
         x = held[part, :, :].reshape(256, CHANNELS).astype(F32)
-        mixed = jnp.where(live, x + acc_m[at, :], 0.0).astype(BF16)
+        mixed = jnp.where(live, x + acc[256 * g : 256 * g + 256, :], 0.0).astype(BF16)
         output[:, part, :] = dot(swap, mixed).astype(BF16).reshape(16, 16, CHANNELS)
-        normed = (x - mean) * inverse
-        slope = jnp.where(live & (normed * scale + shift > 0), acc_b[at, :], 0.0)
-        shift_grad += jnp.sum(slope, axis=0, keepdims=True)
-        scale_grad += jnp.sum(slope * normed, axis=0, keepdims=True)
-        kept[at, :] = up[part, :, :].reshape(256, CHANNELS).astype(F32) + inverse * (slope * scale)
-    block = stack_lines(pack_lines(scale_grad, shift_grad), 4)
-    sums[...] = block
 
 
 def place_of(share):
     return (share // 3, share % 3) if share < 30 else (10, 2 * (share - 30))
 
 
-def share_kernel(parts, sums, shares):
-    lines = jnp.sum(sums[...], axis=0)
-    first = lines.astype(BF16).astype(F32)
-    second = lines - first
-    block = stack_lines([first[e : e + 1] for e in range(3)] + [second[e : e + 1] for e in range(3)], 8)
-    for tile in range(TILES):
+def share_kernel(parts, output, shares):
+    for tile in reversed(range(TILES)):
         total = jnp.sum(parts[:, tile, :, :].astype(F32), axis=0)
+        if tile == TILES - 1:
+            sums = total[8:9] + total[9:10] + total[10:11]
+            pieces = split(sums)[:2]
+            lines = [piece[:, 128 * m : 128 * m + 128] for piece in pieces for m in range(3)]
+            block = stack_lines(lines, 8)
         for share in range(32):
             if place_of(share)[0] == tile:
                 third = place_of(share)[1]
@@ -307,12 +369,13 @@
     total = jnp.sum(parts[...].astype(F32), axis=0)
     for i in range(mine.shape[0]):
         mine[i, :, :] = total[0:16].astype(BF16)
-    sums[...] = total[16:24]
-
-
-def finish_kernel(counts, sums, stats, film, action, held, kept, grad_film, grad_inputs):
-    lines = sums[0:3, :] + sums[3:6, :]
-    scale_grad, shift_grad = unpack_lines(lines)
+    lines = total[16:19] + total[19:22]
+    sums[...] = jnp.concatenate([lines[0:1], lines[1:2], lines[2:3]], axis=1)
+
+
+def finish_kernel(counts, sums, other, stats, film, action, held, kept, grad_film, grad_inputs):
+    total = sums[...] + other[...]
+    scale_grad, shift_grad = total[:, :CHANNELS], total[:, CHANNELS:]
     cells, mean, inverse, scale, shift = norm_terms(stats, film)
     grad_film[:, :CHANNELS] = action[...] * scale_grad
     grad_film[:, CHANNELS:] = action[...] * shift_grad
@@ -347,25 +410,28 @@
 
 SMEM = pl.BlockSpec(memory_space=pltpu.SMEM)
 VMEM = pl.BlockSpec(memory_space=pltpu.VMEM)
-
-
-def call(kernel, scalars, arrays, outs, scratch=(), flops=0, name=None):
+ANY = pl.BlockSpec(memory_space=pl.ANY)
+
+
+def call(kernel, scalars, arrays, outs, scratch=(), flops=0, name=None, left=0, sems=None):
+    sems = left if sems is None else sems
     shapes = [jax.ShapeDtypeStruct(shape, dtype) for shape, dtype in outs]
     moved = sum(x.size * x.dtype.itemsize for x in [*arrays, *shapes])
     return pl.pallas_call(
         kernel,
         out_shape=shapes,
-        in_specs=[SMEM] * len(scalars) + [VMEM] * len(arrays),
+        in_specs=[SMEM] * len(scalars) + [VMEM] * (len(arrays) - left) + [ANY] * left,
         out_specs=[VMEM] * len(outs),
-        scratch_shapes=[pltpu.VMEM(*s) for s in scratch],
+        scratch_shapes=[pltpu.VMEM(*s) for s in scratch]
+        + ([pltpu.SemaphoreType.DMA((sems,))] if sems else []),
         compiler_params=pltpu.CompilerParams(vmem_limit_bytes=VMEM_LIMIT),
         cost_estimate=pl.CostEstimate(flops=flops, bytes_accessed=moved, transcendentals=0),
         name=name,
     )(*scalars, *arrays)
 
 
-def exchange(array, axis):
-    return lax.all_to_all(array, axis, 0, 0, tiled=True)
+def exchange(array, axis, groups=None):
+    return lax.all_to_all(array, axis, 0, 0, axis_index_groups=groups, tiled=True)
 
 
 def body(features, cotangent, counts, neighbours, send_x, send_y, action, conv_weight, film_weight):
@@ -375,6 +441,7 @@
     block = ((VOXELS, 16, CHANNELS), BF16)
     face = ((16, 16, CHANNELS), BF16)
     spaced = ((6, 6, 6, 16, CHANNELS), BF16)
+    joined = ((16, 16, 384), BF16)
     held, up, stats, faces, film = call(
         pack_kernel,
         [count, send_x[0, 0]],
@@ -391,49 +458,68 @@
     upper = lax.ppermute(faces[0], "gx", down_x)
     stats = exchange(stats, "gx")
     weight = jnp.transpose(conv_weight, (1, 0, 2))
-    cross, cross_up, stats = call(
+    face_low, face_high, stats = call(
         cross_kernel,
         [send_y[0, 0]],
         [held, up, lower, upper, stats],
-        [((2, *face[0]), BF16), ((2, *face[0]), BF16), ((size_y, 4, 128), F32)],
+        [joined, joined, ((size_y, 4, 128), F32)],
         flops=10**8,
         name="cross",
     )
-    lower_y = lax.ppermute(cross[1], "gy", up_y)
-    upper_y = lax.ppermute(cross[0], "gy", down_y)
-    lower_u = lax.ppermute(cross_up[1], "gy", up_y)
-    upper_u = lax.ppermute(cross_up[0], "gy", down_y)
+    side_l = lax.ppermute(face_high, "gy", up_y)
+    side_u = lax.ppermute(face_low, "gy", down_y)
     stats = exchange(stats, "gy")
-    gradients, padded = call(
+    core = lax.axis_index("gx") & 1
+    swapped = [(i, i ^ 1) for i in range(size_x)]
+    fields = [held, up, lower, upper, side_l, side_u, rule, stats, film]
+    half = ((8, TILES, 16, 384), BF16)
+    near, far, padded = call(
         weight_kernel,
-        [count],
-        [held, up, lower, upper, lower_y, upper_y, rule, stats, film],
-        [((16, TILES, 16, 384), BF16), spaced],
+        [count, core.reshape(1)],
+        fields,
+        [half, half, spaced],
         [block, face, face, face, face, ((4, 256, 1024), BF16)],
         flops=4 * 10**9,
         name="weight",
     )
-    gradients = exchange(gradients, "gx")
-    output, kept, sums = call(
-        field_kernel,
+    other = lax.ppermute(far, "gx", swapped)
+    taps = ((27, CHANNELS, CHANNELS), BF16)
+    total = ((1024, CHANNELS), F32)
+    kept, sums = call(
+        back_kernel,
         [count],
-        [held, up, lower, upper, lower_u, upper_u, rule, stats, film, weight, padded],
-        [((SLOTS, VOXELS, CHANNELS), BF16), ((1024, CHANNELS), F32), ((4, 128), F32)],
-        [spaced, ((1024, CHANNELS), F32), ((1024, CHANNELS), F32)],
-        flops=6 * 10**9,
-        name="field",
-    )
-    sums = lax.all_gather(sums, "gx")
-    (shares,) = call(share_kernel, [], [gradients, sums], [((size_y, 24, 128), BF16)], name="share")
+        [*fields, weight],
+        [total, ((1, 2 * CHANNELS), F32)],
+        [spaced, total, face, face, taps],
+        flops=3 * 10**9,
+        name="back",
+        left=1,
+    )
+    (parts,) = call(combine_kernel, [], [near, other, sums], [half], name="combine")
+    parts = exchange(parts, "gx", [list(range(c, size_x, 2)) for c in range(2)])
+    (output,) = call(
+        forward_kernel,
+        [count],
+        [held, weight, padded],
+        [((SLOTS, VOXELS, CHANNELS), BF16)],
+        [total, taps, spaced],
+        flops=3 * 10**9,
+        name="forward",
+        left=2,
+    )
+    (shares,) = call(
+        share_kernel, [], [parts, output], [((size_y, 24, 128), BF16)], name="share", left=1, sems=0
+    )
     shares = exchange(shares, "gy")
     mine, sums = call(
-        own_kernel, [], [shares], [((size_y, 16, 128), BF16), ((8, 128), F32)], name="own"
-    )
+        own_kernel, [], [shares], [((size_y, 16, 128), BF16), ((1, 2 * CHANNELS), F32)], name="own"
+    )
+    other = lax.ppermute(sums, "gx", swapped)
     tiles = exchange(mine, "gy")
     grad_film, grad_inputs = call(
         finish_kernel,
         [count],
-        [sums, stats, film, action[:, None], held, kept],
+        [sums, other, stats, film, action[:, None], held, kept],
         [((128, 2 * CHANNELS), F32), ((SLOTS, VOXELS, CHANNELS), BF16)],
         flops=10**9,
         name="finish",

time: 191 us -> 151 us (0.79)
  blocking collectives: 55.6 us -> 25.3 us
  waiting for transfers between devices: 43.1 us -> 21.6 us
  Pallas kernels: 38.3 us -> 46.7 us
  starting transfers between devices: 44.6 us -> 48.3 us
    ppermute x4, waiting for transfers between devices: 35.5 us -> 0.27 us  [the longest x1 0.26 us: body(): other = lax.ppermute(sums, 'gx', swapped)]
    all_gather x1 -> x0, blocking collectives: 24.8 us -> none  [body(): sums = lax.all_gather(sums, 'gx')]
    all_to_all x3, waiting for transfers between devices: 7.6 us -> 21.3 us  [exchange(): lax.all_to_all(array, axis, 0, 0, axis_index_groups=groups, tiled=True)]
    pallas_call x8 -> x10, Pallas kernels: 38.3 us -> 46.7 us  [call(): pl.pallas_call(kernel, out_shape=shapes, in_specs=[SMEM] * len(scalars) +...]
    all_to_all x2, blocking collectives: 30.8 us -> 25.3 us  [exchange(): lax.all_to_all(array, axis, 0, 0, axis_index_groups=groups, tiled=True)]
    all_to_all x3, starting transfers between devices: 23.4 us -> 26.5 us  [exchange(): lax.all_to_all(array, axis, 0, 0, axis_index_groups=groups, tiled=True)]
    unnamed x22 -> x20, local copies, waits for them, and re-layouts: 4.08 us -> 4.67 us
  transfers between devices with their start and end apart: 9 -> 9, of which waited for: 4 -> 4; matrix products, arithmetic and copies ran while one was open for 1% -> 0% of each run, Pallas kernels for 9% -> 15%
where the time goes in v4:
time: 151 us; the launch traced here: 150 us
  starting transfers between devices  48.3 us (32%)
  Pallas kernels  46.7 us (31%)
  blocking collectives  25.3 us (17%)
  waiting for transfers between devices  21.6 us (14%)
  local copies, waits for them, and re-layouts  6.39 us (4%)
    pallas_call x10, Pallas kernels, call(): pl.pallas_call(kernel, out_shape=shapes, in_specs=[SMEM] * len(scalars) +...  46.7 us
    all_to_all x3, starting transfers between devices, exchange(): lax.all_to_all(array, axis, 0, 0, axis_index_groups=groups, tiled=True)  26.5 us
    all_to_all x2, blocking collectives, exchange(): lax.all_to_all(array, axis, 0, 0, axis_index_groups=groups, tiled=True)  25.3 us
    all_to_all x3, waiting for transfers between devices, exchange(): lax.all_to_all(array, axis, 0, 0, axis_index_groups=groups, tiled=True)  21.3 us
    ppermute x1, starting transfers between devices, body(): upper = lax.ppermute(faces[0], 'gx', down_x)  5.49 us
    unnamed x20, local copies, waits for them, and re-layouts  4.67 us
    ppermute x1, starting transfers between devices, body(): lower = lax.ppermute(faces[1], 'gx', up_x)  4.59 us
    ppermute x1, starting transfers between devices, body(): other = lax.ppermute(far, 'gx', swapped)  4.2 us
  transfers between devices with their start and end apart: 9, of which 4 were waited for; matrix products, arithmetic and copies ran while one was open for 0% of the time, Pallas kernels for 15%

profile of v4, /device:TPU:1, one launch (start us, length us, event | category | flops | bytes accessed | tf_op | source)
XLA Modules:
  0.0 149.7 jit_solution(12159566466850102910)
XLA Ops:
  1.3 2.8 %pack.1 = (bf16[64,16,192]{2,1,0:T(8,128)(2,1)}, bf16[64,16,192]{2,1,0:T(8,128)(2,1)}, f32[16,4,128]{2,1,0:T(4,128)}, bf16[2,16,16,192]{3,2,1,0:T(8,128)(2,1)}, f32[1,384]{1,0:T(1,128)}) custom-call(s32[1]{0:T(128)} %bitcast.16.counts, s32[2,8]{1,0:T(2,128)} %bitcast.31, bf16[16,64,192]{2,1,0:T(8,128)(2,1)} %bitcast.27, bf16[16,64,192]{2,1,0:T(8,128)(2,1)} %bitcast.28, ...), custom_call_target="tpu_custom_call" | custom-call | flops 1000000000 | bytes 2000896 | tf_op jit(solution)/shard_map/pack/pallas_call | solution.py:420
  4.1 1.0 slice_bitcast_fusion
  5.1 4.6 %collective-permute-start = (bf16[16,16,192]{2,1,0:T(8,128)(2,1)S(1)}, bf16[16,16,192]{2,1,0:T(8,128)(2,1)S(1)}, u32[]{:S(2)}, u32[]{:S(2)}) collective-permute-start(bf16[16,16,192]{2,1,0:T(8,128)(2,1)S(1)} %get-tuple-element.39), channel_id=1, source_target_pairs={{0,32},{32,64},{64,96},{96,128},{128,160},{160,192},{192,224},{224... | collective-permute-start | bytes 294920 | tf_op jit(solution)/shard_map/ppermute | solution.py:457
  9.7 5.5 %collective-permute-start.1 = (bf16[16,16,192]{2,1,0:T(8,128)(2,1)S(1)}, bf16[16,16,192]{2,1,0:T(8,128)(2,1)S(1)}, u32[]{:S(2)}, u32[]{:S(2)}) collective-permute-start(bf16[16,16,192]{2,1,0:T(8,128)(2,1)S(1)} %get-tuple-element.38), channel_id=1, source_target_pairs={{32,0},{64,32},{96,64},{128,96},{160,128},{192,160},{224,192},{256... | collective-permute-start | bytes 294920 | tf_op jit(solution)/shard_map/ppermute | solution.py:458
  15.2 9.2 %all_to_all.25.stats = f32[16,4,128]{2,1,0:T(4,128)} all-to-all(f32[16,4,128]{2,1,0:T(4,128)} %get-tuple-element.24), channel_id=1, replica_groups=mesh['gx'=16,'gy'=32] {'gx'}, dimensions={0} | all-to-all | bytes 65536 | tf_op jit(solution)/shard_map/all_to_all | solution.py:434
  24.4 0.0 collective-permute-done.lower
  24.4 0.0 copy-start.3
  24.4 0.0 collective-permute-done.1.upper
  24.4 0.0 copy-start.4
  24.4 0.6 copy-done.3
  25.0 0.0 copy-done.4
  25.1 2.5 %cross.1 = (bf16[16,16,384]{2,1,0:T(8,128)(2,1)}, bf16[16,16,384]{2,1,0:T(8,128)(2,1)}, f32[32,4,128]{2,1,0:T(4,128)}) custom-call(s32[2,12]{1,0:T(2,128)} %bitcast.22, bf16[64,16,192]{2,1,0:T(8,128)(2,1)} %get-tuple-element.21.held, bf16[64,16,192]{2,1,0:T(8,128)(2,1)} %get-tuple-element.22.up, bf16[16,16,192]{2,1,0:T(8,128)(2,1)} %copy-done.3, ...), custom_call_target="tpu_custom_call" | custom-call | flops 100000000 | bytes 1474560 | tf_op jit(solution)/shard_map/cross/pallas_call | solution.py:420
  27.5 3.2 %collective-permute-start.2 = (bf16[16,16,384]{2,1,0:T(8,128)(2,1)}, bf16[16,16,384]{2,1,0:T(8,128)(2,1)S(1)}, u32[]{:S(2)}, u32[]{:S(2)}) collective-permute-start(bf16[16,16,384]{2,1,0:T(8,128)(2,1)} %get-tuple-element.25), channel_id=1, source_target_pairs={{0,1},{1,2},{2,3},{3,4},{4,5},{5,6},{6,7},{7,8},{8,9},{9,10},{10,1... | collective-permute-start | bytes 589832 | tf_op jit(solution)/shard_map/ppermute | solution.py:469
  30.8 1.3 collective-permute-start.3
  32.1 17.5 %all-to-all-start.1 = ((f32[32,4,128]{2,1,0:T(4,128)}), f32[32,4,128]{2,1,0:T(4,128)S(1)}, u32[]{:S(2)}, u32[]{:S(2)}) async-start(f32[32,4,128]{2,1,0:T(4,128)} %get-tuple-element.27), calls=%async_computation.1 | async-start | bytes 131072 | tf_op jit(solution)/shard_map/all_to_all | solution.py:434
  49.5 11.2 %all-to-all-done.1.stats = f32[32,4,128]{2,1,0:T(4,128)S(1)} async-done(((f32[32,4,128]{2,1,0:T(4,128)}), f32[32,4,128]{2,1,0:T(4,128)S(1)}, u32[]{:S(2)}, u32[]{:S(2)}) %all-to-all-start.1) | async-done | bytes 65568 | tf_op jit(solution)/shard_map/all_to_all | solution.py:434
  60.7 0.0 copy-start.5
  60.7 0.0 collective-permute-done.2.side_l
  60.7 0.0 copy-start.7
  60.7 0.0 collective-permute-done.3.side_u
  60.7 0.0 copy-start.8
  60.7 0.6 copy-done.5
  61.3 0.1 copy-done.7
  61.4 0.1 copy-done.8
  61.5 9.9 %weight.1 = (bf16[8,11,16,384]{3,2,1,0:T(8,128)(2,1)}, bf16[8,11,16,384]{3,2,1,0:T(8,128)(2,1)}, bf16[6,6,6,16,192]{4,3,2,1,0:T(8,128)(2,1)}) custom-call(s32[1]{0:T(128)} %bitcast.17.counts, s32[1]{0:T(128)} %bitcast.6.core, bf16[64,16,192]{2,1,0:T(8,128)(2,1)} %get-tuple-element.21.held, bf16[64,16,192]{2,1,0:T(8,128)(2,1)} %get-tuple-element.22.up, ...), custom_call_target="tpu_custom_call" | custom-call | flops 4000000000 | bytes 4934848 | tf_op jit(solution)/shard_map/weight/pallas_call | solution.py:420
  71.3 4.2 %collective-permute-start.4 = (bf16[8,11,16,384]{3,2,1,0:T(8,128)(2,1)}, bf16[8,11,16,384]{3,2,1,0:T(8,128)(2,1)S(1)}, u32[]{:S(2)}, u32[]{:S(2)}) collective-permute-start(bf16[8,11,16,384]{3,2,1,0:T(8,128)(2,1)} %get-tuple-element.31), channel_id=1, source_target_pairs={{0,32},{32,0},{64,96},{96,64},{128,160},{160,128},{192,224},{224,1... | collective-permute-start | bytes 3244040 | tf_op jit(solution)/shard_map/ppermute | solution.py:485
  75.5 10.2 %back.1 = (f32[1024,192]{1,0:T(8,128)}, f32[1,384]{1,0:T(1,128)}) custom-call(s32[1]{0:T(128)} %bitcast.19.counts, bf16[64,16,192]{2,1,0:T(8,128)(2,1)} %get-tuple-element.21.held, bf16[64,16,192]{2,1,0:T(8,128)(2,1)} %get-tuple-element.22.up, bf16[16,16,192]{2,1,0:T(8,128)(2,1)} %copy-done.3, bf16[16,16,192]{2,1,0:T(8,128)(2,1)} %copy-done.4, ...), custom_call_target="tpu_custom_call" | custom-call | flops 3000000000 | bytes 4223680 | tf_op jit(solution)/shard_map/back/pallas_call | solution.py:420
  85.8 0.0 collective-permute-done.4.other
  85.8 0.0 copy-start.1
  85.8 1.0 copy-done.1
  86.8 2.9 %combine.1 = bf16[8,11,16,384]{3,2,1,0:T(8,128)(2,1)} custom-call(bf16[8,11,16,384]{3,2,1,0:T(8,128)(2,1)} %get-tuple-element.30.near, bf16[8,11,16,384]{3,2,1,0:T(8,128)(2,1)} %copy-done.1, f32[1,384]{1,0:T(1,128)} %get-tuple-element.32.sums), custom_call_target="tpu_custom_call" | custom-call | bytes 3245568 | tf_op jit(solution)/shard_map/combine/pallas_call | solution.py:420
  89.7 3.6 %all-to-all-start.2 = ((bf16[8,11,16,384]{3,2,1,0:T(8,128)(2,1)}), bf16[8,11,16,384]{3,2,1,0:T(8,128)(2,1)S(1)}, u32[]{:S(2)}, u32[]{:S(2)}) async-start(bf16[8,11,16,384]{3,2,1,0:T(8,128)(2,1)} %combine.1), calls=%async_computation.2 | async-start | bytes 2162688 | tf_op jit(solution)/shard_map/all_to_all | solution.py:434
  93.2 9.8 %forward.1.output = bf16[16,64,192]{2,1,0:T(8,128)(2,1)} custom-call(s32[1]{0:T(128)} %bitcast.18.counts, bf16[64,16,192]{2,1,0:T(8,128)(2,1)} %get-tuple-element.21.held, bf16[27,192,192]{2,1,0:T(8,128)(2,1)} %bitcast.26, bf16[6,6,6,16,192]{4,3,2,1,0:T(8,128)(2,1)} %get-tuple-element.29.padded_at), custom_call_target="tpu_custom_call" | custom-call | flops 3000000000 | bytes 4104192 | tf_op jit(solution)/shard_map/forward/pallas_call | solution.py:420
  103.1 0.0 copy-start.6
  103.1 6.4 %all-to-all-done.2.parts = bf16[8,11,16,384]{3,2,1,0:T(8,128)(2,1)S(1)} async-done(((bf16[8,11,16,384]{3,2,1,0:T(8,128)(2,1)}), bf16[8,11,16,384]{3,2,1,0:T(8,128)(2,1)S(1)}, u32[]{:S(2)}, u32[]{:S(2)}) %all-to-all-start.2) | async-done | bytes 1081376 | tf_op jit(solution)/shard_map/all_to_all | solution.py:434
  109.4 0.0 copy-start
  109.4 1.0 copy-done
  110.4 2.1 %share.1 = bf16[32,24,128]{2,1,0:T(8,128)(2,1)} custom-call(bf16[8,11,16,384]{3,2,1,0:T(8,128)(2,1)} %copy-done, bf16[16,64,192]{2,1,0:T(8,128)(2,1)} %forward.1.output), custom_call_target="tpu_custom_call" | custom-call | bytes 1671168 | tf_op jit(solution)/shard_map/share/pallas_call | solution.py:420
  112.5 16.1 %all_to_all.26.parts = bf16[32,24,128]{2,1,0:T(8,128)(2,1)} all-to-all(bf16[32,24,128]{2,1,0:T(8,128)(2,1)} %share.1), channel_id=1, replica_groups=mesh['gx'=16,'gy'=32] {'gy'}, dimensions={0} | all-to-all | bytes 393216 | tf_op jit(solution)/shard_map/all_to_all | solution.py:434
  128.6 1.6 %own.1 = (bf16[32,16,128]{2,1,0:T(8,128)(2,1)}, f32[1,384]{1,0:T(1,128)}) custom-call(bf16[32,24,128]{2,1,0:T(8,128)(2,1)} %all_to_all.26.parts), custom_call_target="tpu_custom_call" | custom-call | bytes 329216 | tf_op jit(solution)/shard_map/own/pallas_call | solution.py:420
  130.3 5.5 %all-to-all-start.4 = ((bf16[32,16,128]{2,1,0:T(8,128)(2,1)}), bf16[32,16,128]{2,1,0:T(8,128)(2,1)S(1)}, u32[]{:S(2)}, u32[]{:S(2)}) async-start(bf16[32,16,128]{2,1,0:T(8,128)(2,1)} %get-tuple-element.36), calls=%async_computation.4 | async-start | bytes 262144 | tf_op jit(solution)/shard_map/all_to_all | solution.py:434
  135.8 3.0 %collective-permute-start.5 = (f32[1,384]{1,0:T(1,128)}, f32[1,384]{1,0:T(1,128)S(1)}, u32[]{:S(2)}, u32[]{:S(2)}) collective-permute-start(f32[1,384]{1,0:T(1,128)} %get-tuple-element.33.sums), channel_id=1, source_target_pairs={{0,32},{32,0},{64,96},{96,64},{128,160},{160,128},{192,224},{224,1... | collective-permute-start | bytes 4616 | tf_op jit(solution)/shard_map/ppermute | solution.py:517
  138.8 0.0 copy-done.6
  138.8 0.7 copy.13.action
  139.5 0.3 collective-permute-done.5.other
  139.8 0.0 copy-start.9
  139.8 0.6 copy-done.9
  140.3 2.9 %finish.1 = (f32[128,384]{1,0:T(8,128)}, bf16[16,64,192]{2,1,0:T(8,128)(2,1)}) custom-call(s32[1]{0:T(128)} %bitcast.20.counts, f32[1,384]{1,0:T(1,128)} %get-tuple-element.33.sums, f32[1,384]{1,0:T(1,128)} %copy-done.9, f32[32,4,128]{2,1,0:T(4,128)} %copy-done.5, f32[1,384]{1,0:T(1,128)} %get-tuple-element.28.film, f32[128,1]{1,0:T(8,128)} %copy.13.action, ...), custom_call_target="tpu_custom_call" | custom-call | flops 1000000000 | bytes 1840128 | tf_op jit(solution)/shard_map/finish/pallas_call | solution.py:420
  143.3 3.7 %all-to-all-done.4.tiles = bf16[32,16,128]{2,1,0:T(8,128)(2,1)S(1)} async-done(((bf16[32,16,128]{2,1,0:T(8,128)(2,1)}), bf16[32,16,128]{2,1,0:T(8,128)(2,1)S(1)}, u32[]{:S(2)}, u32[]{:S(2)}) %all-to-all-start.4) | async-done | bytes 131104 | tf_op jit(solution)/shard_map/all_to_all | solution.py:434
  147.0 0.0 copy-start.2
  147.0 0.7 copy-done.2
  147.7 2.0 %unpack.1 = f32[12,27,192]{2,1,0:T(8,128)} custom-call(bf16[32,16,128]{2,1,0:T(8,128)(2,1)} %copy-done.2), custom_call_target="tpu_custom_call" | custom-call | bytes 379904 | tf_op jit(solution)/shard_map/unpack/pallas_call | solution.py:420
Async XLA Ops:
  5.1 19.3 %collective-permute-start = (bf16[16,16,192]{2,1,0:T(8,128)(2,1)S(1)}, bf16[16,16,192]{2,1,0:T(8,128)(2,1)S(1)}, u32[]{:S(2)}, u32[]{:S(2)}) collective-permute-start(bf16[16,16,192]{2,1,0:T(8,128)(2,1)S(1)} %get-tuple-element.39), channel_id=1, source_target_pairs={{0,32},{32,64},{64,96},{96,128},{128,160},{160,192},{192,224},{224... | collective-permute-start | bytes 294920 | tf_op jit(solution)/shard_map/ppermute | solution.py:457
  9.7 14.7 %collective-permute-start.1 = (bf16[16,16,192]{2,1,0:T(8,128)(2,1)S(1)}, bf16[16,16,192]{2,1,0:T(8,128)(2,1)S(1)}, u32[]{:S(2)}, u32[]{:S(2)}) collective-permute-start(bf16[16,16,192]{2,1,0:T(8,128)(2,1)S(1)} %get-tuple-element.38), channel_id=1, source_target_pairs={{32,0},{64,32},{96,64},{128,96},{160,128},{192,160},{224,192},{256... | collective-permute-start | bytes 294920 | tf_op jit(solution)/shard_map/ppermute | solution.py:458
  24.4 0.7 copy-start.3
  24.4 0.7 copy-start.4
  27.5 33.2 %collective-permute-start.2 = (bf16[16,16,384]{2,1,0:T(8,128)(2,1)}, bf16[16,16,384]{2,1,0:T(8,128)(2,1)S(1)}, u32[]{:S(2)}, u32[]{:S(2)}) collective-permute-start(bf16[16,16,384]{2,1,0:T(8,128)(2,1)} %get-tuple-element.25), channel_id=1, source_target_pairs={{0,1},{1,2},{2,3},{3,4},{4,5},{5,6},{6,7},{7,8},{8,9},{9,10},{10,1... | collective-permute-start | bytes 589832 | tf_op jit(solution)/shard_map/ppermute | solution.py:469
  30.8 30.0 %collective-permute-start.3 = (bf16[16,16,384]{2,1,0:T(8,128)(2,1)}, bf16[16,16,384]{2,1,0:T(8,128)(2,1)S(1)}, u32[]{:S(2)}, u32[]{:S(2)}) collective-permute-start(bf16[16,16,384]{2,1,0:T(8,128)(2,1)} %get-tuple-element.26), channel_id=1, source_target_pairs={{1,0},{2,1},{3,2},{4,3},{5,4},{6,5},{7,6},{8,7},{9,8},{10,9},{11,1... | collective-permute-start | bytes 589832 | tf_op jit(solution)/shard_map/ppermute | solution.py:470
  32.1 28.7 %all-to-all-start.1 = ((f32[32,4,128]{2,1,0:T(4,128)}), f32[32,4,128]{2,1,0:T(4,128)S(1)}, u32[]{:S(2)}, u32[]{:S(2)}) async-start(f32[32,4,128]{2,1,0:T(4,128)} %get-tuple-element.27), calls=%async_computation.1 | async-start | bytes 131072 | tf_op jit(solution)/shard_map/all_to_all | solution.py:434
  60.7 0.6 copy-start.5
  60.7 0.7 copy-start.7
  60.7 0.7 copy-start.8
  71.3 14.4 %collective-permute-start.4 = (bf16[8,11,16,384]{3,2,1,0:T(8,128)(2,1)}, bf16[8,11,16,384]{3,2,1,0:T(8,128)(2,1)S(1)}, u32[]{:S(2)}, u32[]{:S(2)}) collective-permute-start(bf16[8,11,16,384]{3,2,1,0:T(8,128)(2,1)} %get-tuple-element.31), channel_id=1, source_target_pairs={{0,32},{32,0},{64,96},{96,64},{128,160},{160,128},{192,224},{224,1... | collective-permute-start | bytes 3244040 | tf_op jit(solution)/shard_map/ppermute | solution.py:485
  85.8 1.0 copy-start.1
  89.7 19.8 %all-to-all-start.2 = ((bf16[8,11,16,384]{3,2,1,0:T(8,128)(2,1)}), bf16[8,11,16,384]{3,2,1,0:T(8,128)(2,1)S(1)}, u32[]{:S(2)}, u32[]{:S(2)}) async-start(bf16[8,11,16,384]{3,2,1,0:T(8,128)(2,1)} %combine.1), calls=%async_computation.2 | async-start | bytes 2162688 | tf_op jit(solution)/shard_map/all_to_all | solution.py:434
  103.1 35.7 %copy-start.6 = (f32[128]{0:T(128)S(1)}, f32[128]{0:T(128)}, u32[]{:S(2)}) copy-start(f32[128]{0:T(128)} %param.15) | copy-start | bytes 1540
  109.4 1.0 copy-start
  130.3 16.8 %all-to-all-start.4 = ((bf16[32,16,128]{2,1,0:T(8,128)(2,1)}), bf16[32,16,128]{2,1,0:T(8,128)(2,1)S(1)}, u32[]{:S(2)}, u32[]{:S(2)}) async-start(bf16[32,16,128]{2,1,0:T(8,128)(2,1)} %get-tuple-element.36), calls=%async_computation.4 | async-start | bytes 262144 | tf_op jit(solution)/shard_map/all_to_all | solution.py:434
  135.8 4.0 %collective-permute-start.5 = (f32[1,384]{1,0:T(1,128)}, f32[1,384]{1,0:T(1,128)S(1)}, u32[]{:S(2)}, u32[]{:S(2)}) collective-permute-start(f32[1,384]{1,0:T(1,128)} %get-tuple-element.33.sums), channel_id=1, source_target_pairs={{0,32},{32,0},{64,96},{96,64},{128,160},{160,128},{192,224},{224,1... | collective-permute-start | bytes 4616 | tf_op jit(solution)/shard_map/ppermute | solution.py:517
  139.8 0.6 copy-start.9
  147.0 0.7 copy-start.2

commit v5 on v4

--- a/solution.py
+++ b/solution.py
@@ -9,7 +9,7 @@
 VOXELS = 64
 CHANNELS = 192
 TILES = 11
-VMEM_LIMIT = 56 * 1024 * 1024
+MIB = 1024 * 1024
 F32 = jnp.float32
 BF16 = jnp.bfloat16
 
@@ -82,7 +82,7 @@
 
 
 def pack_kernel(
-    counts, send_x, feat, cot, action, film_weight, held, up, stats, faces, film
+    counts, send_x, feat, cot, action, film_weight, held, up, stats, face_low, face_high, film
 ):
     swap = swap_matrix(counts[0])
     total = jnp.zeros((1, CHANNELS), F32)
@@ -103,7 +103,8 @@
         chosen = pick(list_column(send_x, side, 8, 16, 8), 32, 0, SLOTS, 0, 16, 8)
         for i in range(16):
             both = jnp.concatenate([held[48 * side + i], up[48 * side + i]], axis=0)
-            faces[side, i, :, :] = dot(chosen, both).astype(BF16)
+            target = (face_low, face_high)[side]
+            target[i, :, :] = dot(chosen, both).astype(BF16)
     film[...] = lax.dot_general(
         action[...],
         film_weight[...],
@@ -195,43 +196,63 @@
     return part.reshape(1024, CHANNELS)
 
 
+def early_kernel(
+    held, up, lower, upper, side_l, side_u, rule, weight_at,
+    raw, back, turned, wide, low_y, high_y, weight, done,
+):
+    copy = pltpu.make_async_copy(weight_at, weight, done.at[0])
+    copy.start()
+    for which, own, target in ((0, held, raw), (1, up, wide)):
+        low_y[...] = one_field(side_l[...], which)
+        high_y[...] = one_field(side_u[...], which)
+        gather_blocks(rule, 8 * which, own, lower, upper, low_y, high_y, target)
+    same = jnp.where(iota((CHANNELS, CHANNELS), 0) == iota((CHANNELS, CHANNELS), 1), 1.0, 0.0)
+    turned[...] = dot_nt(same.astype(BF16), up[...].reshape(1024, CHANNELS)).astype(BF16)
+    back[...] = jnp.zeros_like(back)
+    copy.wait()
+
+    def step(t, carry):
+        k = 3 * t
+        total = dot(window(wide, k), weight[26 - k])
+        total += dot(window(wide, k + 1), weight[25 - k])
+        back[...] += total + dot(window(wide, k + 2), weight[24 - k])
+        return carry
+
+    lax.fori_loop(0, 9, step, 0)
+
+
 def weight_kernel(
-    counts, core, held, up, lower, upper, side_l, side_u, rule, stats, film,
-    near, far, padded, hid, low, high, low_y, high_y, turned,
+    counts, core, raw, up_turned, rule, stats, film,
+    near, far, padded, turned,
 ):
     cells, mean, inverse, scale, shift = norm_terms(stats, film)
-
-    def act(x):
-        x = (x.astype(F32) - mean) * inverse * scale + shift
-        return jnp.maximum(x, 0.0).astype(BF16)
-
-    live = (iota((256, 1), 0) & 15) < counts[0]
-
-    def local_part(i, carry):
-        at = pl.ds(i * 16, 16)
-        x = act(held[at, :, :].reshape(256, CHANNELS))
-        x = jnp.where(live, x.astype(F32), 0.0).astype(BF16)
-        hid[at, :, :] = x.reshape(16, 16, CHANNELS)
-        return carry
-
-    lax.fori_loop(0, 4, local_part, 0)
-    for source, target in (
-        (lower[...], low),
-        (upper[...], high),
-        (one_field(side_l[...], 0), low_y),
-        (one_field(side_u[...], 0), high_y),
-    ):
-        target[...] = act(source.reshape(256, CHANNELS)).reshape(16, 16, CHANNELS)
-    gather_blocks(rule, 0, hid, low, high, low_y, high_y, padded)
+    live = iota((16, 1), 0) < counts[0]
+    entries = rule[...]
+
+    def act(at, mask):
+        x = raw[at]
+        lead = x.shape[:-2]
+        x = (x.astype(F32).reshape(-1, CHANNELS) - mean) * inverse * scale + shift
+        x = jnp.maximum(x, 0.0).reshape(-1, 16, CHANNELS)
+        x = jnp.where(mask[None], x, 0.0).astype(BF16)
+        padded[at] = x.reshape(*lead, 16, CHANNELS)
+
+    ranges = (slice(0, 1), slice(1, 5), slice(5, 6))
+    for n in range(27):
+        x, y, z = n // 9, n // 3 % 3, n % 3
+        if n == 13:
+            for a in range(1, 5):
+                act((slice(a, a + 1), ranges[1], ranges[1]), live)
+        else:
+            act((ranges[x], ranges[y], ranges[z]), entries[:, n : n + 1] != 16)
 
     row, col = iota((256, CHANNELS), 0), iota((256, CHANNELS), 1)
     group = ((row >> 4) & 7) * 2 + jnp.where(row >= 128, 1 - core[0], core[0])
-    wide = up[...].reshape(1024, CHANNELS)
     for m in range(4):
         place = (row + 4 * m) & 15
         spread = (place < 12) & (col == group * 12 + place)
         spread = jnp.where(spread, 1.0, 0.0).astype(BF16)
-        turned[m, :, :] = dot_nt(spread, wide).astype(BF16)
+        turned[m, :, :] = dot(spread, up_turned[...]).astype(BF16)
 
     line = iota((256, 384), 0) & 15
 
@@ -262,27 +283,14 @@
     store(10, jnp.where(line < 8, second, 0.0))
 
 
-def back_kernel(
-    counts, held, up, lower, upper, side_l, side_u, rule, stats, film,
-    weight_at, kept, sums, wide, acc, low_y, high_y, weight, done,
-):
-    copy = pltpu.make_async_copy(weight_at, weight, done.at[0])
-    copy.start()
+def split(value):
+    first = value.astype(BF16).astype(F32)
+    second = (value - first).astype(BF16).astype(F32)
+    return first, second, value - first - second
+
+
+def slope_kernel(counts, held, up, back, stats, film, kept, lines):
     cells, mean, inverse, scale, shift = norm_terms(stats, film)
-    low_y[...] = one_field(side_l[...], 1)
-    high_y[...] = one_field(side_u[...], 1)
-    gather_blocks(rule, 8, up, lower, upper, low_y, high_y, wide)
-    acc[...] = jnp.zeros_like(acc)
-    copy.wait()
-
-    def step(t, carry):
-        k = 3 * t
-        total = dot(window(wide, k), weight[26 - k])
-        total += dot(window(wide, k + 1), weight[25 - k])
-        acc[...] += total + dot(window(wide, k + 2), weight[24 - k])
-        return carry
-
-    lax.fori_loop(0, 9, step, 0)
     shift_grad = jnp.zeros((1, CHANNELS), F32)
     scale_grad = jnp.zeros((1, CHANNELS), F32)
     live = (iota((256, 1), 0) & 15) < counts[0]
@@ -291,34 +299,19 @@
         part = slice(16 * g, 16 * g + 16)
         x = held[part, :, :].reshape(256, CHANNELS).astype(F32)
         normed = (x - mean) * inverse
-        slope = jnp.where(live & (normed * scale + shift > 0), acc[at, :], 0.0)
+        slope = jnp.where(live & (normed * scale + shift > 0), back[at, :], 0.0)
         shift_grad += jnp.sum(slope, axis=0, keepdims=True)
         scale_grad += jnp.sum(slope * normed, axis=0, keepdims=True)
         kept[at, :] = up[part, :, :].reshape(256, CHANNELS).astype(F32) + inverse * (slope * scale)
-    sums[...] = jnp.concatenate([scale_grad, shift_grad], axis=1)
-
-
-def split(value):
-    first = value.astype(BF16).astype(F32)
-    second = (value - first).astype(BF16).astype(F32)
-    return first, second, value - first - second
-
-
-def combine_kernel(near, other, sums, parts):
-    for i in range(8):
-        parts[i, :, :, :] = (near[i].astype(F32) + other[i].astype(F32)).astype(BF16)
     row = iota((16, 384), 0)
-    lines = jnp.zeros((16, 384), F32)
-    for e, piece in enumerate(split(sums[...])):
-        lines = jnp.where(row == 8 + e, piece, lines)
-    for i in range(8):
-        held = parts[i, TILES - 1, :, :].astype(F32)
-        parts[i, TILES - 1, :, :] = jnp.where(row < 8, held, lines).astype(BF16)
-
-
-def forward_kernel(
-    counts, held, weight_at, padded_at, output, acc, weight, padded, done
-):
+    block = jnp.zeros((16, 384), F32)
+    for e, piece in enumerate(split(jnp.concatenate([scale_grad, shift_grad], axis=1))):
+        block = jnp.where(row == 8 + e, piece, block)
+    lines[...] = block
+
+
+def forward_kernel(counts, held, weight_at, padded_at, output, token, acc, weight, padded, done):
+    token[...] = jnp.zeros_like(token)
     copies = [
         pltpu.make_async_copy(weight_at, weight, done.at[0]),
         pltpu.make_async_copy(padded_at, padded, done.at[1]),
@@ -350,7 +343,7 @@
     return (share // 3, share % 3) if share < 30 else (10, 2 * (share - 30))
 
 
-def share_kernel(parts, output, shares):
+def share_kernel(parts, token, shares):
     for tile in reversed(range(TILES)):
         total = jnp.sum(parts[:, tile, :, :].astype(F32), axis=0)
         if tile == TILES - 1:
@@ -413,8 +406,7 @@
 ANY = pl.BlockSpec(memory_space=pl.ANY)
 
 
-def call(kernel, scalars, arrays, outs, scratch=(), flops=0, name=None, left=0, sems=None):
-    sems = left if sems is None else sems
+def call(kernel, scalars, arrays, outs, scratch=(), flops=0, name=None, left=0, room=12):
     shapes = [jax.ShapeDtypeStruct(shape, dtype) for shape, dtype in outs]
     moved = sum(x.size * x.dtype.itemsize for x in [*arrays, *shapes])
     return pl.pallas_call(
@@ -423,8 +415,8 @@
         in_specs=[SMEM] * len(scalars) + [VMEM] * (len(arrays) - left) + [ANY] * left,
         out_specs=[VMEM] * len(outs),
         scratch_shapes=[pltpu.VMEM(*s) for s in scratch]
-        + ([pltpu.SemaphoreType.DMA((sems,))] if sems else []),
-        compiler_params=pltpu.CompilerParams(vmem_limit_bytes=VMEM_LIMIT),
+        + ([pltpu.SemaphoreType.DMA((left,))] if left else []),
+        compiler_params=pltpu.CompilerParams(vmem_limit_bytes=room * MIB),
         cost_estimate=pl.CostEstimate(flops=flops, bytes_accessed=moved, transcendentals=0),
         name=name,
     )(*scalars, *arrays)
@@ -442,11 +434,11 @@
     face = ((16, 16, CHANNELS), BF16)
     spaced = ((6, 6, 6, 16, CHANNELS), BF16)
     joined = ((16, 16, 384), BF16)
-    held, up, stats, faces, film = call(
+    held, up, stats, face_low, face_high, film = call(
         pack_kernel,
         [count, send_x[0, 0]],
         [features[0, 0], cotangent[0, 0], action[None], film_weight],
-        [block, block, ((size_x, 4, 128), F32), ((2, *face[0]), BF16), ((1, 2 * CHANNELS), F32)],
+        [block, block, ((size_x, 4, 128), F32), face, face, ((1, 2 * CHANNELS), F32)],
         flops=10**9,
         name="pack",
     )
@@ -454,8 +446,8 @@
     down_x = [(i + 1, i) for i in range(size_x - 1)]
     up_y = [(i, i + 1) for i in range(size_y - 1)]
     down_y = [(i + 1, i) for i in range(size_y - 1)]
-    lower = lax.ppermute(faces[1], "gx", up_x)
-    upper = lax.ppermute(faces[0], "gx", down_x)
+    lower = lax.ppermute(face_high, "gx", up_x)
+    upper = lax.ppermute(face_low, "gx", down_x)
     stats = exchange(stats, "gx")
     weight = jnp.transpose(conv_weight, (1, 0, 2))
     face_low, face_high, stats = call(
@@ -471,45 +463,56 @@
     stats = exchange(stats, "gy")
     core = lax.axis_index("gx") & 1
     swapped = [(i, i ^ 1) for i in range(size_x)]
-    fields = [held, up, lower, upper, side_l, side_u, rule, stats, film]
+    taps = ((27, CHANNELS, CHANNELS), BF16)
+    total = ((1024, CHANNELS), F32)
+    raw, back, turned = call(
+        early_kernel,
+        [],
+        [held, up, lower, upper, side_l, side_u, rule, weight],
+        [spaced, total, ((CHANNELS, 1024), BF16)],
+        [spaced, face, face, taps],
+        flops=3 * 10**9,
+        name="early",
+        left=1,
+        room=20,
+    )
     half = ((8, TILES, 16, 384), BF16)
     near, far, padded = call(
         weight_kernel,
         [count, core.reshape(1)],
-        fields,
+        [raw, turned, rule, stats, film],
         [half, half, spaced],
-        [block, face, face, face, face, ((4, 256, 1024), BF16)],
+        [((4, 256, 1024), BF16)],
         flops=4 * 10**9,
         name="weight",
+        room=20,
     )
     other = lax.ppermute(far, "gx", swapped)
-    taps = ((27, CHANNELS, CHANNELS), BF16)
-    total = ((1024, CHANNELS), F32)
-    kept, sums = call(
-        back_kernel,
+    kept, lines = call(
+        slope_kernel,
         [count],
-        [*fields, weight],
-        [total, ((1, 2 * CHANNELS), F32)],
-        [spaced, total, face, face, taps],
-        flops=3 * 10**9,
-        name="back",
-        left=1,
-    )
-    (parts,) = call(combine_kernel, [], [near, other, sums], [half], name="combine")
+        [held, up, back, stats, film],
+        [total, ((16, 384), F32)],
+        flops=10**8,
+        name="slope",
+    )
+    tile = lax.broadcasted_iota(jnp.int32, half[0], 1)
+    row = lax.broadcasted_iota(jnp.int32, half[0], 2)
+    parts = near.astype(F32) + other.astype(F32)
+    parts = jnp.where((tile == TILES - 1) & (row >= 8), lines, parts).astype(BF16)
     parts = exchange(parts, "gx", [list(range(c, size_x, 2)) for c in range(2)])
-    (output,) = call(
+    output, token = call(
         forward_kernel,
         [count],
         [held, weight, padded],
-        [((SLOTS, VOXELS, CHANNELS), BF16)],
+        [((SLOTS, VOXELS, CHANNELS), BF16), ((8, 128), F32)],
         [total, taps, spaced],
         flops=3 * 10**9,
         name="forward",
         left=2,
-    )
-    (shares,) = call(
-        share_kernel, [], [parts, output], [((size_y, 24, 128), BF16)], name="share", left=1, sems=0
-    )
+        room=16,
+    )
+    (shares,) = call(share_kernel, [], [parts, token], [((size_y, 24, 128), BF16)], name="share")
     shares = exchange(shares, "gy")
     mine, sums = call(
         own_kernel, [], [shares], [((size_y, 16, 128), BF16), ((1, 2 * CHANNELS), F32)], name="own"

time: 151 us -> 137 us (0.907)
  Pallas kernels: 46.7 us -> 27.5 us
  waiting for transfers between devices: 21.6 us -> 11.6 us
  local copies, waits for them, and re-layouts: 6.39 us -> 14.4 us
  blocking collectives: 25.3 us -> 28.7 us
    pallas_call x10, Pallas kernels: 46.7 us -> 27.5 us  [call(): pl.pallas_call(kernel, out_shape=shapes, in_specs=[SMEM] * len(scalars) +...]
    all_to_all x3, waiting for transfers between devices: 21.3 us -> 10.6 us  [exchange(): lax.all_to_all(array, axis, 0, 0, axis_index_groups=groups, tiled=True)]
    unnamed x20 -> x32, local copies, waits for them, and re-layouts: 4.67 us -> 14.3 us
    all_to_all x2, blocking collectives: 25.3 us -> 28.7 us  [exchange(): lax.all_to_all(array, axis, 0, 0, axis_index_groups=groups, tiled=True)]
  transfers between devices with their start and end apart: 9 -> 9, of which waited for: 4 -> 5; matrix products, arithmetic and copies ran while one was open for 0% -> 0% of each run, Pallas kernels for 15% -> 12%
where the time goes in v5:
time: 137 us; the launch traced here: 135 us
  starting transfers between devices  49.6 us (36%)
  blocking collectives  28.7 us (21%)
  Pallas kernels  27.5 us (20%)
  local copies, waits for them, and re-layouts  14.4 us (11%)
  waiting for transfers between devices  11.6 us (8%)
  between operations  1.51 us (1%)
    all_to_all x2, blocking collectives, exchange(): lax.all_to_all(array, axis, 0, 0, axis_index_groups=groups, tiled=True)  28.7 us
    pallas_call x10, Pallas kernels, call(): pl.pallas_call(kernel, out_shape=shapes, in_specs=[SMEM] * len(scalars) +...  27.5 us
    all_to_all x3, starting transfers between devices, exchange(): lax.all_to_all(array, axis, 0, 0, axis_index_groups=groups, tiled=True)  25.8 us
    unnamed x32, local copies, waits for them, and re-layouts  14.3 us
    all_to_all x3, waiting for transfers between devices, exchange(): lax.all_to_all(array, axis, 0, 0, axis_index_groups=groups, tiled=True)  10.6 us
    ppermute x1, starting transfers between devices, body(): upper = lax.ppermute(face_low, 'gx', down_x)  5.49 us
    ppermute x1, starting transfers between devices, body(): lower = lax.ppermute(face_high, 'gx', up_x)  4.72 us
    ppermute x1, starting transfers between devices, body(): side_l = lax.ppermute(face_high, 'gy', up_y)  4.21 us
  transfers between devices with their start and end apart: 9, of which 5 were waited for; matrix products, arithmetic and copies ran while one was open for 0% of the time, Pallas kernels for 12%

profile of v5, /device:TPU:1, one launch (start us, length us, event | category | flops | bytes accessed | tf_op | source)
XLA Modules:
  0.0 134.7 jit_solution(15817401697787573288)
XLA Ops:
  1.3 0.0 copy-start.1
  1.3 0.6 copy-done.1
  1.9 0.0 copy-start.7
  1.9 1.0 copy-done.7
  3.0 0.0 copy-start.8
  3.0 1.0 copy-done.8
  4.0 0.0 copy-start.9
  4.0 0.9 copy-done.9
  4.9 0.0 copy-start.11
  5.0 0.7 copy-done.11
  5.6 0.0 copy-start
  5.6 1.2 pack.1
  6.9 0.0 copy-start.10
  6.9 4.7 %collective-permute-start = (bf16[16,16,192]{2,1,0:T(8,128)(2,1)S(1)}, bf16[16,16,192]{2,1,0:T(8,128)(2,1)S(1)}, u32[]{:S(2)}, u32[]{:S(2)}) collective-permute-start(bf16[16,16,192]{2,1,0:T(8,128)(2,1)S(1)} %get-tuple-element.29), channel_id=1, source_target_pairs={{0,32},{32,64},{64,96},{96,128},{128,160},{160,192},{192,224},{224... | collective-permute-start | bytes 294920 | tf_op jit(solution)/shard_map/ppermute | solution.py:449
  11.6 5.5 %collective-permute-start.1 = (bf16[16,16,192]{2,1,0:T(8,128)(2,1)S(1)}, bf16[16,16,192]{2,1,0:T(8,128)(2,1)S(1)}, u32[]{:S(2)}, u32[]{:S(2)}) collective-permute-start(bf16[16,16,192]{2,1,0:T(8,128)(2,1)S(1)} %get-tuple-element.30), channel_id=1, source_target_pairs={{32,0},{64,32},{96,64},{128,96},{160,128},{192,160},{224,192},{256... | collective-permute-start | bytes 294920 | tf_op jit(solution)/shard_map/ppermute | solution.py:450
  17.1 7.9 %all_to_all.25.stats = f32[16,4,128]{2,1,0:T(4,128)S(1)} all-to-all(f32[16,4,128]{2,1,0:T(4,128)S(1)} %get-tuple-element.31), channel_id=1, replica_groups=mesh['gx'=16,'gy'=32] {'gx'}, dimensions={0} | all-to-all | bytes 65536 | tf_op jit(solution)/shard_map/all_to_all | solution.py:426
  25.0 0.0 collective-permute-done.lower
  25.0 0.0 collective-permute-done.1.upper
  25.0 0.0 copy-done
  25.0 1.5 %cross.1 = (bf16[16,16,384]{2,1,0:T(8,128)(2,1)S(1)}, bf16[16,16,384]{2,1,0:T(8,128)(2,1)S(1)}, f32[32,4,128]{2,1,0:T(4,128)}) custom-call(s32[2,12]{1,0:T(2,128)S(1)} %bitcast.17, bf16[64,16,192]{2,1,0:T(8,128)(2,1)S(1)} %get-tuple-element.27.held, bf16[64,16,192]{2,1,0:T(8,128)(2,1)S(1)} %get-tuple-element.28.up, ...), custom_call_target="tpu_custom_call" | custom-call | flops 100000000 | bytes 1474560 | tf_op jit(solution)/shard_map/cross/pallas_call | solution.py:412
  26.6 4.2 %collective-permute-start.2 = (bf16[16,16,384]{2,1,0:T(8,128)(2,1)S(1)}, bf16[16,16,384]{2,1,0:T(8,128)(2,1)S(1)}, u32[]{:S(2)}, u32[]{:S(2)}) collective-permute-start(bf16[16,16,384]{2,1,0:T(8,128)(2,1)S(1)} %get-tuple-element.32), channel_id=1, source_target_pairs={{0,1},{1,2},{2,3},{3,4},{4,5},{5,6},{6,7},{7,8},{8,9},{9,10},{10,1... | collective-permute-start | bytes 589832 | tf_op jit(solution)/shard_map/ppermute | solution.py:461
  30.8 1.3 collective-permute-start.3
  32.1 17.5 %all-to-all-start.1 = ((f32[32,4,128]{2,1,0:T(4,128)}), f32[32,4,128]{2,1,0:T(4,128)S(1)}, u32[]{:S(2)}, u32[]{:S(2)}) async-start(f32[32,4,128]{2,1,0:T(4,128)} %get-tuple-element.36), calls=%async_computation.1 | async-start | bytes 131072 | tf_op jit(solution)/shard_map/all_to_all | solution.py:426
  49.6 0.0 collective-permute-done.2.side_l
  49.6 0.0 collective-permute-done.3.side_u
  49.6 0.0 copy-done.10
  49.6 0.0 copy-start.3
  49.6 1.7 %copy-done.3 = bf16[192,27,192]{2,0,1:T(8,128)(2,1)S(1)} copy-done((bf16[192,27,192]{2,0,1:T(8,128)(2,1)S(1)}, bf16[192,27,192]{2,0,1:T(8,128)(2,1)}, u32[]{:S(2)}) %copy-start.3) | copy-done | bytes 1990680
  51.3 6.8 %early.1 = (bf16[6,6,6,16,192]{4,3,2,1,0:T(8,128)(2,1)S(1)}, f32[1024,192]{1,0:T(8,128)S(1)}, bf16[192,1024]{1,0:T(8,128)(2,1)S(1)}) custom-call(bf16[64,16,192]{2,1,0:T(8,128)(2,1)S(1)} %get-tuple-element.27.held, bf16[64,16,192]{2,1,0:T(8,128)(2,1)S(1)} %get-tuple-element.28.up, bf16[16,16,192]{2,1,0:T(8,128)(2,1)S(1)} %collective-permute-done.lower, ...), custom_call_target="tpu_custom_call" | custom-call | flops 3000000000 | bytes 5875392 | tf_op jit(solution)/shard_map/early/pallas_call | solution.py:412
  58.2 0.0 copy-start.14
  58.2 1.2 copy-done.14
  59.4 1.3 all-to-all-done.1.stats
  60.7 0.0 copy-start.15
  60.8 1.5 %copy-done.15 = bf16[6,6,6,16,192]{4,3,2,1,0:T(8,128)(2,1)S(1)} copy-done((bf16[6,6,6,16,192]{4,3,2,1,0:T(8,128)(2,1)S(1)}, bf16[6,6,6,16,192]{4,3,2,1,0:T(8,128)(2,1)}, u32[]{:S(2)}) %copy-start.15) | copy-done | bytes 1327128
  62.2 6.4 %weight.1 = (bf16[8,11,16,384]{3,2,1,0:T(8,128)(2,1)S(1)}, bf16[8,11,16,384]{3,2,1,0:T(8,128)(2,1)S(1)}, bf16[6,6,6,16,192]{4,3,2,1,0:T(8,128)(2,1)S(1)}) custom-call(s32[1]{0:T(128)} %bitcast.13.counts, s32[1]{0:T(128)} %bitcast.6.core, bf16[6,6,6,16,192]{4,3,2,1,0:T(8,128)(2,1)S(1)} %copy-done.15, bf16[192,1024]{1,0:T(8,128)(2,1)S(1)} %get-tuple-element.35.up_turned, ...), custom_call_target="tpu_custom_call" | custom-call | flops 4000000000 | bytes 5278912 | tf_op jit(solution)/shard_map/weight/pallas_call | solution.py:412
  68.6 0.0 copy-start.12
  68.6 4.2 %collective-permute-start.4 = (bf16[8,11,16,384]{3,2,1,0:T(8,128)(2,1)S(1)}, bf16[8,11,16,384]{3,2,1,0:T(8,128)(2,1)S(1)}, u32[]{:S(2)}, u32[]{:S(2)}) collective-permute-start(bf16[8,11,16,384]{3,2,1,0:T(8,128)(2,1)S(1)} %get-tuple-element.43), channel_id=1, source_target_pairs={{0,32},{32,0},{64,96},{96,64},{128,160},{160,128},{192,224},{224,1... | collective-permute-start | bytes 3244040 | tf_op jit(solution)/shard_map/ppermute | solution.py:490
  72.8 0.9 slope.1
  73.7 0.0 copy-done.12
  73.8 0.0 copy-start.5
  73.8 1.0 copy-done.5
  74.8 0.4 collective-permute-done.4
  75.1 1.3 %select_convert_fusion = bf16[8,11,16,384]{3,2,1,0:T(8,128)(2,1)} fusion(bf16[8,11,16,384]{3,2,1,0:T(8,128)(2,1)S(1)} %collective-permute-done.4, bf16[8,11,16,384]{3,2,1,0:T(8,128)(2,1)S(1)} %get-tuple-element.42, f32[16,384]{1,0:T(8,128)S(1)} %get-tuple-element.41, pred[16]{0:T(512)(128)(4,1)S(1)} %iota_compare_fusion, pred[11]{0:T(512)(128)(4,1)S(1)} %iota_compare_fusion.1), kind=kLoop, calls=%fused_computation | loop fusion | flops 2703360 | bytes 3268635 | tf_op jit(solution)/shard_map/convert_element_type | solution.py:502
  76.5 3.6 %all-to-all-start.2 = ((bf16[8,11,16,384]{3,2,1,0:T(8,128)(2,1)}), bf16[8,11,16,384]{3,2,1,0:T(8,128)(2,1)S(1)}, u32[]{:S(2)}, u32[]{:S(2)}) async-start(bf16[8,11,16,384]{3,2,1,0:T(8,128)(2,1)} %select_convert_fusion), calls=%async_computation.2 | async-start | bytes 2162688 | tf_op jit(solution)/shard_map/all_to_all | solution.py:426
  80.0 0.0 copy-start.4
  80.1 1.7 %copy-done.4 = bf16[192,27,192]{2,0,1:T(8,128)(2,1)S(1)} copy-done((bf16[192,27,192]{2,0,1:T(8,128)(2,1)S(1)}, bf16[192,27,192]{2,0,1:T(8,128)(2,1)}, u32[]{:S(2)}) %copy-start.4) | copy-done | bytes 1990680
  81.8 0.0 copy-start.13
  81.8 1.5 %copy-done.13 = bf16[6,6,6,16,192]{4,3,2,1,0:T(8,128)(2,1)S(1)} copy-done((bf16[6,6,6,16,192]{4,3,2,1,0:T(8,128)(2,1)S(1)}, bf16[6,6,6,16,192]{4,3,2,1,0:T(8,128)(2,1)}, u32[]{:S(2)}) %copy-start.13) | copy-done | bytes 1327128
  83.3 7.2 %forward.1 = (bf16[16,64,192]{2,1,0:T(8,128)(2,1)}, f32[8,128]{1,0:T(8,128)S(1)}) custom-call(s32[1]{0:T(128)} %bitcast.14.counts, bf16[64,16,192]{2,1,0:T(8,128)(2,1)S(1)} %get-tuple-element.27.held, bf16[27,192,192]{2,1,0:T(8,128)(2,1)S(1)} %bitcast.21, bf16[6,6,6,16,192]{4,3,2,1,0:T(8,128)(2,1)S(1)} %copy-done.13), custom_call_target="tpu_custom_call" | custom-call | flops 3000000000 | bytes 4108288 | tf_op jit(solution)/shard_map/forward/pallas_call | solution.py:412
  90.4 0.0 copy-start.2
  90.5 5.4 %all-to-all-done.2.parts = bf16[8,11,16,384]{3,2,1,0:T(8,128)(2,1)S(1)} async-done(((bf16[8,11,16,384]{3,2,1,0:T(8,128)(2,1)}), bf16[8,11,16,384]{3,2,1,0:T(8,128)(2,1)S(1)}, u32[]{:S(2)}, u32[]{:S(2)}) %all-to-all-start.2) | async-done | bytes 1081376 | tf_op jit(solution)/shard_map/all_to_all | solution.py:426
  95.8 0.1 share.1
  96.0 20.8 %all_to_all.26.parts = bf16[32,24,128]{2,1,0:T(8,128)(2,1)S(1)} all-to-all(bf16[32,24,128]{2,1,0:T(8,128)(2,1)S(1)} %share.1), channel_id=1, replica_groups=mesh['gx'=16,'gy'=32] {'gy'}, dimensions={0} | all-to-all | bytes 393216 | tf_op jit(solution)/shard_map/all_to_all | solution.py:426
  116.8 0.7 own.1
  117.5 4.8 %all-to-all-start.4 = ((bf16[32,16,128]{2,1,0:T(8,128)(2,1)}), bf16[32,16,128]{2,1,0:T(8,128)(2,1)S(1)}, u32[]{:S(2)}, u32[]{:S(2)}) async-start(bf16[32,16,128]{2,1,0:T(8,128)(2,1)} %get-tuple-element.48), calls=%async_computation.4 | async-start | bytes 262144 | tf_op jit(solution)/shard_map/all_to_all | solution.py:426
  122.3 3.8 %collective-permute-start.5 = (f32[1,384]{1,0:T(1,128)S(1)}, f32[1,384]{1,0:T(1,128)S(1)}, u32[]{:S(2)}, u32[]{:S(2)}) collective-permute-start(f32[1,384]{1,0:T(1,128)S(1)} %get-tuple-element.45.sums), channel_id=1, source_target_pairs={{0,32},{32,0},{64,96},{96,64},{128,160},{160,128},{192,224},{224,1... | collective-permute-start | bytes 4616 | tf_op jit(solution)/shard_map/ppermute | solution.py:520
  126.1 0.0 copy-done.2
  126.2 0.1 copy.13.action
  126.3 0.7 collective-permute-done.5.other
  126.9 0.0 copy-start.6
  126.9 1.2 copy-done.6
  128.2 1.5 %finish.1 = (f32[128,384]{1,0:T(8,128)}, bf16[16,64,192]{2,1,0:T(8,128)(2,1)}) custom-call(s32[1]{0:T(128)} %bitcast.16.counts, f32[1,384]{1,0:T(1,128)S(1)} %get-tuple-element.45.sums, f32[1,384]{1,0:T(1,128)S(1)} %collective-permute-done.5.other, f32[32,4,128]{2,1,0:T(4,128)S(1)} %all-to-all-done.1.stats, f32[1,384]{1,0:T(1,128)S(1)} %get-tuple-element.37.film, ...), custom_call_target="tpu_custom_call" | custom-call | flops 1000000000 | bytes 1840128 | tf_op jit(solution)/shard_map/finish/pallas_call | solution.py:412
  129.7 3.9 %all-to-all-done.4.tiles = bf16[32,16,128]{2,1,0:T(8,128)(2,1)S(1)} async-done(((bf16[32,16,128]{2,1,0:T(8,128)(2,1)}), bf16[32,16,128]{2,1,0:T(8,128)(2,1)S(1)}, u32[]{:S(2)}, u32[]{:S(2)}) %all-to-all-start.4) | async-done | bytes 131104 | tf_op jit(solution)/shard_map/all_to_all | solution.py:426
  133.6 1.1 unpack.1
  (2 shorter events, 0.0 us)
Async XLA Ops:
  1.3 0.7 copy-start.1
  1.9 1.0 copy-start.7
  3.0 1.0 copy-start.8
  4.0 0.9 copy-start.9
  4.9 0.7 copy-start.11
  5.6 19.4 %copy-start = (s32[1,1,2,12]{3,2,1,0:T(2,128)S(1)}, s32[1,1,2,12]{3,2,1,0:T(2,128)}, u32[]{:S(2)}) copy-start(s32[1,1,2,12]{3,2,1,0:T(2,128)} %param.14) | copy-start | bytes 292
  6.9 42.7 %copy-start.10 = (s32[1,1,16,27]{3,2,1,0:T(8,128)S(1)}, s32[1,1,16,27]{3,2,1,0:T(8,128)}, u32[]{:S(2)}) copy-start(s32[1,1,16,27]{3,2,1,0:T(8,128)} %param.12) | copy-start | bytes 5188
  6.9 18.1 %collective-permute-start = (bf16[16,16,192]{2,1,0:T(8,128)(2,1)S(1)}, bf16[16,16,192]{2,1,0:T(8,128)(2,1)S(1)}, u32[]{:S(2)}, u32[]{:S(2)}) collective-permute-start(bf16[16,16,192]{2,1,0:T(8,128)(2,1)S(1)} %get-tuple-element.29), channel_id=1, source_target_pairs={{0,32},{32,64},{64,96},{96,128},{128,160},{160,192},{192,224},{224... | collective-permute-start | bytes 294920 | tf_op jit(solution)/shard_map/ppermute | solution.py:449
  11.6 13.4 %collective-permute-start.1 = (bf16[16,16,192]{2,1,0:T(8,128)(2,1)S(1)}, bf16[16,16,192]{2,1,0:T(8,128)(2,1)S(1)}, u32[]{:S(2)}, u32[]{:S(2)}) collective-permute-start(bf16[16,16,192]{2,1,0:T(8,128)(2,1)S(1)} %get-tuple-element.30), channel_id=1, source_target_pairs={{32,0},{64,32},{96,64},{128,96},{160,128},{192,160},{224,192},{256... | collective-permute-start | bytes 294920 | tf_op jit(solution)/shard_map/ppermute | solution.py:450
  26.6 23.0 %collective-permute-start.2 = (bf16[16,16,384]{2,1,0:T(8,128)(2,1)S(1)}, bf16[16,16,384]{2,1,0:T(8,128)(2,1)S(1)}, u32[]{:S(2)}, u32[]{:S(2)}) collective-permute-start(bf16[16,16,384]{2,1,0:T(8,128)(2,1)S(1)} %get-tuple-element.32), channel_id=1, source_target_pairs={{0,1},{1,2},{2,3},{3,4},{4,5},{5,6},{6,7},{7,8},{8,9},{9,10},{10,1... | collective-permute-start | bytes 589832 | tf_op jit(solution)/shard_map/ppermute | solution.py:461
  30.8 18.8 %collective-permute-start.3 = (bf16[16,16,384]{2,1,0:T(8,128)(2,1)S(1)}, bf16[16,16,384]{2,1,0:T(8,128)(2,1)S(1)}, u32[]{:S(2)}, u32[]{:S(2)}) collective-permute-start(bf16[16,16,384]{2,1,0:T(8,128)(2,1)S(1)} %get-tuple-element.33), channel_id=1, source_target_pairs={{1,0},{2,1},{3,2},{4,3},{5,4},{6,5},{7,6},{8,7},{9,8},{10,9},{11,1... | collective-permute-start | bytes 589832 | tf_op jit(solution)/shard_map/ppermute | solution.py:462
  32.1 28.7 %all-to-all-start.1 = ((f32[32,4,128]{2,1,0:T(4,128)}), f32[32,4,128]{2,1,0:T(4,128)S(1)}, u32[]{:S(2)}, u32[]{:S(2)}) async-start(f32[32,4,128]{2,1,0:T(4,128)} %get-tuple-element.36), calls=%async_computation.1 | async-start | bytes 131072 | tf_op jit(solution)/shard_map/all_to_all | solution.py:426
  49.6 1.8 %copy-start.3 = (bf16[192,27,192]{2,0,1:T(8,128)(2,1)S(1)}, bf16[192,27,192]{2,0,1:T(8,128)(2,1)}, u32[]{:S(2)}) copy-start(bf16[192,27,192]{2,0,1:T(8,128)(2,1)} %param.16) | copy-start | bytes 5971972
  58.2 1.2 copy-start.14
  60.7 1.5 %copy-start.15 = (bf16[6,6,6,16,192]{4,3,2,1,0:T(8,128)(2,1)S(1)}, bf16[6,6,6,16,192]{4,3,2,1,0:T(8,128)(2,1)}, u32[]{:S(2)}) copy-start(bf16[6,6,6,16,192]{4,3,2,1,0:T(8,128)(2,1)} %copy-done.14) | copy-start | bytes 3981316
  68.6 5.2 %copy-start.12 = (bf16[6,6,6,16,192]{4,3,2,1,0:T(8,128)(2,1)}, bf16[6,6,6,16,192]{4,3,2,1,0:T(8,128)(2,1)S(1)}, u32[]{:S(2)}) copy-start(bf16[6,6,6,16,192]{4,3,2,1,0:T(8,128)(2,1)S(1)} %get-tuple-element.38.padded_at) | copy-start | bytes 3981316
  68.6 6.5 %collective-permute-start.4 = (bf16[8,11,16,384]{3,2,1,0:T(8,128)(2,1)S(1)}, bf16[8,11,16,384]{3,2,1,0:T(8,128)(2,1)S(1)}, u32[]{:S(2)}, u32[]{:S(2)}) collective-permute-start(bf16[8,11,16,384]{3,2,1,0:T(8,128)(2,1)S(1)} %get-tuple-element.43), channel_id=1, source_target_pairs={{0,32},{32,0},{64,96},{96,64},{128,160},{160,128},{192,224},{224,1... | collective-permute-start | bytes 3244040 | tf_op jit(solution)/shard_map/ppermute | solution.py:490
  73.8 1.0 copy-start.5
  76.5 19.4 %all-to-all-start.2 = ((bf16[8,11,16,384]{3,2,1,0:T(8,128)(2,1)}), bf16[8,11,16,384]{3,2,1,0:T(8,128)(2,1)S(1)}, u32[]{:S(2)}, u32[]{:S(2)}) async-start(bf16[8,11,16,384]{3,2,1,0:T(8,128)(2,1)} %select_convert_fusion), calls=%async_computation.2 | async-start | bytes 2162688 | tf_op jit(solution)/shard_map/all_to_all | solution.py:426
  80.0 1.8 %copy-start.4 = (bf16[192,27,192]{2,0,1:T(8,128)(2,1)S(1)}, bf16[192,27,192]{2,0,1:T(8,128)(2,1)}, u32[]{:S(2)}) copy-start(bf16[192,27,192]{2,0,1:T(8,128)(2,1)} %param.16) | copy-start | bytes 5971972
  81.8 1.5 %copy-start.13 = (bf16[6,6,6,16,192]{4,3,2,1,0:T(8,128)(2,1)S(1)}, bf16[6,6,6,16,192]{4,3,2,1,0:T(8,128)(2,1)}, u32[]{:S(2)}) copy-start(bf16[6,6,6,16,192]{4,3,2,1,0:T(8,128)(2,1)} %copy-done.12) | copy-start | bytes 3981316
  90.4 35.7 %copy-start.2 = (f32[128]{0:T(128)S(1)}, f32[128]{0:T(128)}, u32[]{:S(2)}) copy-start(f32[128]{0:T(128)} %param.15) | copy-start | bytes 1540
  117.5 16.1 %all-to-all-start.4 = ((bf16[32,16,128]{2,1,0:T(8,128)(2,1)}), bf16[32,16,128]{2,1,0:T(8,128)(2,1)S(1)}, u32[]{:S(2)}, u32[]{:S(2)}) async-start(bf16[32,16,128]{2,1,0:T(8,128)(2,1)} %get-tuple-element.48), calls=%async_computation.4 | async-start | bytes 262144 | tf_op jit(solution)/shard_map/all_to_all | solution.py:426
  122.3 4.7 %collective-permute-start.5 = (f32[1,384]{1,0:T(1,128)S(1)}, f32[1,384]{1,0:T(1,128)S(1)}, u32[]{:S(2)}, u32[]{:S(2)}) collective-permute-start(f32[1,384]{1,0:T(1,128)S(1)} %get-tuple-element.45.sums), channel_id=1, source_target_pairs={{0,32},{32,0},{64,96},{96,64},{128,160},{160,128},{192,224},{224,1... | collective-permute-start | bytes 4616 | tf_op jit(solution)/shard_map/ppermute | solution.py:520
  126.9 1.2 copy-start.6

commit v6 on v5

--- a/solution.py
+++ b/solution.py
@@ -1,3 +1,5 @@
+import math
+
 import jax
 import jax.numpy as jnp
 from jax import lax
@@ -82,9 +84,18 @@
 
 
 def pack_kernel(
-    counts, send_x, feat, cot, action, film_weight, held, up, stats, face_low, face_high, film
+    counts, send_x, feat_at, cot_at, film_at, action_at,
+    held, up, stats, face_low, face_high, film, feat, cot, film_weight, action, done,
 ):
+    pairs = ((feat_at, feat), (cot_at, cot), (film_at, film_weight), (action_at, action))
+    copies = [
+        pltpu.make_async_copy(source, target, done.at[n]) for n, (source, target) in enumerate(pairs)
+    ]
+    for copy in copies:
+        copy.start()
     swap = swap_matrix(counts[0])
+    for copy in copies:
+        copy.wait()
     total = jnp.zeros((1, CHANNELS), F32)
     square = jnp.zeros((1, CHANNELS), F32)
     for g in range(4):
@@ -198,7 +209,7 @@
 
 def early_kernel(
     held, up, lower, upper, side_l, side_u, rule, weight_at,
-    raw, back, turned, wide, low_y, high_y, weight, done,
+    raw_at, back, turned, raw, wide, low_y, high_y, weight, done,
 ):
     copy = pltpu.make_async_copy(weight_at, weight, done.at[0])
     copy.start()
@@ -206,6 +217,9 @@
         low_y[...] = one_field(side_l[...], which)
         high_y[...] = one_field(side_u[...], which)
         gather_blocks(rule, 8 * which, own, lower, upper, low_y, high_y, target)
+        if which == 0:
+            out = pltpu.make_async_copy(raw, raw_at, done.at[1])
+            out.start()
     same = jnp.where(iota((CHANNELS, CHANNELS), 0) == iota((CHANNELS, CHANNELS), 1), 1.0, 0.0)
     turned[...] = dot_nt(same.astype(BF16), up[...].reshape(1024, CHANNELS)).astype(BF16)
     back[...] = jnp.zeros_like(back)
@@ -219,13 +233,24 @@
         return carry
 
     lax.fori_loop(0, 9, step, 0)
+    out.wait()
 
 
 def weight_kernel(
-    counts, core, raw, up_turned, rule, stats, film,
-    near, far, padded, turned,
+    counts, core, up_turned, rule, stats, film, raw_at,
+    near, far, padded_at, raw, padded, turned, done,
 ):
+    copy = pltpu.make_async_copy(raw_at, raw, done.at[0])
+    copy.start()
     cells, mean, inverse, scale, shift = norm_terms(stats, film)
+    row, col = iota((256, CHANNELS), 0), iota((256, CHANNELS), 1)
+    group = ((row >> 4) & 7) * 2 + jnp.where(row >= 128, 1 - core[0], core[0])
+    for m in range(4):
+        place = (row + 4 * m) & 15
+        spread = (place < 12) & (col == group * 12 + place)
+        spread = jnp.where(spread, 1.0, 0.0).astype(BF16)
+        turned[m, :, :] = dot(spread, up_turned[...]).astype(BF16)
+
     live = iota((16, 1), 0) < counts[0]
     entries = rule[...]
 
@@ -237,6 +262,7 @@
         x = jnp.where(mask[None], x, 0.0).astype(BF16)
         padded[at] = x.reshape(*lead, 16, CHANNELS)
 
+    copy.wait()
     ranges = (slice(0, 1), slice(1, 5), slice(5, 6))
     for n in range(27):
         x, y, z = n // 9, n // 3 % 3, n % 3
@@ -246,14 +272,8 @@
         else:
             act((ranges[x], ranges[y], ranges[z]), entries[:, n : n + 1] != 16)
 
-    row, col = iota((256, CHANNELS), 0), iota((256, CHANNELS), 1)
-    group = ((row >> 4) & 7) * 2 + jnp.where(row >= 128, 1 - core[0], core[0])
-    for m in range(4):
-        place = (row + 4 * m) & 15
-        spread = (place < 12) & (col == group * 12 + place)
-        spread = jnp.where(spread, 1.0, 0.0).astype(BF16)
-        turned[m, :, :] = dot(spread, up_turned[...]).astype(BF16)
-
+    out = pltpu.make_async_copy(padded, padded_at, done.at[1])
+    out.start()
     line = iota((256, 384), 0) & 15
 
     def pair(m, k1, k2):
@@ -281,6 +301,7 @@
     first, second = pair(0, 24, 25), pair(1, 26, None)
     store(9, jnp.where(line < 12, first, second))
     store(10, jnp.where(line < 8, second, 0.0))
+    out.wait()
 
 
 def split(value):
@@ -289,7 +310,7 @@
     return first, second, value - first - second
 
 
-def slope_kernel(counts, held, up, back, stats, film, kept, lines):
+def slope_kernel(counts, held, up, back, stats, film, kept_at, lines, kept, done):
     cells, mean, inverse, scale, shift = norm_terms(stats, film)
     shift_grad = jnp.zeros((1, CHANNELS), F32)
     scale_grad = jnp.zeros((1, CHANNELS), F32)
@@ -303,14 +324,19 @@
         shift_grad += jnp.sum(slope, axis=0, keepdims=True)
         scale_grad += jnp.sum(slope * normed, axis=0, keepdims=True)
         kept[at, :] = up[part, :, :].reshape(256, CHANNELS).astype(F32) + inverse * (slope * scale)
+    out = pltpu.make_async_copy(kept, kept_at, done.at[0])
+    out.start()
     row = iota((16, 384), 0)
     block = jnp.zeros((16, 384), F32)
     for e, piece in enumerate(split(jnp.concatenate([scale_grad, shift_grad], axis=1))):
         block = jnp.where(row == 8 + e, piece, block)
     lines[...] = block
-
-
-def forward_kernel(counts, held, weight_at, padded_at, output, token, acc, weight, padded, done):
+    out.wait()
+
+
+def forward_kernel(
+    counts, held, weight_at, padded_at, output, token, acc, weight, padded, done,
+):
     token[...] = jnp.zeros_like(token)
     copies = [
         pltpu.make_async_copy(weight_at, weight, done.at[0]),
@@ -366,7 +392,11 @@
     sums[...] = jnp.concatenate([lines[0:1], lines[1:2], lines[2:3]], axis=1)
 
 
-def finish_kernel(counts, sums, other, stats, film, action, held, kept, grad_film, grad_inputs):
+def finish_kernel(
+    counts, sums, other, stats, film, action, held, kept_at, grad_film, grad_inputs, kept, done,
+):
+    copy = pltpu.make_async_copy(kept_at, kept, done.at[0])
+    copy.start()
     total = sums[...] + other[...]
     scale_grad, shift_grad = total[:, :CHANNELS], total[:, CHANNELS:]
     cells, mean, inverse, scale, shift = norm_terms(stats, film)
@@ -374,6 +404,7 @@
     grad_film[:, CHANNELS:] = action[...] * shift_grad
     swap = swap_matrix(None)
     live = (iota((256, 1), 0) & 15) < counts[0]
+    copy.wait()
     for g in range(4):
         part = slice(16 * g, 16 * g + 16)
         x = held[part, :, :].reshape(256, CHANNELS).astype(F32)
@@ -406,16 +437,24 @@
 ANY = pl.BlockSpec(memory_space=pl.ANY)
 
 
-def call(kernel, scalars, arrays, outs, scratch=(), flops=0, name=None, left=0, room=12):
-    shapes = [jax.ShapeDtypeStruct(shape, dtype) for shape, dtype in outs]
-    moved = sum(x.size * x.dtype.itemsize for x in [*arrays, *shapes])
+def call(kernel, scalars, arrays, outs, scratch=(), flops=0, name=None, left=0, room=12, copies=0):
+    split_at = len(arrays) - left
+    arrays = list(arrays[:split_at]) + [
+        pltpu.with_memory_space_constraint(x, pltpu.HBM) for x in arrays[split_at:]
+    ]
+    moved = sum(x.size * x.dtype.itemsize for x in arrays)
+    shapes, specs = [], []
+    for shape, dtype, *marked in outs:
+        moved += math.prod(shape) * jnp.dtype(dtype).itemsize
+        shapes.append(pltpu.HBM(shape, dtype) if marked else jax.ShapeDtypeStruct(shape, dtype))
+        specs.append(ANY if marked else VMEM)
     return pl.pallas_call(
         kernel,
         out_shape=shapes,
-        in_specs=[SMEM] * len(scalars) + [VMEM] * (len(arrays) - left) + [ANY] * left,
-        out_specs=[VMEM] * len(outs),
+        in_specs=[SMEM] * len(scalars) + [VMEM] * split_at + [ANY] * left,
+        out_specs=specs,
         scratch_shapes=[pltpu.VMEM(*s) for s in scratch]
-        + ([pltpu.SemaphoreType.DMA((left,))] if left else []),
+        + ([pltpu.SemaphoreType.DMA((copies,))] if copies else []),
         compiler_params=pltpu.CompilerParams(vmem_limit_bytes=room * MIB),
         cost_estimate=pl.CostEstimate(flops=flops, bytes_accessed=moved, transcendentals=0),
         name=name,
@@ -430,17 +469,21 @@
     size_x, size_y = lax.axis_size("gx"), lax.axis_size("gy")
     count = counts.reshape(1)
     rule = neighbours[0, 0]
+    list_x = pltpu.with_memory_space_constraint(send_x[0, 0], pltpu.HBM)
     block = ((VOXELS, 16, CHANNELS), BF16)
     face = ((16, 16, CHANNELS), BF16)
     spaced = ((6, 6, 6, 16, CHANNELS), BF16)
     joined = ((16, 16, 384), BF16)
     held, up, stats, face_low, face_high, film = call(
         pack_kernel,
-        [count, send_x[0, 0]],
-        [features[0, 0], cotangent[0, 0], action[None], film_weight],
+        [count, list_x],
+        [features[0, 0], cotangent[0, 0], film_weight, action[None]],
         [block, block, ((size_x, 4, 128), F32), face, face, ((1, 2 * CHANNELS), F32)],
+        [((SLOTS, VOXELS, CHANNELS), BF16), ((SLOTS, VOXELS, CHANNELS), BF16), ((128, 2 * CHANNELS), F32), ((1, 128), F32)],
         flops=10**9,
         name="pack",
+        left=4,
+        copies=4,
     )
     up_x = [(i, i + 1) for i in range(size_x - 1)]
     down_x = [(i + 1, i) for i in range(size_x - 1)]
@@ -469,22 +512,25 @@
         early_kernel,
         [],
         [held, up, lower, upper, side_l, side_u, rule, weight],
-        [spaced, total, ((CHANNELS, 1024), BF16)],
-        [spaced, face, face, taps],
+        [(*spaced, True), total, ((CHANNELS, 1024), BF16)],
+        [spaced, spaced, face, face, taps],
         flops=3 * 10**9,
         name="early",
         left=1,
+        copies=2,
         room=20,
     )
     half = ((8, TILES, 16, 384), BF16)
     near, far, padded = call(
         weight_kernel,
         [count, core.reshape(1)],
-        [raw, turned, rule, stats, film],
-        [half, half, spaced],
-        [((4, 256, 1024), BF16)],
+        [turned, rule, stats, film, raw],
+        [half, half, (*spaced, True)],
+        [spaced, spaced, ((4, 256, 1024), BF16)],
         flops=4 * 10**9,
         name="weight",
+        left=1,
+        copies=2,
         room=20,
     )
     other = lax.ppermute(far, "gx", swapped)
@@ -492,9 +538,11 @@
         slope_kernel,
         [count],
         [held, up, back, stats, film],
-        [total, ((16, 384), F32)],
+        [(*total, True), ((16, 384), F32)],
+        [total],
         flops=10**8,
         name="slope",
+        copies=1,
     )
     tile = lax.broadcasted_iota(jnp.int32, half[0], 1)
     row = lax.broadcasted_iota(jnp.int32, half[0], 2)
@@ -510,6 +558,7 @@
         flops=3 * 10**9,
         name="forward",
         left=2,
+        copies=2,
         room=16,
     )
     (shares,) = call(share_kernel, [], [parts, token], [((size_y, 24, 128), BF16)], name="share")
@@ -524,8 +573,11 @@
         [count],
         [sums, other, stats, film, action[:, None], held, kept],
         [((128, 2 * CHANNELS), F32), ((SLOTS, VOXELS, CHANNELS), BF16)],
+        [total],
         flops=10**9,
         name="finish",
+        left=1,
+        copies=1,
     )
     (grad_weight,) = call(unpack_kernel, [], [tiles], [((12, 27, CHANNELS), F32)], name="unpack")
     return output[None, None], grad_inputs[None, None], grad_weight, grad_film

time: 137 us -> 132 us (0.964)
  local copies, waits for them, and re-layouts: 14.4 us -> 0.13 us
  Pallas kernels: 27.5 us -> 35.4 us
  waiting for transfers between devices: 11.6 us -> 14.7 us
    unnamed x32 -> x6, local copies, waits for them, and re-layouts: 14.3 us -> 0.02 us
    pallas_call x10, Pallas kernels: 27.5 us -> 35.4 us  [call(): pl.pallas_call(kernel, out_shape=shapes, in_specs=[SMEM] * len(scalars) +...]
    all_to_all x3, waiting for transfers between devices: 10.6 us -> 13.6 us  [exchange(): lax.all_to_all(array, axis, 0, 0, axis_index_groups=groups, tiled=True)]
  transfers between devices with their start and end apart: 9 -> 9, of which waited for: 5 -> 5; matrix products, arithmetic and copies ran while one was open for 0% -> 0% of each run, Pallas kernels for 12% -> 17%
where the time goes in v6:
time: 132 us; the launch traced here: 130 us
  starting transfers between devices  49.4 us (37%)
  Pallas kernels  35.4 us (27%)
  blocking collectives  27.4 us (21%)
  waiting for transfers between devices  14.7 us (11%)
  between operations  1.48 us (1%)
  other arithmetic  1.42 us (1%)
    pallas_call x10, Pallas kernels, call(): pl.pallas_call(kernel, out_shape=shapes, in_specs=[SMEM] * len(scalars) +...  35.4 us
    all_to_all x2, blocking collectives, exchange(): lax.all_to_all(array, axis, 0, 0, axis_index_groups=groups, tiled=True)  27.4 us
    all_to_all x3, starting transfers between devices, exchange(): lax.all_to_all(array, axis, 0, 0, axis_index_groups=groups, tiled=True)  25.8 us
    all_to_all x3, waiting for transfers between devices, exchange(): lax.all_to_all(array, axis, 0, 0, axis_index_groups=groups, tiled=True)  13.6 us
    ppermute x1, starting transfers between devices, body(): upper = lax.ppermute(face_low, 'gx', down_x)  5.49 us
    ppermute x1, starting transfers between devices, body(): lower = lax.ppermute(face_high, 'gx', up_x)  4.6 us
    ppermute x1, starting transfers between devices, body(): side_l = lax.ppermute(face_high, 'gy', up_y)  4.21 us
    ppermute x1, starting transfers between devices, body(): other = lax.ppermute(far, 'gx', swapped)  4.21 us
  transfers between devices with their start and end apart: 9, of which 5 were waited for; matrix products, arithmetic and copies ran while one was open for 0% of the time, Pallas kernels for 17%

profile of v6, /device:TPU:1, one launch (start us, length us, event | category | flops | bytes accessed | tf_op | source)
XLA Modules:
  0.0 130.0 jit_solution(15170358192784765422)
XLA Ops:
  1.3 0.0 copy-start
  1.3 2.8 %pack.1 = (bf16[64,16,192]{2,1,0:T(8,128)(2,1)S(1)}, bf16[64,16,192]{2,1,0:T(8,128)(2,1)S(1)}, f32[16,4,128]{2,1,0:T(4,128)S(1)}, bf16[16,16,192]{2,1,0:T(8,128)...) custom-call(s32[1]{0:T(128)} %bitcast.12.counts, s32[2,8]{1,0:T(2,128)} %bitcast.26, ...), custom_call_target="tpu_custom_call" | custom-call | flops 1000000000 | bytes 2000896 | tf_op jit(solution)/shard_map/pack/pallas_call | solution.py:451
  4.1 0.0 copy-start.1
  4.1 4.6 %collective-permute-start = (bf16[16,16,192]{2,1,0:T(8,128)(2,1)S(1)}, bf16[16,16,192]{2,1,0:T(8,128)(2,1)S(1)}, u32[]{:S(2)}, u32[]{:S(2)}) collective-permute-start(bf16[16,16,192]{2,1,0:T(8,128)(2,1)S(1)} %get-tuple-element.29), channel_id=1, source_target_pairs={{0,32},{32,64},{64,96},{96,128},{128,160},{160,192},{192,224},{224... | collective-permute-start | bytes 294920 | tf_op jit(solution)/shard_map/ppermute | solution.py:492
  8.7 5.5 %collective-permute-start.1 = (bf16[16,16,192]{2,1,0:T(8,128)(2,1)S(1)}, bf16[16,16,192]{2,1,0:T(8,128)(2,1)S(1)}, u32[]{:S(2)}, u32[]{:S(2)}) collective-permute-start(bf16[16,16,192]{2,1,0:T(8,128)(2,1)S(1)} %get-tuple-element.30), channel_id=1, source_target_pairs={{32,0},{64,32},{96,64},{128,96},{160,128},{192,160},{224,192},{256... | collective-permute-start | bytes 294920 | tf_op jit(solution)/shard_map/ppermute | solution.py:493
  14.2 7.9 %all_to_all.25.stats = f32[16,4,128]{2,1,0:T(4,128)S(1)} all-to-all(f32[16,4,128]{2,1,0:T(4,128)S(1)} %get-tuple-element.31), channel_id=1, replica_groups=mesh['gx'=16,'gy'=32] {'gx'}, dimensions={0} | all-to-all | bytes 65536 | tf_op jit(solution)/shard_map/all_to_all | solution.py:465
  22.1 0.0 collective-permute-done.lower
  22.1 0.0 collective-permute-done.1.upper
  22.1 0.0 copy-done
  22.1 1.5 %cross.1 = (bf16[16,16,384]{2,1,0:T(8,128)(2,1)S(1)}, bf16[16,16,384]{2,1,0:T(8,128)(2,1)S(1)}, f32[32,4,128]{2,1,0:T(4,128)}) custom-call(s32[2,12]{1,0:T(2,128)S(1)} %bitcast.17, bf16[64,16,192]{2,1,0:T(8,128)(2,1)S(1)} %get-tuple-element.27.held, bf16[64,16,192]{2,1,0:T(8,128)(2,1)S(1)} %get-tuple-element.28.up, ...), custom_call_target="tpu_custom_call" | custom-call | flops 100000000 | bytes 1474560 | tf_op jit(solution)/shard_map/cross/pallas_call | solution.py:451
  23.7 4.2 %collective-permute-start.2 = (bf16[16,16,384]{2,1,0:T(8,128)(2,1)S(1)}, bf16[16,16,384]{2,1,0:T(8,128)(2,1)S(1)}, u32[]{:S(2)}, u32[]{:S(2)}) collective-permute-start(bf16[16,16,384]{2,1,0:T(8,128)(2,1)S(1)} %get-tuple-element.32), channel_id=1, source_target_pairs={{0,1},{1,2},{2,3},{3,4},{4,5},{5,6},{6,7},{7,8},{8,9},{9,10},{10,1... | collective-permute-start | bytes 589832 | tf_op jit(solution)/shard_map/ppermute | solution.py:504
  27.9 1.3 collective-permute-start.3
  29.2 17.5 %all-to-all-start.1 = ((f32[32,4,128]{2,1,0:T(4,128)}), f32[32,4,128]{2,1,0:T(4,128)S(1)}, u32[]{:S(2)}, u32[]{:S(2)}) async-start(f32[32,4,128]{2,1,0:T(4,128)} %get-tuple-element.35), calls=%async_computation.1 | async-start | bytes 131072 | tf_op jit(solution)/shard_map/all_to_all | solution.py:465
  46.7 0.0 collective-permute-done.2.side_l
  46.7 0.0 collective-permute-done.3.side_u
  46.7 0.0 copy-done.1
  46.7 8.5 %early.1 = (bf16[6,6,6,16,192]{4,3,2,1,0:T(8,128)(2,1)}, f32[1024,192]{1,0:T(8,128)S(1)}, bf16[192,1024]{1,0:T(8,128)(2,1)S(1)}) custom-call(bf16[64,16,192]{2,1,0:T(8,128)(2,1)S(1)} %get-tuple-element.27.held, bf16[64,16,192]{2,1,0:T(8,128)(2,1)S(1)} %get-tuple-element.28.up, bf16[16,16,192]{2,1,0:T(8,128)(2,1)S(1)} %collective-permute-done.lower, ...), custom_call_target="tpu_custom_call" | custom-call | flops 3000000000 | bytes 5875392 | tf_op jit(solution)/shard_map/early/pallas_call | solution.py:451
  55.2 2.6 %all-to-all-done.1.stats = f32[32,4,128]{2,1,0:T(4,128)S(1)} async-done(((f32[32,4,128]{2,1,0:T(4,128)}), f32[32,4,128]{2,1,0:T(4,128)S(1)}, u32[]{:S(2)}, u32[]{:S(2)}) %all-to-all-start.1) | async-done | bytes 65568 | tf_op jit(solution)/shard_map/all_to_all | solution.py:465
  57.9 7.3 %weight.1 = (bf16[8,11,16,384]{3,2,1,0:T(8,128)(2,1)S(1)}, bf16[8,11,16,384]{3,2,1,0:T(8,128)(2,1)S(1)}, bf16[6,6,6,16,192]{4,3,2,1,0:T(8,128)(2,1)}) custom-call(s32[1]{0:T(128)} %bitcast.13.counts, s32[1]{0:T(128)} %bitcast.6.core, bf16[192,1024]{1,0:T(8,128)(2,1)S(1)} %get-tuple-element.34.up_turned, s32[16,27]{1,0:T(8,128)S(1)} %bitcast.19, ...), custom_call_target="tpu_custom_call" | custom-call | flops 4000000000 | bytes 5278912 | tf_op jit(solution)/shard_map/weight/pallas_call | solution.py:451
  65.2 4.2 %collective-permute-start.4 = (bf16[8,11,16,384]{3,2,1,0:T(8,128)(2,1)S(1)}, bf16[8,11,16,384]{3,2,1,0:T(8,128)(2,1)S(1)}, u32[]{:S(2)}, u32[]{:S(2)}) collective-permute-start(bf16[8,11,16,384]{3,2,1,0:T(8,128)(2,1)S(1)} %get-tuple-element.43), channel_id=1, source_target_pairs={{0,32},{32,0},{64,96},{96,64},{128,160},{160,128},{192,224},{224,1... | collective-permute-start | bytes 3244040 | tf_op jit(solution)/shard_map/ppermute | solution.py:536
  69.4 1.9 %slope.1 = (f32[1024,192]{1,0:T(8,128)}, f32[16,384]{1,0:T(8,128)S(1)}) custom-call(s32[1]{0:T(128)} %bitcast.15.counts, bf16[64,16,192]{2,1,0:T(8,128)(2,1)S(1)} %get-tuple-element.27.held, bf16[64,16,192]{2,1,0:T(8,128)(2,1)S(1)} %get-tuple-element.28.up, f32[1024,192]{1,0:T(8,128)S(1)} %get-tuple-element.40.back, f32[32,4,128]{2,1,0:T(4,128)S(1)} %all-to-all-done.1.stats, ...), custom_call_target="tpu_custom_call" | custom-call | flops 100000000 | bytes 2450944 | tf_op jit(solution)/shard_map/slope/pallas_call | solution.py:451
  71.3 0.4 collective-permute-done.4
  71.7 1.4 %select_convert_fusion = bf16[8,11,16,384]{3,2,1,0:T(8,128)(2,1)} fusion(bf16[8,11,16,384]{3,2,1,0:T(8,128)(2,1)S(1)} %collective-permute-done.4, bf16[8,11,16,384]{3,2,1,0:T(8,128)(2,1)S(1)} %get-tuple-element.42, f32[16,384]{1,0:T(8,128)S(1)} %get-tuple-element.41, pred[16]{0:T(512)(128)(4,1)S(1)} %iota_compare_fusion, pred[11]{0:T(512)(128)(4,1)S(1)} %iota_compare_fusion.1), kind=kLoop, calls=%fused_computation | loop fusion | flops 2703360 | bytes 3268635 | tf_op jit(solution)/shard_map/convert_element_type | solution.py:550
  73.1 3.6 %all-to-all-start.2 = ((bf16[8,11,16,384]{3,2,1,0:T(8,128)(2,1)}), bf16[8,11,16,384]{3,2,1,0:T(8,128)(2,1)S(1)}, u32[]{:S(2)}, u32[]{:S(2)}) async-start(bf16[8,11,16,384]{3,2,1,0:T(8,128)(2,1)} %select_convert_fusion), calls=%async_computation.2 | async-start | bytes 2162688 | tf_op jit(solution)/shard_map/all_to_all | solution.py:465
  76.7 8.8 %forward.1 = (bf16[16,64,192]{2,1,0:T(8,128)(2,1)}, f32[8,128]{1,0:T(8,128)S(1)}) custom-call(s32[1]{0:T(128)} %bitcast.14.counts, bf16[64,16,192]{2,1,0:T(8,128)(2,1)S(1)} %get-tuple-element.27.held, bf16[27,192,192]{2,1,0:T(8,128)(2,1)} %bitcast.23, bf16[6,6,6,16,192]{4,3,2,1,0:T(8,128)(2,1)} %get-tuple-element.38.padded_at), custom_call_target="tpu_custom_call" | custom-call | flops 3000000000 | bytes 4108288 | tf_op jit(solution)/shard_map/forward/pallas_call | solution.py:451
  85.5 0.0 copy-start.2
  85.5 7.0 %all-to-all-done.2.parts = bf16[8,11,16,384]{3,2,1,0:T(8,128)(2,1)S(1)} async-done(((bf16[8,11,16,384]{3,2,1,0:T(8,128)(2,1)}), bf16[8,11,16,384]{3,2,1,0:T(8,128)(2,1)S(1)}, u32[]{:S(2)}, u32[]{:S(2)}) %all-to-all-start.2) | async-done | bytes 1081376 | tf_op jit(solution)/shard_map/all_to_all | solution.py:465
  92.5 0.1 share.1
  92.6 19.5 %all_to_all.26.parts = bf16[32,24,128]{2,1,0:T(8,128)(2,1)S(1)} all-to-all(bf16[32,24,128]{2,1,0:T(8,128)(2,1)S(1)} %share.1), channel_id=1, replica_groups=mesh['gx'=16,'gy'=32] {'gy'}, dimensions={0} | all-to-all | bytes 393216 | tf_op jit(solution)/shard_map/all_to_all | solution.py:465
  112.2 0.7 own.1
  112.9 4.8 %all-to-all-start.4 = ((bf16[32,16,128]{2,1,0:T(8,128)(2,1)}), bf16[32,16,128]{2,1,0:T(8,128)(2,1)S(1)}, u32[]{:S(2)}, u32[]{:S(2)}) async-start(bf16[32,16,128]{2,1,0:T(8,128)(2,1)} %get-tuple-element.48), calls=%async_computation.4 | async-start | bytes 262144 | tf_op jit(solution)/shard_map/all_to_all | solution.py:465
  117.7 3.8 %collective-permute-start.5 = (f32[1,384]{1,0:T(1,128)S(1)}, f32[1,384]{1,0:T(1,128)S(1)}, u32[]{:S(2)}, u32[]{:S(2)}) collective-permute-start(f32[1,384]{1,0:T(1,128)S(1)} %get-tuple-element.45.sums), channel_id=1, source_target_pairs={{0,32},{32,0},{64,96},{96,64},{128,160},{160,128},{192,224},{224,1... | collective-permute-start | bytes 4616 | tf_op jit(solution)/shard_map/ppermute | solution.py:569
  121.5 0.0 copy-done.2
  121.5 0.1 copy.13.action
  121.6 0.7 collective-permute-done.5.other
  122.3 2.6 %finish.1 = (f32[128,384]{1,0:T(8,128)}, bf16[16,64,192]{2,1,0:T(8,128)(2,1)}) custom-call(s32[1]{0:T(128)} %bitcast.16.counts, f32[1,384]{1,0:T(1,128)S(1)} %get-tuple-element.45.sums, f32[1,384]{1,0:T(1,128)S(1)} %collective-permute-done.5.other, f32[32,4,128]{2,1,0:T(4,128)S(1)} %all-to-all-done.1.stats, f32[1,384]{1,0:T(1,128)S(1)} %get-tuple-element.36.film, ...), custom_call_target="tpu_custom_call" | custom-call | flops 1000000000 | bytes 1840128 | tf_op jit(solution)/shard_map/finish/pallas_call | solution.py:451
  124.9 4.0 %all-to-all-done.4.tiles = bf16[32,16,128]{2,1,0:T(8,128)(2,1)S(1)} async-done(((bf16[32,16,128]{2,1,0:T(8,128)(2,1)}), bf16[32,16,128]{2,1,0:T(8,128)(2,1)S(1)}, u32[]{:S(2)}, u32[]{:S(2)}) %all-to-all-start.4) | async-done | bytes 131104 | tf_op jit(solution)/shard_map/all_to_all | solution.py:465
  129.0 1.1 unpack.1
  (2 shorter events, 0.0 us)
Async XLA Ops:
  1.3 20.8 %copy-start = (s32[1,1,2,12]{3,2,1,0:T(2,128)S(1)}, s32[1,1,2,12]{3,2,1,0:T(2,128)}, u32[]{:S(2)}) copy-start(s32[1,1,2,12]{3,2,1,0:T(2,128)} %param.14) | copy-start | bytes 292
  4.1 42.6 %copy-start.1 = (s32[1,1,16,27]{3,2,1,0:T(8,128)S(1)}, s32[1,1,16,27]{3,2,1,0:T(8,128)}, u32[]{:S(2)}) copy-start(s32[1,1,16,27]{3,2,1,0:T(8,128)} %param.12) | copy-start | bytes 5188
  4.1 18.0 %collective-permute-start = (bf16[16,16,192]{2,1,0:T(8,128)(2,1)S(1)}, bf16[16,16,192]{2,1,0:T(8,128)(2,1)S(1)}, u32[]{:S(2)}, u32[]{:S(2)}) collective-permute-start(bf16[16,16,192]{2,1,0:T(8,128)(2,1)S(1)} %get-tuple-element.29), channel_id=1, source_target_pairs={{0,32},{32,64},{64,96},{96,128},{128,160},{160,192},{192,224},{224... | collective-permute-start | bytes 294920 | tf_op jit(solution)/shard_map/ppermute | solution.py:492
  8.7 13.4 %collective-permute-start.1 = (bf16[16,16,192]{2,1,0:T(8,128)(2,1)S(1)}, bf16[16,16,192]{2,1,0:T(8,128)(2,1)S(1)}, u32[]{:S(2)}, u32[]{:S(2)}) collective-permute-start(bf16[16,16,192]{2,1,0:T(8,128)(2,1)S(1)} %get-tuple-element.30), channel_id=1, source_target_pairs={{32,0},{64,32},{96,64},{128,96},{160,128},{192,160},{224,192},{256... | collective-permute-start | bytes 294920 | tf_op jit(solution)/shard_map/ppermute | solution.py:493
  23.7 23.0 %collective-permute-start.2 = (bf16[16,16,384]{2,1,0:T(8,128)(2,1)S(1)}, bf16[16,16,384]{2,1,0:T(8,128)(2,1)S(1)}, u32[]{:S(2)}, u32[]{:S(2)}) collective-permute-start(bf16[16,16,384]{2,1,0:T(8,128)(2,1)S(1)} %get-tuple-element.32), channel_id=1, source_target_pairs={{0,1},{1,2},{2,3},{3,4},{4,5},{5,6},{6,7},{7,8},{8,9},{9,10},{10,1... | collective-permute-start | bytes 589832 | tf_op jit(solution)/shard_map/ppermute | solution.py:504
  27.9 18.8 %collective-permute-start.3 = (bf16[16,16,384]{2,1,0:T(8,128)(2,1)S(1)}, bf16[16,16,384]{2,1,0:T(8,128)(2,1)S(1)}, u32[]{:S(2)}, u32[]{:S(2)}) collective-permute-start(bf16[16,16,384]{2,1,0:T(8,128)(2,1)S(1)} %get-tuple-element.33), channel_id=1, source_target_pairs={{1,0},{2,1},{3,2},{4,3},{5,4},{6,5},{7,6},{8,7},{9,8},{10,9},{11,1... | collective-permute-start | bytes 589832 | tf_op jit(solution)/shard_map/ppermute | solution.py:505
  29.2 28.7 %all-to-all-start.1 = ((f32[32,4,128]{2,1,0:T(4,128)}), f32[32,4,128]{2,1,0:T(4,128)S(1)}, u32[]{:S(2)}, u32[]{:S(2)}) async-start(f32[32,4,128]{2,1,0:T(4,128)} %get-tuple-element.35), calls=%async_computation.1 | async-start | bytes 131072 | tf_op jit(solution)/shard_map/all_to_all | solution.py:465
  65.2 6.5 %collective-permute-start.4 = (bf16[8,11,16,384]{3,2,1,0:T(8,128)(2,1)S(1)}, bf16[8,11,16,384]{3,2,1,0:T(8,128)(2,1)S(1)}, u32[]{:S(2)}, u32[]{:S(2)}) collective-permute-start(bf16[8,11,16,384]{3,2,1,0:T(8,128)(2,1)S(1)} %get-tuple-element.43), channel_id=1, source_target_pairs={{0,32},{32,0},{64,96},{96,64},{128,160},{160,128},{192,224},{224,1... | collective-permute-start | bytes 3244040 | tf_op jit(solution)/shard_map/ppermute | solution.py:536
  73.1 19.4 %all-to-all-start.2 = ((bf16[8,11,16,384]{3,2,1,0:T(8,128)(2,1)}), bf16[8,11,16,384]{3,2,1,0:T(8,128)(2,1)S(1)}, u32[]{:S(2)}, u32[]{:S(2)}) async-start(bf16[8,11,16,384]{3,2,1,0:T(8,128)(2,1)} %select_convert_fusion), calls=%async_computation.2 | async-start | bytes 2162688 | tf_op jit(solution)/shard_map/all_to_all | solution.py:465
  85.5 36.0 %copy-start.2 = (f32[128]{0:T(128)S(1)}, f32[128]{0:T(128)}, u32[]{:S(2)}) copy-start(f32[128]{0:T(128)} %param.15) | copy-start | bytes 1540
  112.9 16.1 %all-to-all-start.4 = ((bf16[32,16,128]{2,1,0:T(8,128)(2,1)}), bf16[32,16,128]{2,1,0:T(8,128)(2,1)S(1)}, u32[]{:S(2)}, u32[]{:S(2)}) async-start(bf16[32,16,128]{2,1,0:T(8,128)(2,1)} %get-tuple-element.48), calls=%async_computation.4 | async-start | bytes 262144 | tf_op jit(solution)/shard_map/all_to_all | solution.py:465
  117.7 4.7 %collective-permute-start.5 = (f32[1,384]{1,0:T(1,128)S(1)}, f32[1,384]{1,0:T(1,128)S(1)}, u32[]{:S(2)}, u32[]{:S(2)}) collective-permute-start(f32[1,384]{1,0:T(1,128)S(1)} %get-tuple-element.45.sums), channel_id=1, source_target_pairs={{0,32},{32,0},{64,96},{96,64},{128,160},{160,128},{192,224},{224,1... | collective-permute-start | bytes 4616 | tf_op jit(solution)/shard_map/ppermute | solution.py:569

commit v7 on v6

--- a/solution.py
+++ b/solution.py
@@ -208,18 +208,14 @@
 
 
 def early_kernel(
-    held, up, lower, upper, side_l, side_u, rule, weight_at,
-    raw_at, back, turned, raw, wide, low_y, high_y, weight, done,
+    up, lower, upper, side_l, side_u, rule, weight_at,
+    back, turned, wide, low_y, high_y, weight, done,
 ):
     copy = pltpu.make_async_copy(weight_at, weight, done.at[0])
     copy.start()
-    for which, own, target in ((0, held, raw), (1, up, wide)):
-        low_y[...] = one_field(side_l[...], which)
-        high_y[...] = one_field(side_u[...], which)
-        gather_blocks(rule, 8 * which, own, lower, upper, low_y, high_y, target)
-        if which == 0:
-            out = pltpu.make_async_copy(raw, raw_at, done.at[1])
-            out.start()
+    low_y[...] = one_field(side_l[...], 1)
+    high_y[...] = one_field(side_u[...], 1)
+    gather_blocks(rule, 8, up, lower, upper, low_y, high_y, wide)
     same = jnp.where(iota((CHANNELS, CHANNELS), 0) == iota((CHANNELS, CHANNELS), 1), 1.0, 0.0)
     turned[...] = dot_nt(same.astype(BF16), up[...].reshape(1024, CHANNELS)).astype(BF16)
     back[...] = jnp.zeros_like(back)
@@ -233,15 +229,12 @@
         return carry
 
     lax.fori_loop(0, 9, step, 0)
-    out.wait()
 
 
 def weight_kernel(
-    counts, core, up_turned, rule, stats, film, raw_at,
-    near, far, padded_at, raw, padded, turned, done,
+    counts, core, held, lower, upper, side_l, side_u, up_turned, rule, stats, film,
+    near, far, padded_at, hid, low, high, low_y, high_y, padded, turned, done,
 ):
-    copy = pltpu.make_async_copy(raw_at, raw, done.at[0])
-    copy.start()
     cells, mean, inverse, scale, shift = norm_terms(stats, film)
     row, col = iota((256, CHANNELS), 0), iota((256, CHANNELS), 1)
     group = ((row >> 4) & 7) * 2 + jnp.where(row >= 128, 1 - core[0], core[0])
@@ -251,28 +244,25 @@
         spread = jnp.where(spread, 1.0, 0.0).astype(BF16)
         turned[m, :, :] = dot(spread, up_turned[...]).astype(BF16)
 
-    live = iota((16, 1), 0) < counts[0]
-    entries = rule[...]
-
-    def act(at, mask):
-        x = raw[at]
-        lead = x.shape[:-2]
-        x = (x.astype(F32).reshape(-1, CHANNELS) - mean) * inverse * scale + shift
-        x = jnp.maximum(x, 0.0).reshape(-1, 16, CHANNELS)
-        x = jnp.where(mask[None], x, 0.0).astype(BF16)
-        padded[at] = x.reshape(*lead, 16, CHANNELS)
-
-    copy.wait()
-    ranges = (slice(0, 1), slice(1, 5), slice(5, 6))
-    for n in range(27):
-        x, y, z = n // 9, n // 3 % 3, n % 3
-        if n == 13:
-            for a in range(1, 5):
-                act((slice(a, a + 1), ranges[1], ranges[1]), live)
-        else:
-            act((ranges[x], ranges[y], ranges[z]), entries[:, n : n + 1] != 16)
-
-    out = pltpu.make_async_copy(padded, padded_at, done.at[1])
+    def act(x):
+        x = (x.astype(F32) - mean) * inverse * scale + shift
+        return jnp.maximum(x, 0.0)
+
+    live = (iota((256, 1), 0) & 15) < counts[0]
+    for g in range(4):
+        part = slice(16 * g, 16 * g + 16)
+        x = act(held[part, :, :].reshape(256, CHANNELS))
+        hid[part, :, :] = jnp.where(live, x, 0.0).astype(BF16).reshape(16, 16, CHANNELS)
+    for source, target in (
+        (lower[...], low),
+        (upper[...], high),
+        (one_field(side_l[...], 0), low_y),
+        (one_field(side_u[...], 0), high_y),
+    ):
+        x = act(source.reshape(256, CHANNELS))
+        target[...] = x.astype(BF16).reshape(16, 16, CHANNELS)
+    gather_blocks(rule, 0, hid, low, high, low_y, high_y, padded)
+    out = pltpu.make_async_copy(padded, padded_at, done.at[0])
     out.start()
     line = iota((256, 384), 0) & 15
 
@@ -508,29 +498,28 @@
     swapped = [(i, i ^ 1) for i in range(size_x)]
     taps = ((27, CHANNELS, CHANNELS), BF16)
     total = ((1024, CHANNELS), F32)
-    raw, back, turned = call(
+    back, turned = call(
         early_kernel,
         [],
-        [held, up, lower, upper, side_l, side_u, rule, weight],
-        [(*spaced, True), total, ((CHANNELS, 1024), BF16)],
-        [spaced, spaced, face, face, taps],
+        [up, lower, upper, side_l, side_u, rule, weight],
+        [total, ((CHANNELS, 1024), BF16)],
+        [spaced, face, face, taps],
         flops=3 * 10**9,
         name="early",
         left=1,
-        copies=2,
+        copies=1,
         room=20,
     )
     half = ((8, TILES, 16, 384), BF16)
     near, far, padded = call(
         weight_kernel,
         [count, core.reshape(1)],
-        [turned, rule, stats, film, raw],
+        [held, lower, upper, side_l, side_u, turned, rule, stats, film],
         [half, half, (*spaced, True)],
-        [spaced, spaced, ((4, 256, 1024), BF16)],
+        [block, face, face, face, face, spaced, ((4, 256, 1024), BF16)],
         flops=4 * 10**9,
         name="weight",
-        left=1,
-        copies=2,
+        copies=1,
         room=20,
     )
     other = lax.ppermute(far, "gx", swapped)

time: 132 us -> 130 us (0.985)
  Pallas kernels: 35.4 us -> 33.5 us
    pallas_call x10, Pallas kernels: 35.4 us -> 33.5 us  [call(): pl.pallas_call(kernel, out_shape=shapes, in_specs=[SMEM] * len(scalars) +...]
  transfers between devices with their start and end apart: 9 -> 9, of which waited for: 5 -> 5; matrix products, arithmetic and copies ran while one was open for 0% -> 0% of each run, Pallas kernels for 17% -> 16%
where the time goes in v7:
time: 130 us; the launch traced here: 128 us
  starting transfers between devices  49.5 us (38%)
  Pallas kernels  33.5 us (26%)
  blocking collectives  26.4 us (20%)
  waiting for transfers between devices  15.7 us (12%)
  between operations  1.48 us (1%)
  other arithmetic  1.42 us (1%)
    pallas_call x10, Pallas kernels, call(): pl.pallas_call(kernel, out_shape=shapes, in_specs=[SMEM] * len(scalars) +...  33.5 us
    all_to_all x2, blocking collectives, exchange(): lax.all_to_all(array, axis, 0, 0, axis_index_groups=groups, tiled=True)  26.4 us
    all_to_all x3, starting transfers between devices, exchange(): lax.all_to_all(array, axis, 0, 0, axis_index_groups=groups, tiled=True)  25.8 us
    all_to_all x3, waiting for transfers between devices, exchange(): lax.all_to_all(array, axis, 0, 0, axis_index_groups=groups, tiled=True)  14.6 us
    ppermute x1, starting transfers between devices, body(): upper = lax.ppermute(face_low, 'gx', down_x)  5.49 us
    ppermute x1, starting transfers between devices, body(): lower = lax.ppermute(face_high, 'gx', up_x)  4.6 us
    ppermute x1, starting transfers between devices, body(): other = lax.ppermute(far, 'gx', swapped)  4.21 us
    ppermute x1, starting transfers between devices, body(): side_l = lax.ppermute(face_high, 'gy', up_y)  4.21 us
  transfers between devices with their start and end apart: 9, of which 5 were waited for; matrix products, arithmetic and copies ran while one was open for 0% of the time, Pallas kernels for 16%

profile of v7, /device:TPU:1, one launch (start us, length us, event | category | flops | bytes accessed | tf_op | source)
XLA Modules:
  0.0 128.0 jit_solution(2140940618778158115)
XLA Ops:
  1.3 0.0 copy-start
  1.3 2.8 %pack.1 = (bf16[64,16,192]{2,1,0:T(8,128)(2,1)S(1)}, bf16[64,16,192]{2,1,0:T(8,128)(2,1)S(1)}, f32[16,4,128]{2,1,0:T(4,128)S(1)}, bf16[16,16,192]{2,1,0:T(8,128)...) custom-call(s32[1]{0:T(128)} %bitcast.12.counts, s32[2,8]{1,0:T(2,128)} %bitcast.26, ...), custom_call_target="tpu_custom_call" | custom-call | flops 1000000000 | bytes 2000896 | tf_op jit(solution)/shard_map/pack/pallas_call | solution.py:441
  4.1 0.0 copy-start.1
  4.1 4.6 %collective-permute-start = (bf16[16,16,192]{2,1,0:T(8,128)(2,1)S(1)}, bf16[16,16,192]{2,1,0:T(8,128)(2,1)S(1)}, u32[]{:S(2)}, u32[]{:S(2)}) collective-permute-start(bf16[16,16,192]{2,1,0:T(8,128)(2,1)S(1)} %get-tuple-element.27), channel_id=1, source_target_pairs={{0,32},{32,64},{64,96},{96,128},{128,160},{160,192},{192,224},{224... | collective-permute-start | bytes 294920 | tf_op jit(solution)/shard_map/ppermute | solution.py:482
  8.7 5.5 %collective-permute-start.1 = (bf16[16,16,192]{2,1,0:T(8,128)(2,1)S(1)}, bf16[16,16,192]{2,1,0:T(8,128)(2,1)S(1)}, u32[]{:S(2)}, u32[]{:S(2)}) collective-permute-start(bf16[16,16,192]{2,1,0:T(8,128)(2,1)S(1)} %get-tuple-element.28), channel_id=1, source_target_pairs={{32,0},{64,32},{96,64},{128,96},{160,128},{192,160},{224,192},{256... | collective-permute-start | bytes 294920 | tf_op jit(solution)/shard_map/ppermute | solution.py:483
  14.2 7.9 %all_to_all.25.stats = f32[16,4,128]{2,1,0:T(4,128)S(1)} all-to-all(f32[16,4,128]{2,1,0:T(4,128)S(1)} %get-tuple-element.30), channel_id=1, replica_groups=mesh['gx'=16,'gy'=32] {'gx'}, dimensions={0} | all-to-all | bytes 65536 | tf_op jit(solution)/shard_map/all_to_all | solution.py:455
  22.1 0.0 collective-permute-done.lower
  22.1 0.0 collective-permute-done.1.upper
  22.1 0.0 copy-done
  22.1 1.5 %cross.1 = (bf16[16,16,384]{2,1,0:T(8,128)(2,1)S(1)}, bf16[16,16,384]{2,1,0:T(8,128)(2,1)S(1)}, f32[32,4,128]{2,1,0:T(4,128)}) custom-call(s32[2,12]{1,0:T(2,128)S(1)} %bitcast.17, bf16[64,16,192]{2,1,0:T(8,128)(2,1)S(1)} %get-tuple-element.26.held, bf16[64,16,192]{2,1,0:T(8,128)(2,1)S(1)} %get-tuple-element.29.up, ...), custom_call_target="tpu_custom_call" | custom-call | flops 100000000 | bytes 1474560 | tf_op jit(solution)/shard_map/cross/pallas_call | solution.py:441
  23.7 4.2 %collective-permute-start.2 = (bf16[16,16,384]{2,1,0:T(8,128)(2,1)S(1)}, bf16[16,16,384]{2,1,0:T(8,128)(2,1)S(1)}, u32[]{:S(2)}, u32[]{:S(2)}) collective-permute-start(bf16[16,16,384]{2,1,0:T(8,128)(2,1)S(1)} %get-tuple-element.31), channel_id=1, source_target_pairs={{0,1},{1,2},{2,3},{3,4},{4,5},{5,6},{6,7},{7,8},{8,9},{9,10},{10,1... | collective-permute-start | bytes 589832 | tf_op jit(solution)/shard_map/ppermute | solution.py:494
  27.9 1.3 %collective-permute-start.3 = (bf16[16,16,384]{2,1,0:T(8,128)(2,1)S(1)}, bf16[16,16,384]{2,1,0:T(8,128)(2,1)S(1)}, u32[]{:S(2)}, u32[]{:S(2)}) collective-permute-start(bf16[16,16,384]{2,1,0:T(8,128)(2,1)S(1)} %get-tuple-element.32), channel_id=1, source_target_pairs={{1,0},{2,1},{3,2},{4,3},{5,4},{6,5},{7,6},{8,7},{9,8},{10,9},{11,1... | collective-permute-start | bytes 589832 | tf_op jit(solution)/shard_map/ppermute | solution.py:495
  29.2 17.5 %all-to-all-start.1 = ((f32[32,4,128]{2,1,0:T(4,128)}), f32[32,4,128]{2,1,0:T(4,128)S(1)}, u32[]{:S(2)}, u32[]{:S(2)}) async-start(f32[32,4,128]{2,1,0:T(4,128)} %get-tuple-element.34), calls=%async_computation.1 | async-start | bytes 131072 | tf_op jit(solution)/shard_map/all_to_all | solution.py:455
  46.7 0.0 collective-permute-done.2.side_l
  46.7 0.0 collective-permute-done.3.side_u
  46.7 0.0 copy-done.1
  46.7 7.5 %early.1 = (f32[1024,192]{1,0:T(8,128)S(1)}, bf16[192,1024]{1,0:T(8,128)(2,1)S(1)}) custom-call(bf16[64,16,192]{2,1,0:T(8,128)(2,1)S(1)} %get-tuple-element.29.up, bf16[16,16,192]{2,1,0:T(8,128)(2,1)S(1)} %collective-permute-done.lower, bf16[16,16,192]{2,1,0:T(8,128)(2,1)S(1)} %collective-permute-done.1.upper, ...), custom_call_target="tpu_custom_call" | custom-call | flops 3000000000 | bytes 4155072 | tf_op jit(solution)/shard_map/early/pallas_call | solution.py:441
  54.2 3.6 %all-to-all-done.1.stats = f32[32,4,128]{2,1,0:T(4,128)S(1)} async-done(((f32[32,4,128]{2,1,0:T(4,128)}), f32[32,4,128]{2,1,0:T(4,128)S(1)}, u32[]{:S(2)}, u32[]{:S(2)}) %all-to-all-start.1) | async-done | bytes 65568 | tf_op jit(solution)/shard_map/all_to_all | solution.py:455
  57.9 6.3 %weight.1 = (bf16[8,11,16,384]{3,2,1,0:T(8,128)(2,1)S(1)}, bf16[8,11,16,384]{3,2,1,0:T(8,128)(2,1)S(1)}, bf16[6,6,6,16,192]{4,3,2,1,0:T(8,128)(2,1)}) custom-call(s32[1]{0:T(128)} %bitcast.13.counts, s32[1]{0:T(128)} %bitcast.6.core, bf16[64,16,192]{2,1,0:T(8,128)(2,1)S(1)} %get-tuple-element.26.held, bf16[16,16,192]{2,1,0:T(8,128)(2,1)S(1)} %collective-permute-done.lower, ...), custom_call_target="tpu_custom_call" | custom-call | flops 4000000000 | bytes 4934848 | tf_op jit(solution)/shard_map/weight/pallas_call | solution.py:441
  64.2 4.2 %collective-permute-start.4 = (bf16[8,11,16,384]{3,2,1,0:T(8,128)(2,1)S(1)}, bf16[8,11,16,384]{3,2,1,0:T(8,128)(2,1)S(1)}, u32[]{:S(2)}, u32[]{:S(2)}) collective-permute-start(bf16[8,11,16,384]{3,2,1,0:T(8,128)(2,1)S(1)} %get-tuple-element.41), channel_id=1, source_target_pairs={{0,32},{32,0},{64,96},{96,64},{128,160},{160,128},{192,224},{224,1... | collective-permute-start | bytes 3244040 | tf_op jit(solution)/shard_map/ppermute | solution.py:525
  68.5 1.9 %slope.1 = (f32[1024,192]{1,0:T(8,128)}, f32[16,384]{1,0:T(8,128)S(1)}) custom-call(s32[1]{0:T(128)} %bitcast.15.counts, bf16[64,16,192]{2,1,0:T(8,128)(2,1)S(1)} %get-tuple-element.26.held, bf16[64,16,192]{2,1,0:T(8,128)(2,1)S(1)} %get-tuple-element.29.up, f32[1024,192]{1,0:T(8,128)S(1)} %get-tuple-element.38.back, f32[32,4,128]{2,1,0:T(4,128)S(1)} %all-to-all-done.1.stats, ...), custom_call_target="tpu_custom_call" | custom-call | flops 100000000 | bytes 2450944 | tf_op jit(solution)/shard_map/slope/pallas_call | solution.py:441
  70.3 0.4 collective-permute-done.4
  70.7 1.4 %select_convert_fusion = bf16[8,11,16,384]{3,2,1,0:T(8,128)(2,1)} fusion(bf16[8,11,16,384]{3,2,1,0:T(8,128)(2,1)S(1)} %collective-permute-done.4, bf16[8,11,16,384]{3,2,1,0:T(8,128)(2,1)S(1)} %get-tuple-element.40, f32[16,384]{1,0:T(8,128)S(1)} %get-tuple-element.39, pred[16]{0:T(512)(128)(4,1)S(1)} %iota_compare_fusion, pred[11]{0:T(512)(128)(4,1)S(1)} %iota_compare_fusion.1), kind=kLoop, calls=%fused_computation | loop fusion | flops 2703360 | bytes 3268635 | tf_op jit(solution)/shard_map/convert_element_type | solution.py:539
  72.1 3.6 %all-to-all-start.2 = ((bf16[8,11,16,384]{3,2,1,0:T(8,128)(2,1)}), bf16[8,11,16,384]{3,2,1,0:T(8,128)(2,1)S(1)}, u32[]{:S(2)}, u32[]{:S(2)}) async-start(bf16[8,11,16,384]{3,2,1,0:T(8,128)(2,1)} %select_convert_fusion), calls=%async_computation.2 | async-start | bytes 2162688 | tf_op jit(solution)/shard_map/all_to_all | solution.py:455
  75.7 8.8 %forward.1 = (bf16[16,64,192]{2,1,0:T(8,128)(2,1)}, f32[8,128]{1,0:T(8,128)S(1)}) custom-call(s32[1]{0:T(128)} %bitcast.14.counts, bf16[64,16,192]{2,1,0:T(8,128)(2,1)S(1)} %get-tuple-element.26.held, bf16[27,192,192]{2,1,0:T(8,128)(2,1)} %bitcast.23, bf16[6,6,6,16,192]{4,3,2,1,0:T(8,128)(2,1)} %get-tuple-element.36.padded_at), custom_call_target="tpu_custom_call" | custom-call | flops 3000000000 | bytes 4108288 | tf_op jit(solution)/shard_map/forward/pallas_call | solution.py:441
  84.5 0.0 copy-start.2
  84.5 7.0 %all-to-all-done.2.parts = bf16[8,11,16,384]{3,2,1,0:T(8,128)(2,1)S(1)} async-done(((bf16[8,11,16,384]{3,2,1,0:T(8,128)(2,1)}), bf16[8,11,16,384]{3,2,1,0:T(8,128)(2,1)S(1)}, u32[]{:S(2)}, u32[]{:S(2)}) %all-to-all-start.2) | async-done | bytes 1081376 | tf_op jit(solution)/shard_map/all_to_all | solution.py:455
  91.5 0.1 share.1
  91.7 18.5 %all_to_all.26.parts = bf16[32,24,128]{2,1,0:T(8,128)(2,1)S(1)} all-to-all(bf16[32,24,128]{2,1,0:T(8,128)(2,1)S(1)} %share.1), channel_id=1, replica_groups=mesh['gx'=16,'gy'=32] {'gy'}, dimensions={0} | all-to-all | bytes 393216 | tf_op jit(solution)/shard_map/all_to_all | solution.py:455
  110.2 0.7 own.1
  110.9 4.8 %all-to-all-start.4 = ((bf16[32,16,128]{2,1,0:T(8,128)(2,1)}), bf16[32,16,128]{2,1,0:T(8,128)(2,1)S(1)}, u32[]{:S(2)}, u32[]{:S(2)}) async-start(bf16[32,16,128]{2,1,0:T(8,128)(2,1)} %get-tuple-element.46), calls=%async_computation.4 | async-start | bytes 262144 | tf_op jit(solution)/shard_map/all_to_all | solution.py:455
  115.7 3.8 %collective-permute-start.5 = (f32[1,384]{1,0:T(1,128)S(1)}, f32[1,384]{1,0:T(1,128)S(1)}, u32[]{:S(2)}, u32[]{:S(2)}) collective-permute-start(f32[1,384]{1,0:T(1,128)S(1)} %get-tuple-element.43.sums), channel_id=1, source_target_pairs={{0,32},{32,0},{64,96},{96,64},{128,160},{160,128},{192,224},{224,1... | collective-permute-start | bytes 4616 | tf_op jit(solution)/shard_map/ppermute | solution.py:558
  119.5 0.0 copy-done.2
  119.5 0.1 copy.13.action
  119.6 0.7 collective-permute-done.5.other
  120.3 2.6 %finish.1 = (f32[128,384]{1,0:T(8,128)}, bf16[16,64,192]{2,1,0:T(8,128)(2,1)}) custom-call(s32[1]{0:T(128)} %bitcast.16.counts, f32[1,384]{1,0:T(1,128)S(1)} %get-tuple-element.43.sums, f32[1,384]{1,0:T(1,128)S(1)} %collective-permute-done.5.other, f32[32,4,128]{2,1,0:T(4,128)S(1)} %all-to-all-done.1.stats, f32[1,384]{1,0:T(1,128)S(1)} %get-tuple-element.35.film, ...), custom_call_target="tpu_custom_call" | custom-call | flops 1000000000 | bytes 1840128 | tf_op jit(solution)/shard_map/finish/pallas_call | solution.py:441
  122.9 4.0 %all-to-all-done.4.tiles = bf16[32,16,128]{2,1,0:T(8,128)(2,1)S(1)} async-done(((bf16[32,16,128]{2,1,0:T(8,128)(2,1)}), bf16[32,16,128]{2,1,0:T(8,128)(2,1)S(1)}, u32[]{:S(2)}, u32[]{:S(2)}) %all-to-all-start.4) | async-done | bytes 131104 | tf_op jit(solution)/shard_map/all_to_all | solution.py:455
  127.0 1.1 unpack.1
  (2 shorter events, 0.0 us)
Async XLA Ops:
  1.3 20.8 %copy-start = (s32[1,1,2,12]{3,2,1,0:T(2,128)S(1)}, s32[1,1,2,12]{3,2,1,0:T(2,128)}, u32[]{:S(2)}) copy-start(s32[1,1,2,12]{3,2,1,0:T(2,128)} %param.14) | copy-start | bytes 292
  4.1 42.6 %copy-start.1 = (s32[1,1,16,27]{3,2,1,0:T(8,128)S(1)}, s32[1,1,16,27]{3,2,1,0:T(8,128)}, u32[]{:S(2)}) copy-start(s32[1,1,16,27]{3,2,1,0:T(8,128)} %param.12) | copy-start | bytes 5188
  4.1 18.0 %collective-permute-start = (bf16[16,16,192]{2,1,0:T(8,128)(2,1)S(1)}, bf16[16,16,192]{2,1,0:T(8,128)(2,1)S(1)}, u32[]{:S(2)}, u32[]{:S(2)}) collective-permute-start(bf16[16,16,192]{2,1,0:T(8,128)(2,1)S(1)} %get-tuple-element.27), channel_id=1, source_target_pairs={{0,32},{32,64},{64,96},{96,128},{128,160},{160,192},{192,224},{224... | collective-permute-start | bytes 294920 | tf_op jit(solution)/shard_map/ppermute | solution.py:482
  8.7 13.4 %collective-permute-start.1 = (bf16[16,16,192]{2,1,0:T(8,128)(2,1)S(1)}, bf16[16,16,192]{2,1,0:T(8,128)(2,1)S(1)}, u32[]{:S(2)}, u32[]{:S(2)}) collective-permute-start(bf16[16,16,192]{2,1,0:T(8,128)(2,1)S(1)} %get-tuple-element.28), channel_id=1, source_target_pairs={{32,0},{64,32},{96,64},{128,96},{160,128},{192,160},{224,192},{256... | collective-permute-start | bytes 294920 | tf_op jit(solution)/shard_map/ppermute | solution.py:483
  23.7 23.0 %collective-permute-start.2 = (bf16[16,16,384]{2,1,0:T(8,128)(2,1)S(1)}, bf16[16,16,384]{2,1,0:T(8,128)(2,1)S(1)}, u32[]{:S(2)}, u32[]{:S(2)}) collective-permute-start(bf16[16,16,384]{2,1,0:T(8,128)(2,1)S(1)} %get-tuple-element.31), channel_id=1, source_target_pairs={{0,1},{1,2},{2,3},{3,4},{4,5},{5,6},{6,7},{7,8},{8,9},{9,10},{10,1... | collective-permute-start | bytes 589832 | tf_op jit(solution)/shard_map/ppermute | solution.py:494
  27.9 18.8 %collective-permute-start.3 = (bf16[16,16,384]{2,1,0:T(8,128)(2,1)S(1)}, bf16[16,16,384]{2,1,0:T(8,128)(2,1)S(1)}, u32[]{:S(2)}, u32[]{:S(2)}) collective-permute-start(bf16[16,16,384]{2,1,0:T(8,128)(2,1)S(1)} %get-tuple-element.32), channel_id=1, source_target_pairs={{1,0},{2,1},{3,2},{4,3},{5,4},{6,5},{7,6},{8,7},{9,8},{10,9},{11,1... | collective-permute-start | bytes 589832 | tf_op jit(solution)/shard_map/ppermute | solution.py:495
  29.2 28.7 %all-to-all-start.1 = ((f32[32,4,128]{2,1,0:T(4,128)}), f32[32,4,128]{2,1,0:T(4,128)S(1)}, u32[]{:S(2)}, u32[]{:S(2)}) async-start(f32[32,4,128]{2,1,0:T(4,128)} %get-tuple-element.34), calls=%async_computation.1 | async-start | bytes 131072 | tf_op jit(solution)/shard_map/all_to_all | solution.py:455
  64.2 6.5 %collective-permute-start.4 = (bf16[8,11,16,384]{3,2,1,0:T(8,128)(2,1)S(1)}, bf16[8,11,16,384]{3,2,1,0:T(8,128)(2,1)S(1)}, u32[]{:S(2)}, u32[]{:S(2)}) collective-permute-start(bf16[8,11,16,384]{3,2,1,0:T(8,128)(2,1)S(1)} %get-tuple-element.41), channel_id=1, source_target_pairs={{0,32},{32,0},{64,96},{96,64},{128,160},{160,128},{192,224},{224,1... | collective-permute-start | bytes 3244040 | tf_op jit(solution)/shard_map/ppermute | solution.py:525
  72.1 19.4 %all-to-all-start.2 = ((bf16[8,11,16,384]{3,2,1,0:T(8,128)(2,1)}), bf16[8,11,16,384]{3,2,1,0:T(8,128)(2,1)S(1)}, u32[]{:S(2)}, u32[]{:S(2)}) async-start(bf16[8,11,16,384]{3,2,1,0:T(8,128)(2,1)} %select_convert_fusion), calls=%async_computation.2 | async-start | bytes 2162688 | tf_op jit(solution)/shard_map/all_to_all | solution.py:455
  84.5 35.0 %copy-start.2 = (f32[128]{0:T(128)S(1)}, f32[128]{0:T(128)}, u32[]{:S(2)}) copy-start(f32[128]{0:T(128)} %param.15) | copy-start | bytes 1540
  110.9 16.1 %all-to-all-start.4 = ((bf16[32,16,128]{2,1,0:T(8,128)(2,1)}), bf16[32,16,128]{2,1,0:T(8,128)(2,1)S(1)}, u32[]{:S(2)}, u32[]{:S(2)}) async-start(bf16[32,16,128]{2,1,0:T(8,128)(2,1)} %get-tuple-element.46), calls=%async_computation.4 | async-start | bytes 262144 | tf_op jit(solution)/shard_map/all_to_all | solution.py:455
  115.7 4.7 %collective-permute-start.5 = (f32[1,384]{1,0:T(1,128)S(1)}, f32[1,384]{1,0:T(1,128)S(1)}, u32[]{:S(2)}, u32[]{:S(2)}) collective-permute-start(f32[1,384]{1,0:T(1,128)S(1)} %get-tuple-element.43.sums), channel_id=1, source_target_pairs={{0,32},{32,0},{64,96},{96,64},{128,160},{160,128},{192,224},{224,1... | collective-permute-start | bytes 4616 | tf_op jit(solution)/shard_map/ppermute | solution.py:558

commit v8 on v7

--- a/solution.py
+++ b/solution.py
@@ -84,10 +84,9 @@
 
 
 def pack_kernel(
-    counts, send_x, feat_at, cot_at, film_at, action_at,
-    held, up, stats, face_low, face_high, film, feat, cot, film_weight, action, done,
+    counts, send_x, feat_at, cot_at, held, up, stats, face_low, face_high, feat, cot, done,
 ):
-    pairs = ((feat_at, feat), (cot_at, cot), (film_at, film_weight), (action_at, action))
+    pairs = ((feat_at, feat), (cot_at, cot))
     copies = [
         pltpu.make_async_copy(source, target, done.at[n]) for n, (source, target) in enumerate(pairs)
     ]
@@ -116,13 +115,6 @@
             both = jnp.concatenate([held[48 * side + i], up[48 * side + i]], axis=0)
             target = (face_low, face_high)[side]
             target[i, :, :] = dot(chosen, both).astype(BF16)
-    film[...] = lax.dot_general(
-        action[...],
-        film_weight[...],
-        (((1,), (0,)), ((), ())),
-        precision=lax.Precision.HIGHEST,
-        preferred_element_type=F32,
-    )
 
 
 def cross_kernel(send_y, held, up, lower, upper, stats, face_low, face_high, spread):
@@ -208,18 +200,30 @@
 
 
 def early_kernel(
-    up, lower, upper, side_l, side_u, rule, weight_at,
-    back, turned, wide, low_y, high_y, weight, done,
+    up, lower, upper, side_l, side_u, rule, weight_at, film_at, action_at,
+    back, turned, film, wide, low_y, high_y, weight, film_weight, action, done,
 ):
-    copy = pltpu.make_async_copy(weight_at, weight, done.at[0])
-    copy.start()
+    pairs = ((weight_at, weight), (film_at, film_weight), (action_at, action))
+    copies = [
+        pltpu.make_async_copy(source, target, done.at[n]) for n, (source, target) in enumerate(pairs)
+    ]
+    for copy in copies:
+        copy.start()
     low_y[...] = one_field(side_l[...], 1)
     high_y[...] = one_field(side_u[...], 1)
     gather_blocks(rule, 8, up, lower, upper, low_y, high_y, wide)
     same = jnp.where(iota((CHANNELS, CHANNELS), 0) == iota((CHANNELS, CHANNELS), 1), 1.0, 0.0)
     turned[...] = dot_nt(same.astype(BF16), up[...].reshape(1024, CHANNELS)).astype(BF16)
     back[...] = jnp.zeros_like(back)
-    copy.wait()
+    for copy in copies:
+        copy.wait()
+    film[...] = lax.dot_general(
+        action[...],
+        film_weight[...],
+        (((1,), (0,)), ((), ())),
+        precision=lax.Precision.HIGHEST,
+        preferred_element_type=F32,
+    )
 
     def step(t, carry):
         k = 3 * t
@@ -464,16 +468,16 @@
     face = ((16, 16, CHANNELS), BF16)
     spaced = ((6, 6, 6, 16, CHANNELS), BF16)
     joined = ((16, 16, 384), BF16)
-    held, up, stats, face_low, face_high, film = call(
+    held, up, stats, face_low, face_high = call(
         pack_kernel,
         [count, list_x],
-        [features[0, 0], cotangent[0, 0], film_weight, action[None]],
-        [block, block, ((size_x, 4, 128), F32), face, face, ((1, 2 * CHANNELS), F32)],
-        [((SLOTS, VOXELS, CHANNELS), BF16), ((SLOTS, VOXELS, CHANNELS), BF16), ((128, 2 * CHANNELS), F32), ((1, 128), F32)],
+        [features[0, 0], cotangent[0, 0]],
+        [block, block, ((size_x, 4, 128), F32), face, face],
+        [((SLOTS, VOXELS, CHANNELS), BF16), ((SLOTS, VOXELS, CHANNELS), BF16)],
         flops=10**9,
         name="pack",
-        left=4,
-        copies=4,
+        left=2,
+        copies=2,
     )
     up_x = [(i, i + 1) for i in range(size_x - 1)]
     down_x = [(i + 1, i) for i in range(size_x - 1)]
@@ -498,16 +502,16 @@
     swapped = [(i, i ^ 1) for i in range(size_x)]
     taps = ((27, CHANNELS, CHANNELS), BF16)
     total = ((1024, CHANNELS), F32)
-    back, turned = call(
+    back, turned, film = call(
         early_kernel,
         [],
-        [up, lower, upper, side_l, side_u, rule, weight],
-        [total, ((CHANNELS, 1024), BF16)],
-        [spaced, face, face, taps],
+        [up, lower, upper, side_l, side_u, rule, weight, film_weight, action[None]],
+        [total, ((CHANNELS, 1024), BF16), ((1, 2 * CHANNELS), F32)],
+        [spaced, face, face, taps, ((128, 2 * CHANNELS), F32), ((1, 128), F32)],
         flops=3 * 10**9,
         name="early",
-        left=1,
-        copies=1,
+        left=3,
+        copies=3,
         room=20,
     )
     half = ((8, TILES, 16, 384), BF16)

time: 130 us -> 130 us (level)
  no operation moved by 1% of the time
where the time goes in v8:
time: 130 us; the launch traced here: 128 us
  starting transfers between devices  49.5 us (38%)
  Pallas kernels  33.3 us (26%)
  blocking collectives  26.6 us (20%)
  waiting for transfers between devices  15.6 us (12%)
  between operations  1.48 us (1%)
  other arithmetic  1.4 us (1%)
    pallas_call x10, Pallas kernels, call(): pl.pallas_call(kernel, out_shape=shapes, in_specs=[SMEM] * len(scalars) +...  33.3 us
    all_to_all x2, blocking collectives, exchange(): lax.all_to_all(array, axis, 0, 0, axis_index_groups=groups, tiled=True)  26.6 us
    all_to_all x3, starting transfers between devices, exchange(): lax.all_to_all(array, axis, 0, 0, axis_index_groups=groups, tiled=True)  25.8 us
    all_to_all x3, waiting for transfers between devices, exchange(): lax.all_to_all(array, axis, 0, 0, axis_index_groups=groups, tiled=True)  14.5 us
    ppermute x1, starting transfers between devices, body(): upper = lax.ppermute(face_low, 'gx', down_x)  5.49 us
    ppermute x1, starting transfers between devices, body(): lower = lax.ppermute(face_high, 'gx', up_x)  4.59 us
    ppermute x1, starting transfers between devices, body(): other = lax.ppermute(far, 'gx', swapped)  4.22 us
    ppermute x1, starting transfers between devices, body(): side_l = lax.ppermute(face_high, 'gy', up_y)  4.21 us
  transfers between devices with their start and end apart: 9, of which 5 were waited for; matrix products, arithmetic and copies ran while one was open for 0% of the time, Pallas kernels for 16%

profile of v8, /device:TPU:1, one launch (start us, length us, event | category | flops | bytes accessed | tf_op | source)
XLA Modules:
  0.0 128.0 jit_solution(681883021284235845)
XLA Ops:
  1.3 0.0 copy-start
  1.3 2.6 %pack.1 = (bf16[64,16,192]{2,1,0:T(8,128)(2,1)S(1)}, bf16[64,16,192]{2,1,0:T(8,128)(2,1)S(1)}, f32[16,4,128]{2,1,0:T(4,128)S(1)}, bf16[16,16,192]{2,1,0:T(8,128)(2,1)S(1)}, bf16[16,16,192]{2,1,0:T(8,128)(2,1)S(1)}) custom-call(s32[1]{0:T(128)} %bitcast.12.counts, s32[2,8]{1,0:T(2,128)} %bitcast.26, bf16[16,64,192]{2,1,0:T(8,128)(2,1)} %bitcast.24, ...), custom_call_target="tpu_custom_call" | custom-call | flops 1000000000 | bytes 1802240 | tf_op jit(solution)/shard_map/pack/pallas_call | solution.py:445
  3.9 0.0 copy-start.1
  3.9 4.6 %collective-permute-start = (bf16[16,16,192]{2,1,0:T(8,128)(2,1)S(1)}, bf16[16,16,192]{2,1,0:T(8,128)(2,1)S(1)}, u32[]{:S(2)}, u32[]{:S(2)}) collective-permute-start(bf16[16,16,192]{2,1,0:T(8,128)(2,1)S(1)} %get-tuple-element.27), channel_id=1, source_target_pairs={{0,32},{32,64},{64,96},{96,128},{128,160},{160,192},{192,224},{224... | collective-permute-start | bytes 294920 | tf_op jit(solution)/shard_map/ppermute | solution.py:486
  8.5 5.5 %collective-permute-start.1 = (bf16[16,16,192]{2,1,0:T(8,128)(2,1)S(1)}, bf16[16,16,192]{2,1,0:T(8,128)(2,1)S(1)}, u32[]{:S(2)}, u32[]{:S(2)}) collective-permute-start(bf16[16,16,192]{2,1,0:T(8,128)(2,1)S(1)} %get-tuple-element.28), channel_id=1, source_target_pairs={{32,0},{64,32},{96,64},{128,96},{160,128},{192,160},{224,192},{256... | collective-permute-start | bytes 294920 | tf_op jit(solution)/shard_map/ppermute | solution.py:487
  14.0 7.9 %all_to_all.25.stats = f32[16,4,128]{2,1,0:T(4,128)S(1)} all-to-all(f32[16,4,128]{2,1,0:T(4,128)S(1)} %get-tuple-element.30), channel_id=1, replica_groups=mesh['gx'=16,'gy'=32] {'gx'}, dimensions={0} | all-to-all | bytes 65536 | tf_op jit(solution)/shard_map/all_to_all | solution.py:459
  21.9 0.0 collective-permute-done.lower
  21.9 0.0 collective-permute-done.1.upper
  21.9 0.0 copy-done
  21.9 1.5 %cross.1 = (bf16[16,16,384]{2,1,0:T(8,128)(2,1)S(1)}, bf16[16,16,384]{2,1,0:T(8,128)(2,1)S(1)}, f32[32,4,128]{2,1,0:T(4,128)}) custom-call(s32[2,12]{1,0:T(2,128)S(1)} %bitcast.17, bf16[64,16,192]{2,1,0:T(8,128)(2,1)S(1)} %get-tuple-element.26.held, bf16[64,16,192]{2,1,0:T(8,128)(2,1)S(1)} %get-tuple-element.29.up, ...), custom_call_target="tpu_custom_call" | custom-call | flops 100000000 | bytes 1474560 | tf_op jit(solution)/shard_map/cross/pallas_call | solution.py:445
  23.5 4.2 %collective-permute-start.2 = (bf16[16,16,384]{2,1,0:T(8,128)(2,1)S(1)}, bf16[16,16,384]{2,1,0:T(8,128)(2,1)S(1)}, u32[]{:S(2)}, u32[]{:S(2)}) collective-permute-start(bf16[16,16,384]{2,1,0:T(8,128)(2,1)S(1)} %get-tuple-element.31), channel_id=1, source_target_pairs={{0,1},{1,2},{2,3},{3,4},{4,5},{5,6},{6,7},{7,8},{8,9},{9,10},{10,1... | collective-permute-start | bytes 589832 | tf_op jit(solution)/shard_map/ppermute | solution.py:498
  27.7 1.3 %collective-permute-start.3 = (bf16[16,16,384]{2,1,0:T(8,128)(2,1)S(1)}, bf16[16,16,384]{2,1,0:T(8,128)(2,1)S(1)}, u32[]{:S(2)}, u32[]{:S(2)}) collective-permute-start(bf16[16,16,384]{2,1,0:T(8,128)(2,1)S(1)} %get-tuple-element.32), channel_id=1, source_target_pairs={{1,0},{2,1},{3,2},{4,3},{5,4},{6,5},{7,6},{8,7},{9,8},{10,9},{11,1... | collective-permute-start | bytes 589832 | tf_op jit(solution)/shard_map/ppermute | solution.py:499
  29.0 17.5 %all-to-all-start.1 = ((f32[32,4,128]{2,1,0:T(4,128)}), f32[32,4,128]{2,1,0:T(4,128)S(1)}, u32[]{:S(2)}, u32[]{:S(2)}) async-start(f32[32,4,128]{2,1,0:T(4,128)} %get-tuple-element.34), calls=%async_computation.1 | async-start | bytes 131072 | tf_op jit(solution)/shard_map/all_to_all | solution.py:459
  46.5 0.0 collective-permute-done.2.side_l
  46.5 0.0 collective-permute-done.3.side_u
  46.5 0.0 copy-done.1
  46.5 7.7 %early.1 = (f32[1024,192]{1,0:T(8,128)S(1)}, bf16[192,1024]{1,0:T(8,128)(2,1)S(1)}, f32[1,384]{1,0:T(1,128)S(1)}) custom-call(bf16[64,16,192]{2,1,0:T(8,128)(2,1)S(1)} %get-tuple-element.29.up, bf16[16,16,192]{2,1,0:T(8,128)(2,1)S(1)} %collective-permute-done.lower, bf16[16,16,192]{2,1,0:T(8,128)(2,1)S(1)} %collective-permute-done.1.upper, ...), custom_call_target="tpu_custom_call" | custom-call | flops 3000000000 | bytes 4353728 | tf_op jit(solution)/shard_map/early/pallas_call | solution.py:445
  54.2 3.5 %all-to-all-done.1.stats = f32[32,4,128]{2,1,0:T(4,128)S(1)} async-done(((f32[32,4,128]{2,1,0:T(4,128)}), f32[32,4,128]{2,1,0:T(4,128)S(1)}, u32[]{:S(2)}, u32[]{:S(2)}) %all-to-all-start.1) | async-done | bytes 65568 | tf_op jit(solution)/shard_map/all_to_all | solution.py:459
  57.7 6.3 %weight.1 = (bf16[8,11,16,384]{3,2,1,0:T(8,128)(2,1)S(1)}, bf16[8,11,16,384]{3,2,1,0:T(8,128)(2,1)S(1)}, bf16[6,6,6,16,192]{4,3,2,1,0:T(8,128)(2,1)}) custom-call(s32[1]{0:T(128)} %bitcast.13.counts, s32[1]{0:T(128)} %bitcast.5.core, bf16[64,16,192]{2,1,0:T(8,128)(2,1)S(1)} %get-tuple-element.26.held, bf16[16,16,192]{2,1,0:T(8,128)(2,1)S(1)} %collective-permute-done.lower, ...), custom_call_target="tpu_custom_call" | custom-call | flops 4000000000 | bytes 4934848 | tf_op jit(solution)/shard_map/weight/pallas_call | solution.py:445
  64.0 4.2 %collective-permute-start.4 = (bf16[8,11,16,384]{3,2,1,0:T(8,128)(2,1)S(1)}, bf16[8,11,16,384]{3,2,1,0:T(8,128)(2,1)S(1)}, u32[]{:S(2)}, u32[]{:S(2)}) collective-permute-start(bf16[8,11,16,384]{3,2,1,0:T(8,128)(2,1)S(1)} %get-tuple-element.41), channel_id=1, source_target_pairs={{0,32},{32,0},{64,96},{96,64},{128,160},{160,128},{192,224},{224,1... | collective-permute-start | bytes 3244040 | tf_op jit(solution)/shard_map/ppermute | solution.py:529
  68.3 1.9 %slope.1 = (f32[1024,192]{1,0:T(8,128)}, f32[16,384]{1,0:T(8,128)S(1)}) custom-call(s32[1]{0:T(128)} %bitcast.15.counts, bf16[64,16,192]{2,1,0:T(8,128)(2,1)S(1)} %get-tuple-element.26.held, bf16[64,16,192]{2,1,0:T(8,128)(2,1)S(1)} %get-tuple-element.29.up, f32[1024,192]{1,0:T(8,128)S(1)} %get-tuple-element.38.back, f32[32,4,128]{2,1,0:T(4,128)S(1)} %all-to-all-done.1.stats, ...), custom_call_target="tpu_custom_call" | custom-call | flops 100000000 | bytes 2450944 | tf_op jit(solution)/shard_map/slope/pallas_call | solution.py:445
  70.2 0.4 collective-permute-done.4
  70.5 1.4 %select_convert_fusion = bf16[8,11,16,384]{3,2,1,0:T(8,128)(2,1)} fusion(bf16[8,11,16,384]{3,2,1,0:T(8,128)(2,1)S(1)} %collective-permute-done.4, bf16[8,11,16,384]{3,2,1,0:T(8,128)(2,1)S(1)} %get-tuple-element.40, f32[16,384]{1,0:T(8,128)S(1)} %get-tuple-element.39, pred[16]{0:T(512)(128)(4,1)S(1)} %iota_compare_fusion, pred[11]{0:T(512)(128)(4,1)S(1)} %iota_compare_fusion.1), kind=kLoop, calls=%fused_computation | loop fusion | flops 2703360 | bytes 3268635 | tf_op jit(solution)/shard_map/convert_element_type | solution.py:543
  71.9 3.6 %all-to-all-start.2 = ((bf16[8,11,16,384]{3,2,1,0:T(8,128)(2,1)}), bf16[8,11,16,384]{3,2,1,0:T(8,128)(2,1)S(1)}, u32[]{:S(2)}, u32[]{:S(2)}) async-start(bf16[8,11,16,384]{3,2,1,0:T(8,128)(2,1)} %select_convert_fusion), calls=%async_computation.2 | async-start | bytes 2162688 | tf_op jit(solution)/shard_map/all_to_all | solution.py:459
  75.5 8.8 %forward.1 = (bf16[16,64,192]{2,1,0:T(8,128)(2,1)}, f32[8,128]{1,0:T(8,128)S(1)}) custom-call(s32[1]{0:T(128)} %bitcast.14.counts, bf16[64,16,192]{2,1,0:T(8,128)(2,1)S(1)} %get-tuple-element.26.held, bf16[27,192,192]{2,1,0:T(8,128)(2,1)} %bitcast.23, bf16[6,6,6,16,192]{4,3,2,1,0:T(8,128)(2,1)} %get-tuple-element.36.padded_at), custom_call_target="tpu_custom_call" | custom-call | flops 3000000000 | bytes 4108288 | tf_op jit(solution)/shard_map/forward/pallas_call | solution.py:445
  84.3 0.0 copy-start.2
  84.3 7.0 %all-to-all-done.2.parts = bf16[8,11,16,384]{3,2,1,0:T(8,128)(2,1)S(1)} async-done(((bf16[8,11,16,384]{3,2,1,0:T(8,128)(2,1)}), bf16[8,11,16,384]{3,2,1,0:T(8,128)(2,1)S(1)}, u32[]{:S(2)}, u32[]{:S(2)}) %all-to-all-start.2) | async-done | bytes 1081376 | tf_op jit(solution)/shard_map/all_to_all | solution.py:459
  91.3 0.1 share.1
  91.4 18.7 %all_to_all.26.parts = bf16[32,24,128]{2,1,0:T(8,128)(2,1)S(1)} all-to-all(bf16[32,24,128]{2,1,0:T(8,128)(2,1)S(1)} %share.1), channel_id=1, replica_groups=mesh['gx'=16,'gy'=32] {'gy'}, dimensions={0} | all-to-all | bytes 393216 | tf_op jit(solution)/shard_map/all_to_all | solution.py:459
  110.1 0.7 own.1
  110.8 4.8 %all-to-all-start.4 = ((bf16[32,16,128]{2,1,0:T(8,128)(2,1)}), bf16[32,16,128]{2,1,0:T(8,128)(2,1)S(1)}, u32[]{:S(2)}, u32[]{:S(2)}) async-start(bf16[32,16,128]{2,1,0:T(8,128)(2,1)} %get-tuple-element.46), calls=%async_computation.4 | async-start | bytes 262144 | tf_op jit(solution)/shard_map/all_to_all | solution.py:459
  115.6 3.8 %collective-permute-start.5 = (f32[1,384]{1,0:T(1,128)S(1)}, f32[1,384]{1,0:T(1,128)S(1)}, u32[]{:S(2)}, u32[]{:S(2)}) collective-permute-start(f32[1,384]{1,0:T(1,128)S(1)} %get-tuple-element.43.sums), channel_id=1, source_target_pairs={{0,32},{32,0},{64,96},{96,64},{128,160},{160,128},{192,224},{224,1... | collective-permute-start | bytes 4616 | tf_op jit(solution)/shard_map/ppermute | solution.py:562
  119.4 0.0 copy-done.2
  119.4 0.1 copy.13.action
  119.6 0.7 collective-permute-done.5.other
  120.2 2.6 %finish.1 = (f32[128,384]{1,0:T(8,128)}, bf16[16,64,192]{2,1,0:T(8,128)(2,1)}) custom-call(s32[1]{0:T(128)} %bitcast.16.counts, f32[1,384]{1,0:T(1,128)S(1)} %get-tuple-element.43.sums, f32[1,384]{1,0:T(1,128)S(1)} %collective-permute-done.5.other, f32[32,4,128]{2,1,0:T(4,128)S(1)} %all-to-all-done.1.stats, f32[1,384]{1,0:T(1,128)S(1)} %get-tuple-element.35.film, ...), custom_call_target="tpu_custom_call" | custom-call | flops 1000000000 | bytes 1840128 | tf_op jit(solution)/shard_map/finish/pallas_call | solution.py:445
  122.9 4.0 %all-to-all-done.4.tiles = bf16[32,16,128]{2,1,0:T(8,128)(2,1)S(1)} async-done(((bf16[32,16,128]{2,1,0:T(8,128)(2,1)}), bf16[32,16,128]{2,1,0:T(8,128)(2,1)S(1)}, u32[]{:S(2)}, u32[]{:S(2)}) %all-to-all-start.4) | async-done | bytes 131104 | tf_op jit(solution)/shard_map/all_to_all | solution.py:459
  126.9 1.1 unpack.1
  (2 shorter events, 0.0 us)
Async XLA Ops:
  1.3 20.7 %copy-start = (s32[1,1,2,12]{3,2,1,0:T(2,128)S(1)}, s32[1,1,2,12]{3,2,1,0:T(2,128)}, u32[]{:S(2)}) copy-start(s32[1,1,2,12]{3,2,1,0:T(2,128)} %param.14) | copy-start | bytes 292
  3.9 42.6 %copy-start.1 = (s32[1,1,16,27]{3,2,1,0:T(8,128)S(1)}, s32[1,1,16,27]{3,2,1,0:T(8,128)}, u32[]{:S(2)}) copy-start(s32[1,1,16,27]{3,2,1,0:T(8,128)} %param.12) | copy-start | bytes 5188
  3.9 18.0 %collective-permute-start = (bf16[16,16,192]{2,1,0:T(8,128)(2,1)S(1)}, bf16[16,16,192]{2,1,0:T(8,128)(2,1)S(1)}, u32[]{:S(2)}, u32[]{:S(2)}) collective-permute-start(bf16[16,16,192]{2,1,0:T(8,128)(2,1)S(1)} %get-tuple-element.27), channel_id=1, source_target_pairs={{0,32},{32,64},{64,96},{96,128},{128,160},{160,192},{192,224},{224... | collective-permute-start | bytes 294920 | tf_op jit(solution)/shard_map/ppermute | solution.py:486
  8.5 13.4 %collective-permute-start.1 = (bf16[16,16,192]{2,1,0:T(8,128)(2,1)S(1)}, bf16[16,16,192]{2,1,0:T(8,128)(2,1)S(1)}, u32[]{:S(2)}, u32[]{:S(2)}) collective-permute-start(bf16[16,16,192]{2,1,0:T(8,128)(2,1)S(1)} %get-tuple-element.28), channel_id=1, source_target_pairs={{32,0},{64,32},{96,64},{128,96},{160,128},{192,160},{224,192},{256... | collective-permute-start | bytes 294920 | tf_op jit(solution)/shard_map/ppermute | solution.py:487
  23.5 23.0 %collective-permute-start.2 = (bf16[16,16,384]{2,1,0:T(8,128)(2,1)S(1)}, bf16[16,16,384]{2,1,0:T(8,128)(2,1)S(1)}, u32[]{:S(2)}, u32[]{:S(2)}) collective-permute-start(bf16[16,16,384]{2,1,0:T(8,128)(2,1)S(1)} %get-tuple-element.31), channel_id=1, source_target_pairs={{0,1},{1,2},{2,3},{3,4},{4,5},{5,6},{6,7},{7,8},{8,9},{9,10},{10,1... | collective-permute-start | bytes 589832 | tf_op jit(solution)/shard_map/ppermute | solution.py:498
  27.7 18.8 %collective-permute-start.3 = (bf16[16,16,384]{2,1,0:T(8,128)(2,1)S(1)}, bf16[16,16,384]{2,1,0:T(8,128)(2,1)S(1)}, u32[]{:S(2)}, u32[]{:S(2)}) collective-permute-start(bf16[16,16,384]{2,1,0:T(8,128)(2,1)S(1)} %get-tuple-element.32), channel_id=1, source_target_pairs={{1,0},{2,1},{3,2},{4,3},{5,4},{6,5},{7,6},{8,7},{9,8},{10,9},{11,1... | collective-permute-start | bytes 589832 | tf_op jit(solution)/shard_map/ppermute | solution.py:499
  29.0 28.7 %all-to-all-start.1 = ((f32[32,4,128]{2,1,0:T(4,128)}), f32[32,4,128]{2,1,0:T(4,128)S(1)}, u32[]{:S(2)}, u32[]{:S(2)}) async-start(f32[32,4,128]{2,1,0:T(4,128)} %get-tuple-element.34), calls=%async_computation.1 | async-start | bytes 131072 | tf_op jit(solution)/shard_map/all_to_all | solution.py:459
  64.0 6.5 %collective-permute-start.4 = (bf16[8,11,16,384]{3,2,1,0:T(8,128)(2,1)S(1)}, bf16[8,11,16,384]{3,2,1,0:T(8,128)(2,1)S(1)}, u32[]{:S(2)}, u32[]{:S(2)}) collective-permute-start(bf16[8,11,16,384]{3,2,1,0:T(8,128)(2,1)S(1)} %get-tuple-element.41), channel_id=1, source_target_pairs={{0,32},{32,0},{64,96},{96,64},{128,160},{160,128},{192,224},{224,1... | collective-permute-start | bytes 3244040 | tf_op jit(solution)/shard_map/ppermute | solution.py:529
  71.9 19.4 %all-to-all-start.2 = ((bf16[8,11,16,384]{3,2,1,0:T(8,128)(2,1)}), bf16[8,11,16,384]{3,2,1,0:T(8,128)(2,1)S(1)}, u32[]{:S(2)}, u32[]{:S(2)}) async-start(bf16[8,11,16,384]{3,2,1,0:T(8,128)(2,1)} %select_convert_fusion), calls=%async_computation.2 | async-start | bytes 2162688 | tf_op jit(solution)/shard_map/all_to_all | solution.py:459
  84.3 35.2 %copy-start.2 = (f32[128]{0:T(128)S(1)}, f32[128]{0:T(128)}, u32[]{:S(2)}) copy-start(f32[128]{0:T(128)} %param.15) | copy-start | bytes 1540
  110.8 16.1 %all-to-all-start.4 = ((bf16[32,16,128]{2,1,0:T(8,128)(2,1)}), bf16[32,16,128]{2,1,0:T(8,128)(2,1)S(1)}, u32[]{:S(2)}, u32[]{:S(2)}) async-start(bf16[32,16,128]{2,1,0:T(8,128)(2,1)} %get-tuple-element.46), calls=%async_computation.4 | async-start | bytes 262144 | tf_op jit(solution)/shard_map/all_to_all | solution.py:459
  115.6 4.7 %collective-permute-start.5 = (f32[1,384]{1,0:T(1,128)S(1)}, f32[1,384]{1,0:T(1,128)S(1)}, u32[]{:S(2)}, u32[]{:S(2)}) collective-permute-start(f32[1,384]{1,0:T(1,128)S(1)} %get-tuple-element.43.sums), channel_id=1, source_target_pairs={{0,32},{32,0},{64,96},{96,64},{128,160},{160,128},{192,224},{224,1... | collective-permute-start | bytes 4616 | tf_op jit(solution)/shard_map/ppermute | solution.py:562
